TPU v7x, 256 devices: a whole 4x4x8 slice. The times are simulated.
256 devices in a mesh: pts: 64 (over z, y, core), out: 4 (over x).
Axes of the slice: x: 4, y: 4, z: 8, core: 2. Of those that a mesh axis runs over, the one named last changes fastest.
Arguments:
- points: bfloat16 [262144, 256], P('pts'), may hold values from -0.625 to 0.625
- rep_weights: float32 [4, 262144, 16], P('out', 'pts'), may hold values from -6 to 6
- batch_index: int32 [512], replicated, may hold values from 0 to 262143
- targets: float32 [4, 512, 16], replicated, may hold values from -6 to 6
- noise_var: float32 [4], replicated, may hold values from 0.5 to 2
- coregion: float32 [4, 4], replicated, as said below
- frequencies: bfloat16 [256, 2048], replicated, may hold values from -12 to 12
- phases: float32 [2048], replicated, may hold values from -3.140625 to 3.140625
Outputs:
- new_weights: float32 [4, 262144, 16], P('out', 'pts')
Inputs may be any that keep to these rules, and one draw needn't show every extreme that they name: `coregion`: symmetric and positive definite.
All inputs are finite; a program needn't handle non-finite values.
Results may differ from a plain program's by a relative error of at most 0.0031.
Values may be sent and summed in bfloat16 or wider, within the bound.
No kernel may reach another device: no remote copies, remote signals or barrier semaphores. Data moves between devices by JAX's collectives and lax.ppermute only.
A program may use at most 128 MiB of HBM per device.

v0:
```python
import math

import jax
import jax.numpy as jnp
from jax import lax
from jax.sharding import PartitionSpec as P

LENGTH = 0.5
STEP_SIZE = 0.5


def kernel_block(batch_rows, slab):
    row_norm = jnp.sum(jnp.square(batch_rows.astype(jnp.float32)), 1)
    col_norm = jnp.sum(jnp.square(slab.astype(jnp.float32)), 1)
    inner = jnp.dot(batch_rows, slab.T, preferred_element_type=jnp.float32)
    squared = row_norm[:, None] + col_norm[None, :] - 2.0 * inner
    scaled_r = math.sqrt(5.0) / LENGTH * jnp.sqrt(jnp.maximum(squared, 0.0))
    return ((1.0 + scaled_r + scaled_r * scaled_r / 3.0) * jnp.exp(-scaled_r)).astype(jnp.bfloat16)


def feature_map(slab, freq_cols, phase_cols, total_features):
    angle_arg = jnp.dot(slab, freq_cols, preferred_element_type=jnp.float32) + phase_cols
    return (math.sqrt(2.0 / total_features) * jnp.cos(angle_arg)).astype(jnp.bfloat16)


def shards(points, rep_weights, batch_index, targets, noise_var, coregion, frequencies, phases):
    highest = lax.Precision.HIGHEST
    shard_rows = points.shape[0]
    total_features = frequencies.shape[1]
    total_points = shard_rows * lax.axis_size("pts")
    first_row = lax.axis_index("pts") * shard_rows
    mine_out = lax.axis_index("out")
    local_idx = batch_index - first_row
    inside = (local_idx >= 0) & (local_idx < shard_rows)
    picked = points[jnp.clip(local_idx, 0, shard_rows - 1)].astype(jnp.float32)
    picked = jnp.where(inside[:, None], picked, 0.0)
    batch_rows = lax.psum(picked, "pts").astype(jnp.bfloat16)
    ratio = jnp.float32(total_points) / jnp.float32(batch_index.shape[0])
    low_weights = rep_weights.astype(jnp.bfloat16)
    block_rows = math.gcd(shard_rows, 512)
    nblocks = shard_rows // block_rows
    slabs = points.reshape(nblocks, block_rows, points.shape[1])
    coreg_row = lax.dynamic_slice_in_dim(coregion, mine_out, 1, 0)[0]
    own_slabs = low_weights[0].reshape(nblocks, block_rows, -1)

    def project_whole(totals, inputs):
        slab, weights = inputs
        feats = feature_map(slab, frequencies, phases, total_features)
        term = lax.dot_general(
            feats, weights, (((0,), (0,)), ((), ())), preferred_element_type=jnp.float32
        )
        return (totals + term, feats)

    projected, feats_all = lax.scan(
        project_whole,
        jnp.zeros((total_features, low_weights.shape[2]), jnp.float32),
        (slabs, own_slabs),
    )
    kern = kernel_block(batch_rows, points)
    partial_value = jnp.dot(kern, low_weights[0], preferred_element_type=jnp.float32)
    summed = lax.psum(partial_value, "pts")
    every_out = lax.all_gather(summed[None], "out", axis=0, tiled=True)
    fitted = jnp.einsum("pq,qms->pms", coregion, every_out, precision=highest)
    scaled = (fitted - targets) / noise_var[:, None, None]
    weighted = jnp.einsum("q,qms->ms", coreg_row, scaled, precision=highest).astype(jnp.bfloat16)
    data_grad = lax.dot_general(
        kern, weighted, (((0,), (0,)), ((), ())), preferred_element_type=jnp.float32
    )
    totals = lax.psum(projected, "pts")
    every_proj = lax.all_gather(
        totals[None].astype(jnp.bfloat16), "out", axis=0, tiled=True
    ).astype(jnp.float32)
    mixed = jnp.einsum("q,qfs->fs", coreg_row, every_proj, precision=highest).astype(jnp.bfloat16)
    regular = jnp.einsum(
        "bnf,fs->bns", feats_all, mixed, preferred_element_type=jnp.float32
    ).reshape(shard_rows, -1)
    gradient = ratio * data_grad + regular
    return (rep_weights[0] - STEP_SIZE * gradient)[None]


def solution(mesh):
    in_specs = (P("pts", None), P("out", "pts", None), P(), P(), P(), P(), P(), P())
    out_specs = P("out", "pts", None)
    return jax.shard_map(shards, mesh=mesh, in_specs=in_specs, out_specs=out_specs, check_vma=False)
```

profile of v0, /device:TPU:1, one launch (start us, length us, event | category | flops | bytes accessed | tf_op | source)
XLA Modules:
  0.0 700.8 jit_solution(12898487641695800740)
XLA Ops:
  0.0 1.0 convert_element_type.39
  1.1 131.9 %while.13 = (s32[]{:T(128)}, f32[2048,16]{0,1:T(8,128)S(1)}, bf16[8,512,2048]{2,1,0:T(8,128)(2,1)}, bf16[8,512,256]{2,1,0:T(8,128)(2,1)}, bf16[256,2048]{1,0:T(8...) while((s32[]{:T(128)}, f32[2048,16]{0,1:T(8,128)S(1)}, ...), condition=%wide.region_5.6_spmd.clone, body=%wide.region_4.5_spmd.clone.sunk | while | flops 573636608 | bytes 7890035 | solution.py:54
  1.1 16.1 %bitcast_dynamic-update-slice_fusion.2 = (bf16[8,512,2048]{2,1,0:T(8,128)(2,1)}, bf16[512,2048]{1,0:T(8,128)(2,1)S(1)}) fusion(bf16[8,512,2048]{2,1,0:T(8,128)(2,1)} %get-tuple-element.159, s32[]{:T(128)S(6)} %copy.27, f32[2048]{0:T(1024)} %get-tuple-element.171, bf16[256,2048]{1,0:T(8,128)(2,1)} %get-tuple-element.170, ...), kind=kOutput, calls=%fused_computation.3.clone.1 | convolution fusion | flops 540016640 | bytes 5514240 | tf_op jit(solution)/shard_map/while/body/eval_jaxpr/dot_general | solution.py:22
  17.2 0.4 convolution_add_fusion.2
  17.6 16.1 %bitcast_dynamic-update-slice_fusion.2 = (bf16[8,512,2048]{2,1,0:T(8,128)(2,1)}, bf16[512,2048]{1,0:T(8,128)(2,1)S(1)}) fusion(bf16[8,512,2048]{2,1,0:T(8,128)(2,1)} %get-tuple-element.159, s32[]{:T(128)S(6)} %copy.27, f32[2048]{0:T(1024)} %get-tuple-element.171, bf16[256,2048]{1,0:T(8,128)(2,1)} %get-tuple-element.170, ...), kind=kOutput, calls=%fused_computation.3.clone.1 | convolution fusion | flops 540016640 | bytes 5514240 | tf_op jit(solution)/shard_map/while/body/eval_jaxpr/dot_general | solution.py:22
  33.7 0.4 convolution_add_fusion.2
  34.1 16.1 %bitcast_dynamic-update-slice_fusion.2 = (bf16[8,512,2048]{2,1,0:T(8,128)(2,1)}, bf16[512,2048]{1,0:T(8,128)(2,1)S(1)}) fusion(bf16[8,512,2048]{2,1,0:T(8,128)(2,1)} %get-tuple-element.159, s32[]{:T(128)S(6)} %copy.27, f32[2048]{0:T(1024)} %get-tuple-element.171, bf16[256,2048]{1,0:T(8,128)(2,1)} %get-tuple-element.170, ...), kind=kOutput, calls=%fused_computation.3.clone.1 | convolution fusion | flops 540016640 | bytes 5514240 | tf_op jit(solution)/shard_map/while/body/eval_jaxpr/dot_general | solution.py:22
  50.2 0.4 convolution_add_fusion.2
  50.6 16.1 %bitcast_dynamic-update-slice_fusion.2 = (bf16[8,512,2048]{2,1,0:T(8,128)(2,1)}, bf16[512,2048]{1,0:T(8,128)(2,1)S(1)}) fusion(bf16[8,512,2048]{2,1,0:T(8,128)(2,1)} %get-tuple-element.159, s32[]{:T(128)S(6)} %copy.27, f32[2048]{0:T(1024)} %get-tuple-element.171, bf16[256,2048]{1,0:T(8,128)(2,1)} %get-tuple-element.170, ...), kind=kOutput, calls=%fused_computation.3.clone.1 | convolution fusion | flops 540016640 | bytes 5514240 | tf_op jit(solution)/shard_map/while/body/eval_jaxpr/dot_general | solution.py:22
  66.7 0.4 convolution_add_fusion.2
  67.1 16.1 %bitcast_dynamic-update-slice_fusion.2 = (bf16[8,512,2048]{2,1,0:T(8,128)(2,1)}, bf16[512,2048]{1,0:T(8,128)(2,1)S(1)}) fusion(bf16[8,512,2048]{2,1,0:T(8,128)(2,1)} %get-tuple-element.159, s32[]{:T(128)S(6)} %copy.27, f32[2048]{0:T(1024)} %get-tuple-element.171, bf16[256,2048]{1,0:T(8,128)(2,1)} %get-tuple-element.170, ...), kind=kOutput, calls=%fused_computation.3.clone.1 | convolution fusion | flops 540016640 | bytes 5514240 | tf_op jit(solution)/shard_map/while/body/eval_jaxpr/dot_general | solution.py:22
  83.2 0.4 convolution_add_fusion.2
  83.6 16.1 %bitcast_dynamic-update-slice_fusion.2 = (bf16[8,512,2048]{2,1,0:T(8,128)(2,1)}, bf16[512,2048]{1,0:T(8,128)(2,1)S(1)}) fusion(bf16[8,512,2048]{2,1,0:T(8,128)(2,1)} %get-tuple-element.159, s32[]{:T(128)S(6)} %copy.27, f32[2048]{0:T(1024)} %get-tuple-element.171, bf16[256,2048]{1,0:T(8,128)(2,1)} %get-tuple-element.170, ...), kind=kOutput, calls=%fused_computation.3.clone.1 | convolution fusion | flops 540016640 | bytes 5514240 | tf_op jit(solution)/shard_map/while/body/eval_jaxpr/dot_general | solution.py:22
  99.7 0.4 convolution_add_fusion.2
  100.1 16.1 %bitcast_dynamic-update-slice_fusion.2 = (bf16[8,512,2048]{2,1,0:T(8,128)(2,1)}, bf16[512,2048]{1,0:T(8,128)(2,1)S(1)}) fusion(bf16[8,512,2048]{2,1,0:T(8,128)(2,1)} %get-tuple-element.159, s32[]{:T(128)S(6)} %copy.27, f32[2048]{0:T(1024)} %get-tuple-element.171, bf16[256,2048]{1,0:T(8,128)(2,1)} %get-tuple-element.170, ...), kind=kOutput, calls=%fused_computation.3.clone.1 | convolution fusion | flops 540016640 | bytes 5514240 | tf_op jit(solution)/shard_map/while/body/eval_jaxpr/dot_general | solution.py:22
  116.2 0.4 convolution_add_fusion.2
  116.6 16.1 %bitcast_dynamic-update-slice_fusion.2 = (bf16[8,512,2048]{2,1,0:T(8,128)(2,1)}, bf16[512,2048]{1,0:T(8,128)(2,1)S(1)}) fusion(bf16[8,512,2048]{2,1,0:T(8,128)(2,1)} %get-tuple-element.159, s32[]{:T(128)S(6)} %copy.27, f32[2048]{0:T(1024)} %get-tuple-element.171, bf16[256,2048]{1,0:T(8,128)(2,1)} %get-tuple-element.170, ...), kind=kOutput, calls=%fused_computation.3.clone.1 | convolution fusion | flops 540016640 | bytes 5514240 | tf_op jit(solution)/shard_map/while/body/eval_jaxpr/dot_general | solution.py:22
  132.7 0.4 convolution_add_fusion.2
  133.0 2.2 multiply_reduce_fusion
  135.3 3.4 gather_fusion
  138.9 252.6 %all-reduce.3 = bf16[512,256]{1,0:T(8,128)(2,1)S(1)} all-reduce(f32[512,256]{1,0:T(8,128)S(1)} %convert_select_fusion), channel_id=1, replica_groups=mesh['pts'=64,'out'=4] {'pts'}, use_global_device_ids=true, to_apply=%region_0.1 | all-reduce | flops 131072 | bytes 786432 | tf_op jit(solution)/shard_map/psum | solution.py:37
  391.6 7.9 %multiply_convert_fusion.1 = bf16[512,4096]{1,0:T(8,128)(2,1)S(1)} fusion(bf16[4096,256]{1,0:T(8,128)(2,1)} %bitcast.80, f32[4096]{0:T(1024)S(1)} %multiply_reduce_fusion, f32[512]{0:T(512)S(1)} %multiply_reduce_fusion.1, bf16[512,256]{1,0:T(8,128)(2,1)S(1)} %all-reduce.3), kind=kOutput, calls=%fused_computation.10 | convolution fusion | flops 1098907648 | bytes 6572032 | tf_op jit(solution)/shard_map/dot_general | solution.py:15
  399.5 2.0 copy-done.1
  401.5 1.2 convolution_bitcast_fusion.2
  402.6 246.2 %all-reduce.4 = (bf16[2048,16]{0,1:T(8,128)(2,1)S(1)}, f32[1,512,16]{1,2,0:T(8,128)S(1)}) all-reduce(f32[2048,16]{0,1:T(8,128)S(1)} %get-tuple-element.44, f32[1,512,16]{1,2,0:T(8,128)S(1)} %convolution_bitcast_fusion.2), channel_id=1, replica_groups=mesh['pts'=64,'out'=4] {'pts'}, use_global_device_ids=true, to_apply=%region_6.7 | all-reduce | flops 40960 | bytes 262144 | tf_op jit(solution)/shard_map/psum | solution.py:69
  648.9 10.2 %all-gather = bf16[8192,16]{0,1:T(8,128)(2,1)S(1)} all-gather(bf16[2048,16]{0,1:T(8,128)(2,1)S(1)} %get-tuple-element.97), channel_id=2, replica_groups=mesh['pts'=64,'out'=4] {'out'}, dimensions={0}, use_global_device_ids=true | all-gather | bytes 327680 | tf_op jit(solution)/shard_map/all_gather | solution.py:70
  659.3 10.5 %fusion.18 = bf16[1,2048,16]{0,1,2:T(8,128)(2,1)} fusion(bf16[4,2048,16]{1,0,2:T(4,128)(2,1)S(1)} %reshape.22, f32[4,4]{1,0:T(4,128)S(1)} %copy-done, s32[]{:T(128)S(6)} %select_n.12), kind=kOutput, calls=%fused_computation.34 | convolution fusion | flops 1572864 | bytes 328196 | tf_op jit(solution)/shard_map/q,qfs->fs/dot_general | solution.py:73
  669.8 7.0 copy.17
  676.8 10.3 %convolution_bitcast_fusion = f32[8,2,8,512]{3,2,1,0:T(8,128)S(1)} fusion(bf16[8,512,2048]{2,1,0:T(8,128)(2,1)} %get-tuple-element.43, bf16[1,2048,16]{1,2,0:T(8,128)(2,1)S(1)} %copy.17), kind=kOutput, calls=%fused_computation.17 | convolution fusion | flops 268435456 | bytes 17104896 | tf_op jit(solution)/shard_map/bnf,fs->bns/dot_general | solution.py:74
  687.1 9.1 %all_gather.6 = f32[4,512,16]{1,2,0:T(8,128)S(1)} all-gather(f32[1,512,16]{1,2,0:T(8,128)S(1)} %get-tuple-element.98), channel_id=1, replica_groups=mesh['pts'=64,'out'=4] {'out'}, dimensions={0}, use_global_device_ids=true | all-gather | bytes 163840 | tf_op jit(solution)/shard_map/all_gather | solution.py:62
  696.2 0.5 fusion.11
  697.2 3.6 fusion.9
  (24 shorter events, 1.1 us)
Async XLA Ops:
  0.0 659.3 %copy-start = (f32[4,4]{1,0:T(4,128)S(1)}, f32[4,4]{1,0:T(4,128)}, u32[]{:S(2)}) copy-start(f32[4,4]{1,0:T(4,128)} %param.15) | copy-start | bytes 196
  1.1 134.2 %copy-start.3 = (s32[512]{0:T(512)S(1)}, s32[512]{0:T(512)}, u32[]{:S(2)}) copy-start(s32[512]{0:T(512)} %param.12) | copy-start | bytes 6148
  399.5 2.0 copy-start.1
  676.8 19.4 %copy-start.4 = (f32[4,512,16]{1,2,0:T(8,128)S(1)}, f32[4,512,16]{1,2,0:T(8,128)}, u32[]{:S(2)}) copy-start(f32[4,512,16]{1,2,0:T(8,128)} %param.13) | copy-start | bytes 393220
  676.8 19.4 %copy-start.5 = (f32[4]{0:T(128)S(1)}, f32[4]{0:T(128)}, u32[]{:S(2)}) copy-start(f32[4]{0:T(128)} %param.14) | copy-start | bytes 52
  676.8 20.4 %copy-start.2 = (f32[1,4096,16]{1,2,0:T(8,128)S(1)}, f32[1,4096,16]{1,2,0:T(8,128)}, u32[]{:S(2)}) copy-start(f32[1,4096,16]{1,2,0:T(8,128)} %param.11) | copy-start | bytes 786436
where the time goes:
time: 711 us; the launch traced here: 701 us
  blocking collectives  518 us (73%)
  matrix products  166 us (23%)
  local copies, waits for them, and re-layouts  12.8 us (2%)
    psum x1, blocking collectives, shards(): batch_rows = lax.psum(picked, 'pts').astype(jnp.bfloat16)  253 us
    psum x1, blocking collectives, shards(): totals = lax.psum(projected, 'pts')  246 us
    dot_general x8, matrix products, feature_map(): jnp.dot(slab, freq_cols, preferred_element_type=jnp.float32) + phase_cols  129 us

commit v1 on v0

v1 whole, which is shorter than its diff:
```python
import math

import jax
import jax.numpy as jnp
from jax import lax
from jax.sharding import Mesh
from jax.sharding import PartitionSpec as P

LENGTH = 0.5
STEP_SIZE = 0.5
SLOTS = 8
SIN_TURNS = (
    6.283185160088695,
    -41.34165503124932,
    81.60100406363227,
    -76.54978208799582,
    39.53670460277009,
)
POINT_AXES = ("z", "y", "core")
CHIP_AXES = ("z", "y")


def cos_turns(turns):
    rest = turns - jnp.round(turns)
    quarter = 0.25 - jnp.abs(rest)
    square = quarter * quarter
    poly = jnp.float32(SIN_TURNS[-1])
    for coefficient in SIN_TURNS[-2::-1]:
        poly = poly * square + jnp.float32(coefficient)
    return poly * quarter


def matern(squared):
    scaled_square = (5.0 / (LENGTH * LENGTH)) * jnp.maximum(squared, 0.0)
    scaled_r = scaled_square * lax.rsqrt(jnp.maximum(scaled_square, 1e-30))
    return ((1.0 + scaled_r + scaled_square * (1.0 / 3.0)) * jnp.exp(-scaled_r)).astype(jnp.bfloat16)


def swap_core(value):
    return lax.ppermute(value, "core", [(0, 1), (1, 0)])


def shards(points, rep_weights, batch_index, targets, noise_var, coregion, frequencies, phases):
    highest = lax.Precision.HIGHEST
    n_out = lax.axis_size("out")
    n_chips = lax.axis_size("z") * lax.axis_size("y")
    n_pts = 2 * n_chips
    rows, width = points.shape
    draws = rep_weights.shape[2]
    minibatch = batch_index.shape[0]
    total_features = frequencies.shape[1]
    own_rows = minibatch // n_out
    own_features = total_features // n_out
    out = lax.axis_index("out")
    core = lax.axis_index("core")
    chip = lax.axis_index("z") * lax.axis_size("y") + lax.axis_index("y")
    shard = chip * 2 + core
    ratio = (rows * n_pts) / minibatch

    m_iota = lax.iota(jnp.int32, minibatch)
    before = (batch_index[None, :] < batch_index[:, None]) | (
        (batch_index[None, :] == batch_index[:, None]) & (m_iota[None, :] < m_iota[:, None])
    )
    rank = jnp.sum(before.astype(jnp.int32), 1)
    own_rank = lax.iota(jnp.int32, own_rows) * n_out + out
    chosen = own_rank[:, None] == rank[None, :]
    own_index = jnp.sum(jnp.where(chosen, batch_index[None, :], 0), 1)
    own_shard = own_index // rows
    starts = jnp.sum((own_index[None, :] < (own_shard * rows)[:, None]).astype(jnp.int32), 1)
    slot = lax.iota(jnp.int32, own_rows) - starts
    same_shard = (batch_index // rows)[None, :] == (batch_index // rows)[:, None]
    most = jnp.max(jnp.sum(same_shard.astype(jnp.int32), 1))
    overflow = most > SLOTS * n_out

    local = jnp.pad(own_index - shard * rows, (0, SLOTS))
    first = jnp.sum((own_index < shard * rows).astype(jnp.int32))
    mine = jnp.clip(lax.dynamic_slice(local, (first,), (SLOTS,)), 0, rows - 1)
    sent_rows = points[mine].reshape(SLOTS, 2, width // 2).transpose(1, 0, 2).reshape(2 * SLOTS, width // 2)
    sent_rows = jnp.broadcast_to(sent_rows[None], (n_chips, 2 * SLOTS, width // 2))
    got_rows = lax.all_to_all(sent_rows, CHIP_AXES, 0, 0)

    own_weights = rep_weights[0].T
    low = own_weights.astype(jnp.bfloat16)
    all_low = [low]
    for k in range(1, n_out):
        all_low.append(lax.ppermute(low, "out", [(i, (i + k) % n_out) for i in range(n_out)]))

    freq = lax.dynamic_slice(frequencies, (0, out * own_features), (width, own_features))
    phase = lax.dynamic_slice(phases, (out * own_features,), (own_features,))
    turns = lax.dot_general(
        freq, points, (((0,), (1,)), ((), ())), preferred_element_type=jnp.float32
    ) * (0.5 / math.pi) + (phase * (0.5 / math.pi))[:, None]
    feats = (math.sqrt(2.0 / total_features) * cos_turns(turns)).astype(jnp.bfloat16)

    weights = jnp.concatenate(all_low, 0)
    projected = lax.dot_general(
        weights, feats, (((1,), (1,)), ((), ())), preferred_element_type=jnp.float32
    )
    cols = n_out * draws
    tiles = projected.reshape(cols // 8, 8, own_features // 128, 128).transpose(0, 2, 1, 3)
    tiles = tiles.reshape(n_chips, 8, 128)
    got = jnp.sum(lax.all_to_all(tiles, CHIP_AXES, 0, 0), 0)
    got = got + swap_core(got)
    got = lax.all_to_all(jnp.broadcast_to(got[None], (n_chips, 8, 128)), CHIP_AXES, 0, 0)
    projected = got.reshape(cols // 8, own_features // 128, 8, 128).transpose(0, 2, 1, 3)
    projected = projected.reshape(n_out, draws * own_features)

    other_rows = swap_core(got_rows)

    def place(_):
        own_core = (own_shard % 2) == core
        at = (own_shard // 2) * (2 * SLOTS) + slot
        columns = lax.iota(jnp.int32, n_chips * 2 * SLOTS)
        halves = []
        for half in range(2):
            part = 0.0
            for source, held in ((own_core, got_rows), (~own_core, other_rows)):
                pick = ((at + half * SLOTS)[:, None] == columns[None, :]) & source[:, None]
                part = part + jnp.dot(
                    pick.astype(jnp.bfloat16),
                    held.reshape(n_chips * 2 * SLOTS, width // 2),
                    preferred_element_type=jnp.float32,
                )
            halves.append(part)
        return jnp.concatenate(halves, 1).astype(jnp.bfloat16)

    def fetch(_):
        at = own_index - shard * rows
        inside = (at >= 0) & (at < rows)
        picked = jnp.where(inside[:, None], points[jnp.clip(at, 0, rows - 1)].astype(jnp.float32), 0.0)
        return lax.psum(picked, POINT_AXES).astype(jnp.bfloat16)

    batch_rows = lax.cond(overflow, fetch, place, 0)

    row_norm = jnp.sum(jnp.square(batch_rows.astype(jnp.float32)), 1)
    col_norm = jnp.sum(jnp.square(points.astype(jnp.float32)), 1)
    inner = lax.dot_general(
        batch_rows, points, (((1,), (1,)), ((), ())), preferred_element_type=jnp.float32
    )
    kern = matern(row_norm[:, None] + col_norm[None, :] - 2.0 * inner)
    partial = lax.dot_general(
        weights, kern, (((1,), (1,)), ((), ())), preferred_element_type=jnp.float32
    )
    half_cols = cols // 2
    halves = partial.reshape(2, half_cols, own_rows)
    kept = lax.dynamic_index_in_dim(halves, core, 0, keepdims=False)
    given = lax.dynamic_index_in_dim(halves, 1 - core, 0, keepdims=False)
    kept = (kept + swap_core(given)).astype(jnp.bfloat16)
    kept = lax.all_to_all(jnp.broadcast_to(kept[None], (n_chips, half_cols, own_rows)), CHIP_AXES, 0, 0)
    kept = jnp.sum(kept.astype(jnp.float32), 0)
    other = swap_core(kept)
    lower = jnp.where(core == 0, kept, other)
    upper = jnp.where(core == 0, other, kept)
    partial = jnp.concatenate([lower, upper], 0).reshape(n_out, draws * own_rows)

    order = (out - lax.iota(jnp.int32, n_out)) % n_out
    mixer = coregion[order][:, order]
    noise = noise_var[order]
    own_targets = jnp.einsum("im,qms->qsi", chosen.astype(jnp.float32), targets[order], precision=highest)
    fitted = jnp.dot(mixer, partial, precision=highest)
    scaled = (fitted - own_targets.reshape(n_out, draws * own_rows)) / noise[:, None]
    weighted = jnp.dot(mixer, scaled, precision=highest).astype(jnp.bfloat16)
    mixed = jnp.dot(mixer, projected, precision=highest).astype(jnp.bfloat16)
    gradient = ratio * jnp.dot(
        weighted.reshape(cols, own_rows), kern, preferred_element_type=jnp.float32
    ) + jnp.dot(mixed.reshape(cols, own_features), feats, preferred_element_type=jnp.float32)
    gradient = gradient.reshape(n_out, draws, rows)
    total = gradient[0]
    sent = gradient[1:].astype(jnp.bfloat16)
    for k in range(1, n_out):
        part = lax.ppermute(sent[k - 1], "out", [(i, (i - k) % n_out) for i in range(n_out)])
        total = total + part.astype(jnp.float32)
    return (own_weights - STEP_SIZE * total).T[None]


def solution(mesh):
    fine = Mesh(mesh.devices.reshape(8, 4, 2, 4), ("z", "y", "core", "out"))
    in_specs = (P(POINT_AXES, None), P("out", POINT_AXES, None), P(), P(), P(), P(), P(), P())
    out_specs = P("out", POINT_AXES, None)
    return jax.shard_map(shards, mesh=fine, in_specs=in_specs, out_specs=out_specs, check_vma=False)
```

time: 711 us -> 123 us (0.17); the launches traced: 701 us -> 122 us
  blocking collectives: 518 us -> 0 us
  matrix products: 166 us -> 23.9 us
  starting transfers between devices: 0 us -> 46.8 us
  waiting for transfers between devices: 0 us -> 27.8 us
    psum x2 -> x0, blocking collectives: 499 us -> none  [the longest x1 253 us: shards(): batch_rows = lax.psum(picked, 'pts').astype(jnp.bfloat16)]
    dot_general x23 -> x14, matrix products: 166 us -> 23.9 us  [the longest x1 7.77 us: shards(): lax.dot_general(freq, points, (((0,), (1,)), ((), ())), preferred_element...]
    all_to_all x0 -> x4, starting transfers between devices: none -> 28.2 us  [the longest x1 11.3 us: shards(): got_rows = lax.all_to_all(sent_rows, CHIP_AXES, 0, 0)]
    all_to_all x0 -> x4, waiting for transfers between devices: none -> 20.9 us  [the longest x1 8.55 us: shards(): lax.all_to_all(jnp.broadcast_to(got[None], (n_chips, 8, 128)), CHIP_AXES,...]
    all_gather x2 -> x0, blocking collectives: 19.3 us -> none  [the longest x1 10.2 us: shards(): lax.all_gather(totals[None].astype(jnp.bfloat16), 'out', axis=0, tiled=True)]
    ppermute x0 -> x10, starting transfers between devices: none -> 18.6 us  [the longest x4 9.99 us: swap_core(): return lax.ppermute(value, 'core', [(0, 1), (1, 0)])]
    dot_general x2 -> x0, local copies, waits for them, and re-layouts: 7.13 us -> none  [the longest x1 6.99 us: shards(): jnp.einsum('q,qfs->fs', coreg_row, every_proj, precision=highest)]
  transfers between devices with their start and end apart: 0 -> 14, of which waited for: 0 -> 6; matrix products, arithmetic and copies ran while one was open for 0% -> 30% of each run, Pallas kernels for 0% -> 0%
where the time goes in v1:
time: 123 us; the launch traced here: 122 us
  starting transfers between devices  46.8 us (38%)
  waiting for transfers between devices  27.8 us (23%)
  matrix products  23.9 us (19%)
  local copies, waits for them, and re-layouts  10.2 us (8%)
  other arithmetic  10 us (8%)
  between operations  2.93 us (2%)
    all_to_all x1, starting transfers between devices, shards(): got_rows = lax.all_to_all(sent_rows, CHIP_AXES, 0, 0)  11.3 us
    ppermute x4, starting transfers between devices, swap_core(): return lax.ppermute(value, 'core', [(0, 1), (1, 0)])  9.99 us
    all_to_all x1, starting transfers between devices, shards(): got = jnp.sum(lax.all_to_all(tiles, CHIP_AXES, 0, 0), 0)  9.14 us
    all_to_all x1, waiting for transfers between devices, shards(): lax.all_to_all(jnp.broadcast_to(got[None], (n_chips, 8, 128)), CHIP_AXES,...  8.55 us
    dot_general x1, matrix products, shards(): lax.dot_general(freq, points, (((0,), (1,)), ((), ())), preferred_element...  7.77 us
    all_to_all x1, waiting for transfers between devices, shards(): lax.all_to_all(jnp.broadcast_to(kept[None], (n_chips, half_cols, own_rows...  6.91 us
    ppermute x3, waiting for transfers between devices, shards(): lax.ppermute(sent[k - 1], 'out', [(i, (i - k) % n_out) for i in range(n_o...  5.69 us
    all_to_all x1, waiting for transfers between devices, shards(): got = jnp.sum(lax.all_to_all(tiles, CHIP_AXES, 0, 0), 0)  5.44 us
  transfers between devices with their start and end apart: 14, of which 6 were waited for; matrix products, arithmetic and copies ran while one was open for 30% of the time, Pallas kernels for 0%

profile of v1, /device:TPU:1, one launch (start us, length us, event | category | flops | bytes accessed | tf_op | source)
XLA Modules:
  0.0 121.9 jit_solution(3299220741032766952)
XLA Ops:
  0.0 1.1 bitcast_convert_fusion
  1.1 3.4 %collective-permute-start.2 = (bf16[16,4096]{1,0:T(8,128)(2,1)S(1)}, bf16[16,4096]{1,0:T(8,128)(2,1)S(1)}, u32[]{:S(2)}, u32[]{:S(2)}) collective-permute-start(bf16[16,4096]{1,0:T(8,128)(2,1)S(1)} %bitcast_convert_fusion), channel_id=1, source_target_pairs={{0,3},{1,0},{2,1},{3,2},{4,7},{5,4},{6,5},{7,6},{8,11},{9,8},{10,9... | collective-permute-start | bytes 393224 | tf_op jit(solution)/shard_map/ppermute | solution.py:86
  5.6 1.1 convert_reduce_fusion
  10.2 2.4 %gather_fusion.3 = bf16[8,256]{1,0:T(8,128)(2,1)S(1)} fusion(bf16[4096,256]{1,0:T(8,128)(2,1)} %param.10, s32[1024]{0:T(1024)S(1)} %pad_clamp_fusion.1), kind=kCustom, calls=%fused_computation.3 | custom fusion | bytes 8224 | tf_op jit(solution)/shard_map/gather | solution.py:78
  13.3 11.3 %all-to-all-start = ((bf16[32,16,128]{2,1,0:T(8,128)(2,1)}), bf16[32,16,128]{2,1,0:T(8,128)(2,1)}, u32[]{:S(2)}, u32[]{:S(2)}) async-start(bf16[32,16,128]{2,1,0:T(8,128)(2,1)} %broadcast_in_dim.38), calls=%async_computation | async-start | bytes 262144 | tf_op jit(solution)/shard_map/all_to_all | solution.py:80
  24.7 2.8 %multiply_reduce_fusion = f32[4096]{0:T(1024)} fusion(bf16[4096,256]{1,0:T(8,128)(2,1)} %param.10), kind=kLoop, calls=%fused_computation.53 | loop fusion | flops 3141632 | bytes 2113536 | tf_op jit(solution)/shard_map/reduce_sum | solution.py:136
  28.3 7.8 %multiply_convert_fusion = bf16[512,4096]{1,0:T(8,128)(2,1)S(1)} fusion(bf16[4096,256]{1,0:T(8,128)(2,1)} %param.10, f32[512]{0:T(512)S(1)} %dynamic-slice_multiply_fusion, bf16[256,2048]{1,0:T(8,128)(2,1)S(1)} %copy-done, s32[]{:T(128)S(6)} %select_n.106), kind=kOutput, calls=%fused_computation.43 | convolution fusion | flops 1111490560 | bytes 6555652 | tf_op jit(solution)/shard_map/dot_general | solution.py:90
  36.2 2.1 %copy-done.2 = bf16[512,4096]{1,0:T(8,128)(2,1)} copy-done((bf16[512,4096]{1,0:T(8,128)(2,1)}, bf16[512,4096]{1,0:T(8,128)(2,1)S(1)}, u32[]{:S(2)}) %copy-start.2) | copy-done | bytes 4194328
  38.3 3.1 %fusion.38 = f32[64,512]{1,0:T(8,128)} fusion(bf16[512,4096]{1,0:T(8,128)(2,1)S(1)} %multiply_convert_fusion, bf16[16,4096]{1,0:T(8,128)(2,1)S(1)} %collective-permute-done.2, bf16[16,4096]{1,0:T(8,128)(2,1)} %collective-permute-done.1, bf16[16,4096]{1,0:T(8,128)(2,1)} %collective-permute-done, bf16[16,4096]{1,0:T(8,128)(2,1)S(1)} %bitcast_convert_fusion), kind=kOutput, calls=%fused_computation.80 | convolution fusion | flops 270532608 | bytes 4849664 | tf_op jit(solution)/shard_map/dot_general | solution.py:96
  41.3 9.1 %all-to-all-start.2 = ((f32[32,8,128]{2,1,0:T(8,128)}), f32[32,8,128]{2,1,0:T(8,128)S(1)}, u32[]{:S(2)}, u32[]{:S(2)}) async-start(f32[32,8,128]{2,1,0:T(8,128)} %bitcast.15), calls=%async_computation.2 | async-start | bytes 262144 | tf_op jit(solution)/shard_map/all_to_all | solution.py:102
  52.0 2.4 %collective-permute-start.3 = (bf16[32,16,128]{2,1,0:T(8,128)(2,1)}, bf16[32,16,128]{2,1,0:T(8,128)(2,1)}, u32[]{:S(2)}, u32[]{:S(2)}) collective-permute-start(bf16[32,16,128]{2,1,0:T(8,128)(2,1)} %all-to-all-done), channel_id=1, source_target_pairs={{0,4},{4,0},{1,5},{5,1},{2,6},{6,2},{3,7},{7,3},{8,12},{12,8},{9,1... | collective-permute-start | bytes 393224 | tf_op jit(solution)/shard_map/ppermute | solution.py:40
  54.4 5.4 %all-to-all-done.2 = f32[32,8,128]{2,1,0:T(8,128)S(1)} async-done(((f32[32,8,128]{2,1,0:T(8,128)}), f32[32,8,128]{2,1,0:T(8,128)S(1)}, u32[]{:S(2)}, u32[]{:S(2)}) %all-to-all-start.2) | async-done | bytes 131104 | tf_op jit(solution)/shard_map/all_to_all | solution.py:102
  59.9 3.6 %collective-permute-start.6 = (f32[8,128]{1,0:T(8,128)S(1)}, f32[8,128]{1,0:T(8,128)}, u32[]{:S(2)}, u32[]{:S(2)}) collective-permute-start(f32[8,128]{1,0:T(8,128)S(1)} %reduce_sum.89), channel_id=1, source_target_pairs={{0,4},{4,0},{1,5},{5,1},{2,6},{6,2},{3,7},{7,3},{8,12},{12,8},{9,1... | collective-permute-start | bytes 12296 | tf_op jit(solution)/shard_map/ppermute | solution.py:40
  63.5 5.1 %conditional.6 = (bf16[128,256]{0,1:T(8,128)(2,1)S(1)}) conditional(s32[]{:T(128)} %convert_element_type.71, (s32[128]{0:T(128)S(1)}, s32[128]{0:T(128)S(1)}, pred[128]{0:T(512)(128)(4,1)S(1)}, s32[128]{0:T(128)S(1)}, s32[128]{0:T(128)S(1)}, /*index=5*/s32[128,128]{1,0:T(8,128)S(1)}, s32[128]{0:T(128)S(1)}, s32[]{:T(128)}, ...), branch_computations={%region_5.7_spmd, %region_7.9_spmd} | conditional | flops 67851136 | bytes 1057168
  63.7 1.2 fusion.7
  64.9 1.2 convolution_add_fusion
  66.1 1.2 fusion.4
  67.3 1.2 convolution_add_fusion.1
  68.7 2.3 %multiply_convert_fusion.1 = bf16[128,4096]{1,0:T(8,128)(2,1)S(1)} fusion(bf16[4096,256]{1,0:T(8,128)(2,1)S(1)} %copy-done.4, f32[4096]{0:T(1024)} %multiply_reduce_fusion, f32[128]{0:T(128)S(1)} %multiply_reduce_fusion.1, bf16[128,256]{0,1:T(8,128)(2,1)S(1)} %get-tuple-element.86), kind=kOutput, calls=%fused_computation.57 | convolution fusion | flops 275251200 | bytes 3228160 | tf_op jit(solution)/shard_map/dot_general | solution.py:137
  71.0 1.0 copy-done.5
  71.9 1.5 %fusion.39 = f32[64,128]{1,0:T(8,128)S(1)} fusion(bf16[128,4096]{1,0:T(8,128)(2,1)S(1)} %multiply_convert_fusion.1, bf16[16,4096]{1,0:T(8,128)(2,1)S(1)} %copy-done.9, bf16[16,4096]{1,0:T(8,128)(2,1)} %collective-permute-done.1, bf16[16,4096]{1,0:T(8,128)(2,1)} %collective-permute-done, bf16[16,4096]{1,0:T(8,128)(2,1)S(1)} %bitcast_convert_fusion), kind=kOutput, calls=%fused_computation.81 | convolution fusion | flops 69206016 | bytes 1605632 | tf_op jit(solution)/shard_map/dot_general | solution.py:141
  74.8 3.9 %all-to-all-start.3 = ((f32[32,8,128]{2,1,0:T(8,128)}), f32[32,8,128]{2,1,0:T(8,128)S(1)}, u32[]{:S(2)}, u32[]{:S(2)}) async-start(f32[32,8,128]{2,1,0:T(8,128)} %broadcast_in_dim.40), calls=%async_computation.3 | async-start | bytes 262144 | tf_op jit(solution)/shard_map/all_to_all | solution.py:104
  78.8 1.1 collective-permute-done.4
  79.9 8.6 %all-to-all-done.3 = f32[32,8,128]{2,1,0:T(8,128)S(1)} async-done(((f32[32,8,128]{2,1,0:T(8,128)}), f32[32,8,128]{2,1,0:T(8,128)S(1)}, u32[]{:S(2)}, u32[]{:S(2)}) %all-to-all-start.3) | async-done | bytes 131104 | tf_op jit(solution)/shard_map/all_to_all | solution.py:104
  89.2 3.9 %all-to-all-start.1 = ((bf16[32,32,128]{2,1,0:T(8,128)(2,1)}), bf16[32,32,128]{2,1,0:T(8,128)(2,1)S(1)}, u32[]{:S(2)}, u32[]{:S(2)}) async-start(bf16[32,32,128]{2,1,0:T(8,128)(2,1)} %broadcast_in_dim.39), calls=%async_computation.1 | async-start | bytes 524288 | tf_op jit(solution)/shard_map/all_to_all | solution.py:149
  96.6 6.9 %all-to-all-done.1 = bf16[32,32,128]{2,1,0:T(8,128)(2,1)S(1)} async-done(((bf16[32,32,128]{2,1,0:T(8,128)(2,1)}), bf16[32,32,128]{2,1,0:T(8,128)(2,1)S(1)}, u32[]{:S(2)}, u32[]{:S(2)}) %all-to-all-start.1) | async-done | bytes 262176 | tf_op jit(solution)/shard_map/all_to_all | solution.py:149
  103.5 3.8 %collective-permute-start.5 = (f32[32,128]{1,0:T(8,128)S(1)}, f32[32,128]{1,0:T(8,128)S(1)}, u32[]{:S(2)}, u32[]{:S(2)}) collective-permute-start(f32[32,128]{1,0:T(8,128)S(1)} %convert_reduce_fusion.2), channel_id=1, source_target_pairs={{0,4},{4,0},{1,5},{5,1},{2,6},{6,2},{3,7},{7,3},{8,12},{12,8},{9,1... | collective-permute-start | bytes 49160 | tf_op jit(solution)/shard_map/ppermute | solution.py:40
  107.3 3.0 %fusion.56 = f32[64,4096]{1,0:T(8,128)S(1)} fusion(bf16[64,512]{1,0:T(8,128)(2,1)S(1)} %reshape.148, bf16[512,4096]{1,0:T(8,128)(2,1)} %copy-done.2), kind=kOutput, calls=%fused_computation.126 | convolution fusion | flops 268435456 | bytes 5308416 | tf_op jit(solution)/shard_map/dot_general | solution.py:166
  111.3 1.6 %collective-permute-start.9 = (bf16[16,4096]{1,0:T(8,128)(2,1)S(1)}, bf16[16,4096]{1,0:T(8,128)(2,1)S(1)}, u32[]{:S(2)}, u32[]{:S(2)}) collective-permute-start(bf16[16,4096]{1,0:T(8,128)(2,1)S(1)} %get-tuple-element.75), channel_id=1, source_target_pairs={{0,1},{1,2},{2,3},{3,0},{4,5},{5,6},{6,7},{7,4},{8,9},{9,10},{10,1... | collective-permute-start | bytes 393224 | tf_op jit(solution)/shard_map/ppermute | solution.py:171
  112.9 1.7 %collective-permute-start.8 = (bf16[16,4096]{1,0:T(8,128)(2,1)S(1)}, bf16[16,4096]{1,0:T(8,128)(2,1)S(1)}, u32[]{:S(2)}, u32[]{:S(2)}) collective-permute-start(bf16[16,4096]{1,0:T(8,128)(2,1)S(1)} %get-tuple-element.76), channel_id=1, source_target_pairs={{0,2},{1,3},{2,0},{3,1},{4,6},{5,7},{6,4},{7,5},{8,10},{9,11},{10,... | collective-permute-start | bytes 393224 | tf_op jit(solution)/shard_map/ppermute | solution.py:171
  115.4 2.3 %collective-permute-done.9 = bf16[16,4096]{1,0:T(8,128)(2,1)S(1)} collective-permute-done((bf16[16,4096]{1,0:T(8,128)(2,1)S(1)}, bf16[16,4096]{1,0:T(8,128)(2,1)S(1)}, u32[]{:S(2)}, u32[]{:S(2)}) %collective-permute-start.9) | collective-permute-done | bytes 131104 | tf_op jit(solution)/shard_map/ppermute | solution.py:171
  117.7 3.4 %collective-permute-done.8 = bf16[16,4096]{1,0:T(8,128)(2,1)S(1)} collective-permute-done((bf16[16,4096]{1,0:T(8,128)(2,1)S(1)}, bf16[16,4096]{1,0:T(8,128)(2,1)S(1)}, u32[]{:S(2)}, u32[]{:S(2)}) %collective-permute-start.8) | collective-permute-done | bytes 131104 | tf_op jit(solution)/shard_map/ppermute | solution.py:171
  (85 shorter events, 13.5 us)
Async XLA Ops:
  0.0 28.3 %copy-start = (bf16[256,2048]{1,0:T(8,128)(2,1)S(1)}, bf16[256,2048]{1,0:T(8,128)(2,1)}, u32[]{:S(2)}) copy-start(bf16[256,2048]{1,0:T(8,128)(2,1)} %param.16) | copy-start | bytes 3145732
  1.1 35.1 %collective-permute-start.2 = (bf16[16,4096]{1,0:T(8,128)(2,1)S(1)}, bf16[16,4096]{1,0:T(8,128)(2,1)S(1)}, u32[]{:S(2)}, u32[]{:S(2)}) collective-permute-start(bf16[16,4096]{1,0:T(8,128)(2,1)S(1)} %bitcast_convert_fusion), channel_id=1, source_target_pairs={{0,3},{1,0},{2,1},{3,2},{4,7},{5,4},{6,5},{7,6},{8,11},{9,8},{10,9... | collective-permute-start | bytes 393224 | tf_op jit(solution)/shard_map/ppermute | solution.py:86
  4.4 31.7 %collective-permute-start.1 = (bf16[16,4096]{1,0:T(8,128)(2,1)S(1)}, bf16[16,4096]{1,0:T(8,128)(2,1)}, u32[]{:S(2)}, u32[]{:S(2)}) collective-permute-start(bf16[16,4096]{1,0:T(8,128)(2,1)S(1)} %bitcast_convert_fusion), channel_id=1, source_target_pairs={{0,2},{1,3},{2,0},{3,1},{4,6},{5,7},{6,4},{7,5},{8,10},{9,11},{10,... | collective-permute-start | bytes 393224 | tf_op jit(solution)/shard_map/ppermute | solution.py:86
  5.0 31.2 %collective-permute-start = (bf16[16,4096]{1,0:T(8,128)(2,1)S(1)}, bf16[16,4096]{1,0:T(8,128)(2,1)}, u32[]{:S(2)}, u32[]{:S(2)}) collective-permute-start(bf16[16,4096]{1,0:T(8,128)(2,1)S(1)} %bitcast_convert_fusion), channel_id=1, source_target_pairs={{0,1},{1,2},{2,3},{3,0},{4,5},{5,6},{6,7},{7,4},{8,9},{9,10},{10,1... | collective-permute-start | bytes 393224 | tf_op jit(solution)/shard_map/ppermute | solution.py:86
  6.7 3.6 %copy-start.12 = (s32[128]{0:T(128)}, s32[128]{0:T(128)S(1)}, u32[]{:S(2)}) copy-start(s32[128]{0:T(128)S(1)} %multiply_add_fusion) | copy-start | bytes 1540
  13.3 28.0 %all-to-all-start = ((bf16[32,16,128]{2,1,0:T(8,128)(2,1)}), bf16[32,16,128]{2,1,0:T(8,128)(2,1)}, u32[]{:S(2)}, u32[]{:S(2)}) async-start(bf16[32,16,128]{2,1,0:T(8,128)(2,1)} %broadcast_in_dim.38), calls=%async_computation | async-start | bytes 262144 | tf_op jit(solution)/shard_map/all_to_all | solution.py:80
  28.3 7.8 %copy-start.11 = (s32[512]{0:T(512)S(1)}, s32[512]{0:T(512)}, u32[]{:S(2)}) copy-start(s32[512]{0:T(512)} %param.12) | copy-start | bytes 6148
  36.1 2.1 %copy-start.2 = (bf16[512,4096]{1,0:T(8,128)(2,1)}, bf16[512,4096]{1,0:T(8,128)(2,1)S(1)}, u32[]{:S(2)}) copy-start(bf16[512,4096]{1,0:T(8,128)(2,1)S(1)} %multiply_convert_fusion) | copy-start | bytes 12582916
  36.1 27.4 %copy-start.4 = (bf16[4096,256]{1,0:T(8,128)(2,1)S(1)}, bf16[4096,256]{1,0:T(8,128)(2,1)}, u32[]{:S(2)}) copy-start(bf16[4096,256]{1,0:T(8,128)(2,1)} %param.10) | copy-start | bytes 6291460
  36.2 5.2 %copy-start.8 = (bf16[16,4096]{1,0:T(8,128)(2,1)}, bf16[16,4096]{1,0:T(8,128)(2,1)S(1)}, u32[]{:S(2)}) copy-start(bf16[16,4096]{1,0:T(8,128)(2,1)S(1)} %collective-permute-done.2) | copy-start | bytes 393220
  41.3 18.5 %all-to-all-start.2 = ((f32[32,8,128]{2,1,0:T(8,128)}), f32[32,8,128]{2,1,0:T(8,128)S(1)}, u32[]{:S(2)}, u32[]{:S(2)}) async-start(f32[32,8,128]{2,1,0:T(8,128)} %bitcast.15), calls=%async_computation.2 | async-start | bytes 262144 | tf_op jit(solution)/shard_map/all_to_all | solution.py:102
  52.0 11.6 %collective-permute-start.3 = (bf16[32,16,128]{2,1,0:T(8,128)(2,1)}, bf16[32,16,128]{2,1,0:T(8,128)(2,1)}, u32[]{:S(2)}, u32[]{:S(2)}) collective-permute-start(bf16[32,16,128]{2,1,0:T(8,128)(2,1)} %all-to-all-done), channel_id=1, source_target_pairs={{0,4},{4,0},{1,5},{5,1},{2,6},{6,2},{3,7},{7,3},{8,12},{12,8},{9,1... | collective-permute-start | bytes 393224 | tf_op jit(solution)/shard_map/ppermute | solution.py:40
  59.9 13.5 %collective-permute-start.6 = (f32[8,128]{1,0:T(8,128)S(1)}, f32[8,128]{1,0:T(8,128)}, u32[]{:S(2)}, u32[]{:S(2)}) collective-permute-start(f32[8,128]{1,0:T(8,128)S(1)} %reduce_sum.89), channel_id=1, source_target_pairs={{0,4},{4,0},{1,5},{5,1},{2,6},{6,2},{3,7},{7,3},{8,12},{12,8},{9,1... | collective-permute-start | bytes 12296 | tf_op jit(solution)/shard_map/ppermute | solution.py:40
  68.7 3.2 %copy-start.9 = (bf16[16,4096]{1,0:T(8,128)(2,1)S(1)}, bf16[16,4096]{1,0:T(8,128)(2,1)}, u32[]{:S(2)}) copy-start(bf16[16,4096]{1,0:T(8,128)(2,1)} %copy-done.8) | copy-start | bytes 393220
  68.7 24.4 %copy-start.10 = (f32[4,4]{1,0:T(4,128)S(1)}, f32[4,4]{1,0:T(4,128)}, u32[]{:S(2)}) copy-start(f32[4,4]{1,0:T(4,128)} %param.15) | copy-start | bytes 196
  68.7 25.7 %copy-start.3 = (f32[4,512,16]{1,2,0:T(8,128)S(1)}, f32[4,512,16]{1,2,0:T(8,128)}, u32[]{:S(2)}) copy-start(f32[4,512,16]{1,2,0:T(8,128)} %param.13) | copy-start | bytes 393220
  71.0 1.0 copy-start.5
  71.9 23.0 %copy-start.1 = (f32[4]{0:T(128)S(1)}, f32[4]{0:T(128)}, u32[]{:S(2)}) copy-start(f32[4]{0:T(128)} %param.14) | copy-start | bytes 52
  71.9 23.7 %copy-start.13 = (s32[128]{0:T(128)S(1)}, s32[128]{0:T(128)}, u32[]{:S(2)}) copy-start(s32[128]{0:T(128)} %copy-done.12) | copy-start | bytes 1540
  74.8 13.7 %all-to-all-start.3 = ((f32[32,8,128]{2,1,0:T(8,128)}), f32[32,8,128]{2,1,0:T(8,128)S(1)}, u32[]{:S(2)}, u32[]{:S(2)}) async-start(f32[32,8,128]{2,1,0:T(8,128)} %broadcast_in_dim.40), calls=%async_computation.3 | async-start | bytes 262144 | tf_op jit(solution)/shard_map/all_to_all | solution.py:104
  78.7 1.3 %collective-permute-start.4 = (f32[32,128]{1,0:T(8,128)S(1)}, f32[32,128]{1,0:T(8,128)S(1)}, u32[]{:S(2)}, u32[]{:S(2)}) collective-permute-start(f32[32,128]{1,0:T(8,128)S(1)} %dynamic-slice_bitcast_fusion), channel_id=1, source_target_pairs={{0,4},{4,0},{1,5},{5,1},{2,6},{6,2},{3,7},{7,3},{8,12},{12,8},{9,1... | collective-permute-start | bytes 49160 | tf_op jit(solution)/shard_map/ppermute | solution.py:40
  89.2 14.2 %all-to-all-start.1 = ((bf16[32,32,128]{2,1,0:T(8,128)(2,1)}), bf16[32,32,128]{2,1,0:T(8,128)(2,1)S(1)}, u32[]{:S(2)}, u32[]{:S(2)}) async-start(bf16[32,32,128]{2,1,0:T(8,128)(2,1)} %broadcast_in_dim.39), calls=%async_computation.1 | async-start | bytes 524288 | tf_op jit(solution)/shard_map/all_to_all | solution.py:149
  94.9 16.0 %copy-start.6 = (bf16[128,4096]{1,0:T(8,128)(2,1)S(1)}, bf16[128,4096]{1,0:T(8,128)(2,1)}, u32[]{:S(2)}) copy-start(bf16[128,4096]{1,0:T(8,128)(2,1)} %copy-done.5) | copy-start | bytes 3145732
  103.5 17.6 %copy-start.7 = (f32[1,4096,16]{1,2,0:T(8,128)S(1)}, f32[1,4096,16]{1,2,0:T(8,128)}, u32[]{:S(2)}) copy-start(f32[1,4096,16]{1,2,0:T(8,128)} %param.11) | copy-start | bytes 786436
  103.5 6.8 %collective-permute-start.5 = (f32[32,128]{1,0:T(8,128)S(1)}, f32[32,128]{1,0:T(8,128)S(1)}, u32[]{:S(2)}, u32[]{:S(2)}) collective-permute-start(f32[32,128]{1,0:T(8,128)S(1)} %convert_reduce_fusion.2), channel_id=1, source_target_pairs={{0,4},{4,0},{1,5},{5,1},{2,6},{6,2},{3,7},{7,3},{8,12},{12,8},{9,1... | collective-permute-start | bytes 49160 | tf_op jit(solution)/shard_map/ppermute | solution.py:40
  111.3 6.4 %collective-permute-start.9 = (bf16[16,4096]{1,0:T(8,128)(2,1)S(1)}, bf16[16,4096]{1,0:T(8,128)(2,1)S(1)}, u32[]{:S(2)}, u32[]{:S(2)}) collective-permute-start(bf16[16,4096]{1,0:T(8,128)(2,1)S(1)} %get-tuple-element.75), channel_id=1, source_target_pairs={{0,1},{1,2},{2,3},{3,0},{4,5},{5,6},{6,7},{7,4},{8,9},{9,10},{10,1... | collective-permute-start | bytes 393224 | tf_op jit(solution)/shard_map/ppermute | solution.py:171
  112.9 8.2 %collective-permute-start.8 = (bf16[16,4096]{1,0:T(8,128)(2,1)S(1)}, bf16[16,4096]{1,0:T(8,128)(2,1)S(1)}, u32[]{:S(2)}, u32[]{:S(2)}) collective-permute-start(bf16[16,4096]{1,0:T(8,128)(2,1)S(1)} %get-tuple-element.76), channel_id=1, source_target_pairs={{0,2},{1,3},{2,0},{3,1},{4,6},{5,7},{6,4},{7,5},{8,10},{9,11},{10,... | collective-permute-start | bytes 393224 | tf_op jit(solution)/shard_map/ppermute | solution.py:171
  114.7 6.5 %collective-permute-start.7 = (bf16[16,4096]{1,0:T(8,128)(2,1)S(1)}, bf16[16,4096]{1,0:T(8,128)(2,1)S(1)}, u32[]{:S(2)}, u32[]{:S(2)}) collective-permute-start(bf16[16,4096]{1,0:T(8,128)(2,1)S(1)} %get-tuple-element.74), channel_id=1, source_target_pairs={{0,3},{1,0},{2,1},{3,2},{4,7},{5,4},{6,5},{7,6},{8,11},{9,8},{10,9... | collective-permute-start | bytes 393224 | tf_op jit(solution)/shard_map/ppermute | solution.py:171

commit v2 on v1

--- a/solution.py
+++ b/solution.py
@@ -77,7 +77,6 @@
     mine = jnp.clip(lax.dynamic_slice(local, (first,), (SLOTS,)), 0, rows - 1)
     sent_rows = points[mine].reshape(SLOTS, 2, width // 2).transpose(1, 0, 2).reshape(2 * SLOTS, width // 2)
     sent_rows = jnp.broadcast_to(sent_rows[None], (n_chips, 2 * SLOTS, width // 2))
-    got_rows = lax.all_to_all(sent_rows, CHIP_AXES, 0, 0)
 
     own_weights = rep_weights[0].T
     low = own_weights.astype(jnp.bfloat16)
@@ -99,11 +98,12 @@
     cols = n_out * draws
     tiles = projected.reshape(cols // 8, 8, own_features // 128, 128).transpose(0, 2, 1, 3)
     tiles = tiles.reshape(n_chips, 8, 128)
-    got = jnp.sum(lax.all_to_all(tiles, CHIP_AXES, 0, 0), 0)
-    got = got + swap_core(got)
-    got = lax.all_to_all(jnp.broadcast_to(got[None], (n_chips, 8, 128)), CHIP_AXES, 0, 0)
-    projected = got.reshape(cols // 8, own_features // 128, 8, 128).transpose(0, 2, 1, 3)
-    projected = projected.reshape(n_out, draws * own_features)
+    got = lax.all_to_all(
+        jnp.concatenate([sent_rows, tiles.astype(jnp.bfloat16)], 1), CHIP_AXES, 0, 0
+    )
+    got_rows = got[:, : 2 * SLOTS]
+    projected = jnp.sum(got[:, 2 * SLOTS :].astype(jnp.float32), 0)
+    projected = (projected + swap_core(projected)).astype(jnp.bfloat16)
 
     other_rows = swap_core(got_rows)
 
@@ -146,8 +146,12 @@
     kept = lax.dynamic_index_in_dim(halves, core, 0, keepdims=False)
     given = lax.dynamic_index_in_dim(halves, 1 - core, 0, keepdims=False)
     kept = (kept + swap_core(given)).astype(jnp.bfloat16)
-    kept = lax.all_to_all(jnp.broadcast_to(kept[None], (n_chips, half_cols, own_rows)), CHIP_AXES, 0, 0)
-    kept = jnp.sum(kept.astype(jnp.float32), 0)
+    sent = jnp.concatenate([kept, projected], 0)
+    got = lax.all_to_all(jnp.broadcast_to(sent[None], (n_chips, *sent.shape)), CHIP_AXES, 0, 0)
+    projected = got[:, half_cols:].astype(jnp.float32)
+    projected = projected.reshape(cols // 8, own_features // 128, 8, 128).transpose(0, 2, 1, 3)
+    projected = projected.reshape(n_out, draws * own_features)
+    kept = jnp.sum(got[:, :half_cols].astype(jnp.float32), 0)
     other = swap_core(kept)
     lower = jnp.where(core == 0, kept, other)
     upper = jnp.where(core == 0, other, kept)

time: 123 us -> 103 us (0.84)
  starting transfers between devices: 46.8 us -> 28.9 us
    all_to_all x4 -> x2, starting transfers between devices: 28.2 us -> 15.1 us  [the longest x1 11.2 us: shards(): lax.all_to_all(jnp.concatenate([sent_rows, tiles.astype(jnp.bfloat16)], 1...]
    ppermute x4, starting transfers between devices: 9.99 us -> 5.92 us  [swap_core(): return lax.ppermute(value, 'core', [(0, 1), (1, 0)])]
    all_to_all x4 -> x2, waiting for transfers between devices: 20.9 us -> 18.3 us  [the longest x1 10.3 us: shards(): lax.all_to_all(jnp.broadcast_to(sent[None], (n_chips, *sent.shape)), CHIP...]
    ppermute x3, waiting for transfers between devices: 5.69 us -> 7.63 us  [shards(): lax.ppermute(sent[k - 1], 'out', [(i, (i - k) % n_out) for i in range(n_o...]
    ppermute x3, starting transfers between devices: 4.11 us -> 2.18 us  [shards(): lax.ppermute(sent[k - 1], 'out', [(i, (i - k) % n_out) for i in range(n_o...]
    reduce_sum x1, other arithmetic: 2.81 us -> 1.21 us  [shards(): col_norm = jnp.sum(jnp.square(points.astype(jnp.float32)), 1)]
  transfers between devices with their start and end apart: 14 -> 12, of which waited for: 6 -> 6; matrix products, arithmetic and copies ran while one was open for 30% -> 32% of each run, Pallas kernels for 0% -> 0%
where the time goes in v2:
time: 103 us; the launch traced here: 102 us
  starting transfers between devices  28.9 us (28%)
  waiting for transfers between devices  26.8 us (26%)
  matrix products  23.2 us (23%)
  other arithmetic  10.3 us (10%)
  local copies, waits for them, and re-layouts  9.57 us (9%)
  between operations  2.99 us (3%)
    all_to_all x1, starting transfers between devices, shards(): lax.all_to_all(jnp.concatenate([sent_rows, tiles.astype(jnp.bfloat16)], 1...  11.2 us
    all_to_all x1, waiting for transfers between devices, shards(): lax.all_to_all(jnp.broadcast_to(sent[None], (n_chips, *sent.shape)), CHIP...  10.3 us
    all_to_all x1, waiting for transfers between devices, shards(): lax.all_to_all(jnp.concatenate([sent_rows, tiles.astype(jnp.bfloat16)], 1...  8.06 us
    dot_general x1, matrix products, shards(): lax.dot_general(freq, points, (((0,), (1,)), ((), ())), preferred_element...  7.78 us
    ppermute x3, waiting for transfers between devices, shards(): lax.ppermute(sent[k - 1], 'out', [(i, (i - k) % n_out) for i in range(n_o...  7.63 us
    ppermute x4, starting transfers between devices, swap_core(): return lax.ppermute(value, 'core', [(0, 1), (1, 0)])  5.92 us
    ppermute x3, starting transfers between devices, shards(): lax.ppermute(low, 'out', [(i, (i + k) % n_out) for i in range(n_out)])  5.72 us
    dot_general x4, matrix products, place(): jnp.dot(pick.astype(jnp.bfloat16), held.reshape(n_chips * 2 * SLOTS, widt...  4.73 us
  transfers between devices with their start and end apart: 12, of which 6 were waited for; matrix products, arithmetic and copies ran while one was open for 32% of the time, Pallas kernels for 0%

profile of v2, /device:TPU:1, one launch (start us, length us, event | category | flops | bytes accessed | tf_op | source)
XLA Modules:
  0.0 102.0 jit_solution(11788595471040135410)
XLA Ops:
  0.0 1.1 %bitcast_convert_fusion = bf16[16,4096]{1,0:T(8,128)(2,1)S(1)} fusion(f32[1,4096,16]{1,2,0:T(8,128)} %param.11), kind=kLoop, calls=%fused_computation.76 | loop fusion | flops 65536 | bytes 393216 | tf_op jit(solution)/shard_map/convert_element_type | solution.py:82
  1.1 2.1 %collective-permute-start = (bf16[16,4096]{1,0:T(8,128)(2,1)S(1)}, bf16[16,4096]{1,0:T(8,128)(2,1)S(1)}, u32[]{:S(2)}, u32[]{:S(2)}) collective-permute-start(bf16[16,4096]{1,0:T(8,128)(2,1)S(1)} %bitcast_convert_fusion), channel_id=1, source_target_pairs={{0,1},{1,2},{2,3},{3,0},{4,5},{5,6},{6,7},{7,4},{8,9},{9,10},{10,1... | collective-permute-start | bytes 393224 | tf_op jit(solution)/shard_map/ppermute | solution.py:85
  3.2 2.5 %collective-permute-start.1 = (bf16[16,4096]{1,0:T(8,128)(2,1)S(1)}, bf16[16,4096]{1,0:T(8,128)(2,1)}, u32[]{:S(2)}, u32[]{:S(2)}) collective-permute-start(bf16[16,4096]{1,0:T(8,128)(2,1)S(1)} %bitcast_convert_fusion), channel_id=1, source_target_pairs={{0,2},{1,3},{2,0},{3,1},{4,6},{5,7},{6,4},{7,5},{8,10},{9,11},{10,... | collective-permute-start | bytes 393224 | tf_op jit(solution)/shard_map/ppermute | solution.py:85
  5.6 1.2 %collective-permute-start.2 = (bf16[16,4096]{1,0:T(8,128)(2,1)S(1)}, bf16[16,4096]{1,0:T(8,128)(2,1)}, u32[]{:S(2)}, u32[]{:S(2)}) collective-permute-start(bf16[16,4096]{1,0:T(8,128)(2,1)S(1)} %bitcast_convert_fusion), channel_id=1, source_target_pairs={{0,3},{1,0},{2,1},{3,2},{4,7},{5,4},{6,5},{7,6},{8,11},{9,8},{10,9... | collective-permute-start | bytes 393224 | tf_op jit(solution)/shard_map/ppermute | solution.py:85
  6.8 1.1 %convert_reduce_fusion = s32[512]{0:T(512)S(1)} fusion(s32[512]{0:T(512)} %param.12), kind=kLoop, calls=%fused_computation.60 | loop fusion | flops 1834496 | bytes 4096 | tf_op jit(solution)/shard_map/reduce_sum | solution.py:64
  7.9 0.9 fusion.29
  8.7 1.2 %fusion.48 = (s32[128]{0:T(128)S(1)}, s32[128]{0:T(128)}, s32[]{:T(128)}, s32[128]{0:T(128)S(1)}, s32[128]{0:T(128)}) fusion(s32[128]{0:T(128)S(1)} %fusion.29, s32[]{:T(128)S(6)} %mul.117), kind=kLoop, calls=%fused_computation.121 | loop fusion | flops 2559 | bytes 2568 | tf_op jit(solution)/shard_map/mul | solution.py:69
  12.0 2.4 %gather_fusion.3 = bf16[8,256]{1,0:T(8,128)(2,1)S(1)} fusion(bf16[4096,256]{1,0:T(8,128)(2,1)} %param.10, s32[1024]{0:T(1024)S(1)} %pad_clamp_fusion.1), kind=kCustom, calls=%fused_computation.3 | custom fusion | bytes 8224 | tf_op jit(solution)/shard_map/gather | solution.py:78
  15.2 7.8 %multiply_convert_fusion = bf16[512,4096]{1,0:T(8,128)(2,1)S(1)} fusion(bf16[4096,256]{1,0:T(8,128)(2,1)} %param.10, f32[512]{0:T(512)S(1)} %dynamic-slice_multiply_fusion, bf16[256,2048]{1,0:T(8,128)(2,1)S(1)} %copy-done, s32[]{:T(128)S(6)} %select_n.102), kind=kOutput, calls=%fused_computation.43 | convolution fusion | flops 1111490560 | bytes 6555652 | tf_op jit(solution)/shard_map/dot_general | solution.py:89
  23.1 2.1 %copy-done.3 = bf16[512,4096]{1,0:T(8,128)(2,1)} copy-done((bf16[512,4096]{1,0:T(8,128)(2,1)}, bf16[512,4096]{1,0:T(8,128)(2,1)S(1)}, u32[]{:S(2)}) %copy-start.3) | copy-done | bytes 4194328
  25.2 2.4 %convolution_convert_fusion.2 = bf16[64,512]{1,0:T(8,128)(2,1)S(1)} fusion(bf16[512,4096]{1,0:T(8,128)(2,1)S(1)} %multiply_convert_fusion, bf16[16,4096]{1,0:T(8,128)(2,1)} %collective-permute-done.2, bf16[16,4096]{1,0:T(8,128)(2,1)} %collective-permute-done.1, bf16[16,4096]{1,0:T(8,128)(2,1)S(1)} %collective-permute-done, ...), kind=kOutput, calls=%fused_computation.58 | convolution fusion | flops 270565376 | bytes 4784128 | tf_op jit(solution)/shard_map/dot_general | solution.py:95
  28.3 11.2 %all-to-all-start = ((bf16[32,24,128]{2,1,0:T(8,128)(2,1)}), bf16[32,24,128]{2,1,0:T(8,128)(2,1)S(1)}, u32[]{:S(2)}, u32[]{:S(2)}) async-start(bf16[32,24,128]{2,1,0:T(8,128)(2,1)} %pad_maximum_fusion.2), calls=%async_computation | async-start | bytes 393216 | tf_op jit(solution)/shard_map/all_to_all | solution.py:101
  40.1 1.2 %multiply_reduce_fusion = f32[4096]{0:T(1024)} fusion(bf16[4096,256]{1,0:T(8,128)(2,1)S(1)} %copy-done.4), kind=kLoop, calls=%fused_computation.53 | loop fusion | flops 3141632 | bytes 2113536 | tf_op jit(solution)/shard_map/reduce_sum | solution.py:136
  41.3 8.1 %all-to-all-done = bf16[32,24,128]{2,1,0:T(8,128)(2,1)S(1)} async-done(((bf16[32,24,128]{2,1,0:T(8,128)(2,1)}), bf16[32,24,128]{2,1,0:T(8,128)(2,1)S(1)}, u32[]{:S(2)}, u32[]{:S(2)}) %all-to-all-start) | async-done | bytes 196640 | tf_op jit(solution)/shard_map/all_to_all | solution.py:101
  50.1 3.2 %collective-permute-start.3 = (bf16[32,16,128]{2,1,0:T(8,128)(2,1)}, bf16[32,16,128]{2,1,0:T(8,128)(2,1)}, u32[]{:S(2)}, u32[]{:S(2)}) collective-permute-start(bf16[32,16,128]{2,1,0:T(8,128)(2,1)} %slice.54), channel_id=1, source_target_pairs={{0,4},{4,0},{1,5},{5,1},{2,6},{6,2},{3,7},{7,3},{8,12},{12,8},{9,1... | collective-permute-start | bytes 393224 | tf_op jit(solution)/shard_map/ppermute | solution.py:40
  54.9 5.8 %conditional.6 = (bf16[128,256]{0,1:T(8,128)(2,1)S(1)}) conditional(s32[]{:T(128)} %convert_element_type.90, (s32[128]{0:T(128)S(1)}, s32[128]{0:T(128)}, pred[128]{0:T(512)(128)(4,1)}, s32[128]{0:T(128)S(1)}, s32[128]{0:T(128)}, /*index=5*/s32[128,128]{1,0:T(8,128)S(1)}, s32[128]{0:T(128)S(1)}, s32[]{:T(128)}, bf16[32,16,128]{2,1,0:T(8,128)(2,1)}, ...), branch_computations={%region_5.7_spmd, %region_7.9_spmd} | conditional | flops 67851136 | bytes 1057168
  55.8 1.2 %fusion.4 = f32[128,128]{0,1:T(8,128)S(1)} fusion(bf16[512,128]{1,0:T(8,128)(2,1)} %bitcast, s32[128]{0:T(128)S(1)} %get-tuple-element.73, pred[128]{0:T(512)(128)(4,1)S(1)} %get-tuple-element.70), kind=kOutput, calls=%fused_computation.14 | convolution fusion | flops 16908288 | bytes 197248 | tf_op jit(solution)/shard_map/cond/branch_0_fun/dot_general | solution.py:119
  57.0 1.2 %convolution_add_fusion.1 = bf16[128,128]{0,1:T(8,128)(2,1)S(1)} fusion(f32[128,128]{0,1:T(8,128)S(1)} %fusion.4, bf16[512,128]{1,0:T(8,128)(2,1)} %bitcast.1, s32[128]{0:T(128)S(1)} %get-tuple-element.73, pred[128]{0:T(512)(128)(4,1)S(1)} %get-tuple-element.69), kind=kOutput, calls=%fused_computation.7 | convolution fusion | flops 16941056 | bytes 230016 | tf_op jit(solution)/shard_map/cond/branch_0_fun/dot_general | solution.py:119
  58.2 1.2 %fusion.7 = f32[128,128]{0,1:T(8,128)S(1)} fusion(bf16[512,128]{1,0:T(8,128)(2,1)} %bitcast, s32[128]{0:T(128)S(1)} %get-tuple-element.72, pred[128]{0:T(512)(128)(4,1)S(1)} %get-tuple-element.70), kind=kOutput, calls=%fused_computation.15 | convolution fusion | flops 16908288 | bytes 197248 | tf_op jit(solution)/shard_map/cond/branch_0_fun/dot_general | solution.py:119
  59.4 1.2 %convolution_add_fusion = bf16[128,128]{0,1:T(8,128)(2,1)S(1)} fusion(f32[128,128]{0,1:T(8,128)S(1)} %fusion.7, bf16[512,128]{1,0:T(8,128)(2,1)} %bitcast.1, s32[128]{0:T(128)S(1)} %get-tuple-element.72, pred[128]{0:T(512)(128)(4,1)S(1)} %get-tuple-element.69), kind=kOutput, calls=%fused_computation.6 | convolution fusion | flops 16941056 | bytes 230016 | tf_op jit(solution)/shard_map/cond/branch_0_fun/dot_general | solution.py:119
  60.8 2.3 %multiply_convert_fusion.1 = bf16[128,4096]{1,0:T(8,128)(2,1)S(1)} fusion(bf16[4096,256]{1,0:T(8,128)(2,1)S(1)} %copy-done.4, f32[4096]{0:T(1024)} %multiply_reduce_fusion, f32[128]{0:T(128)S(1)} %multiply_reduce_fusion.1, bf16[128,256]{0,1:T(8,128)(2,1)S(1)} %get-tuple-element.86), kind=kOutput, calls=%fused_computation.57 | convolution fusion | flops 275251200 | bytes 3228160 | tf_op jit(solution)/shard_map/dot_general | solution.py:137
  63.1 1.0 copy-done.5
  64.1 1.5 %fusion.38 = f32[64,128]{1,0:T(8,128)S(1)} fusion(bf16[128,4096]{1,0:T(8,128)(2,1)S(1)} %multiply_convert_fusion.1, bf16[16,4096]{1,0:T(8,128)(2,1)} %collective-permute-done.2, bf16[16,4096]{1,0:T(8,128)(2,1)} %collective-permute-done.1, bf16[16,4096]{1,0:T(8,128)(2,1)S(1)} %copy-done.13, bf16[16,4096]{1,0:T(8,128)(2,1)S(1)} %bitcast_convert_fusion), kind=kOutput, calls=%fused_computation.83 | convolution fusion | flops 69206016 | bytes 1605632 | tf_op jit(solution)/shard_map/dot_general | solution.py:141
  66.1 0.8 collective-permute-done.4
  67.8 3.9 %all-to-all-start.1 = ((bf16[32,40,128]{2,1,0:T(8,128)(2,1)}), bf16[32,40,128]{2,1,0:T(8,128)(2,1)S(1)}, u32[]{:S(2)}, u32[]{:S(2)}) async-start(bf16[32,40,128]{2,1,0:T(8,128)(2,1)} %broadcast_in_dim.37), calls=%async_computation.1 | async-start | bytes 655360 | tf_op jit(solution)/shard_map/all_to_all | solution.py:150
  74.5 10.3 %all-to-all-done.1 = bf16[32,40,128]{2,1,0:T(8,128)(2,1)S(1)} async-done(((bf16[32,40,128]{2,1,0:T(8,128)(2,1)}), bf16[32,40,128]{2,1,0:T(8,128)(2,1)S(1)}, u32[]{:S(2)}, u32[]{:S(2)}) %all-to-all-start.1) | async-done | bytes 327712 | tf_op jit(solution)/shard_map/all_to_all | solution.py:150
  84.8 2.1 %collective-permute-start.6 = (f32[32,128]{1,0:T(8,128)S(1)}, f32[32,128]{1,0:T(8,128)S(1)}, u32[]{:S(2)}, u32[]{:S(2)}) collective-permute-start(f32[32,128]{1,0:T(8,128)S(1)} %convert_reduce_fusion.2), channel_id=1, source_target_pairs={{0,4},{4,0},{1,5},{5,1},{2,6},{6,2},{3,7},{7,3},{8,12},{12,8},{9,1... | collective-permute-start | bytes 49160 | tf_op jit(solution)/shard_map/ppermute | solution.py:40
  87.4 3.1 %fusion.55 = f32[64,4096]{1,0:T(8,128)S(1)} fusion(bf16[64,512]{1,0:T(8,128)(2,1)S(1)} %reshape.143, bf16[512,4096]{1,0:T(8,128)(2,1)} %copy-done.3), kind=kOutput, calls=%fused_computation.130 | convolution fusion | flops 268435456 | bytes 5308416 | tf_op jit(solution)/shard_map/dot_general | solution.py:170
  91.5 2.1 %collective-permute-start.8 = (bf16[16,4096]{1,0:T(8,128)(2,1)S(1)}, bf16[16,4096]{1,0:T(8,128)(2,1)S(1)}, u32[]{:S(2)}, u32[]{:S(2)}) collective-permute-start(bf16[16,4096]{1,0:T(8,128)(2,1)S(1)} %get-tuple-element.76), channel_id=1, source_target_pairs={{0,2},{1,3},{2,0},{3,1},{4,6},{5,7},{6,4},{7,5},{8,10},{9,11},{10,... | collective-permute-start | bytes 393224 | tf_op jit(solution)/shard_map/ppermute | solution.py:175
  93.6 3.0 %collective-permute-done.7 = bf16[16,4096]{1,0:T(8,128)(2,1)S(1)} collective-permute-done((bf16[16,4096]{1,0:T(8,128)(2,1)S(1)}, bf16[16,4096]{1,0:T(8,128)(2,1)S(1)}, u32[]{:S(2)}, u32[]{:S(2)}) %collective-permute-start.7) | collective-permute-done | bytes 131104 | tf_op jit(solution)/shard_map/ppermute | solution.py:175
  96.6 1.6 %collective-permute-done.8 = bf16[16,4096]{1,0:T(8,128)(2,1)S(1)} collective-permute-done((bf16[16,4096]{1,0:T(8,128)(2,1)S(1)}, bf16[16,4096]{1,0:T(8,128)(2,1)S(1)}, u32[]{:S(2)}, u32[]{:S(2)}) %collective-permute-start.8) | collective-permute-done | bytes 131104 | tf_op jit(solution)/shard_map/ppermute | solution.py:175
  98.2 3.1 %collective-permute-done.9 = bf16[16,4096]{1,0:T(8,128)(2,1)S(1)} collective-permute-done((bf16[16,4096]{1,0:T(8,128)(2,1)S(1)}, bf16[16,4096]{1,0:T(8,128)(2,1)S(1)}, u32[]{:S(2)}, u32[]{:S(2)}) %collective-permute-start.9) | collective-permute-done | bytes 131104 | tf_op jit(solution)/shard_map/ppermute | solution.py:175
  (84 shorter events, 11.3 us)
Async XLA Ops:
  0.0 15.2 %copy-start = (bf16[256,2048]{1,0:T(8,128)(2,1)S(1)}, bf16[256,2048]{1,0:T(8,128)(2,1)}, u32[]{:S(2)}) copy-start(bf16[256,2048]{1,0:T(8,128)(2,1)} %param.16) | copy-start | bytes 3145732
  1.1 22.0 %collective-permute-start = (bf16[16,4096]{1,0:T(8,128)(2,1)S(1)}, bf16[16,4096]{1,0:T(8,128)(2,1)S(1)}, u32[]{:S(2)}, u32[]{:S(2)}) collective-permute-start(bf16[16,4096]{1,0:T(8,128)(2,1)S(1)} %bitcast_convert_fusion), channel_id=1, source_target_pairs={{0,1},{1,2},{2,3},{3,0},{4,5},{5,6},{6,7},{7,4},{8,9},{9,10},{10,1... | collective-permute-start | bytes 393224 | tf_op jit(solution)/shard_map/ppermute | solution.py:85
  3.2 19.9 %collective-permute-start.1 = (bf16[16,4096]{1,0:T(8,128)(2,1)S(1)}, bf16[16,4096]{1,0:T(8,128)(2,1)}, u32[]{:S(2)}, u32[]{:S(2)}) collective-permute-start(bf16[16,4096]{1,0:T(8,128)(2,1)S(1)} %bitcast_convert_fusion), channel_id=1, source_target_pairs={{0,2},{1,3},{2,0},{3,1},{4,6},{5,7},{6,4},{7,5},{8,10},{9,11},{10,... | collective-permute-start | bytes 393224 | tf_op jit(solution)/shard_map/ppermute | solution.py:85
  5.6 17.5 %collective-permute-start.2 = (bf16[16,4096]{1,0:T(8,128)(2,1)S(1)}, bf16[16,4096]{1,0:T(8,128)(2,1)}, u32[]{:S(2)}, u32[]{:S(2)}) collective-permute-start(bf16[16,4096]{1,0:T(8,128)(2,1)S(1)} %bitcast_convert_fusion), channel_id=1, source_target_pairs={{0,3},{1,0},{2,1},{3,2},{4,7},{5,4},{6,5},{7,6},{8,11},{9,8},{10,9... | collective-permute-start | bytes 393224 | tf_op jit(solution)/shard_map/ppermute | solution.py:85
  6.8 8.4 %copy-start.10 = (s32[128]{0:T(128)}, s32[128]{0:T(128)S(1)}, u32[]{:S(2)}) copy-start(s32[128]{0:T(128)S(1)} %multiply_add_fusion) | copy-start | bytes 1540
  15.2 7.8 %copy-start.9 = (s32[512]{0:T(512)S(1)}, s32[512]{0:T(512)}, u32[]{:S(2)}) copy-start(s32[512]{0:T(512)} %param.12) | copy-start | bytes 6148
  23.0 2.1 %copy-start.3 = (bf16[512,4096]{1,0:T(8,128)(2,1)}, bf16[512,4096]{1,0:T(8,128)(2,1)S(1)}, u32[]{:S(2)}) copy-start(bf16[512,4096]{1,0:T(8,128)(2,1)S(1)} %multiply_convert_fusion) | copy-start | bytes 12582916
  23.0 17.1 %copy-start.4 = (bf16[4096,256]{1,0:T(8,128)(2,1)S(1)}, bf16[4096,256]{1,0:T(8,128)(2,1)}, u32[]{:S(2)}) copy-start(bf16[4096,256]{1,0:T(8,128)(2,1)} %param.10) | copy-start | bytes 6291460
  23.1 5.2 %copy-start.12 = (bf16[16,4096]{1,0:T(8,128)(2,1)}, bf16[16,4096]{1,0:T(8,128)(2,1)S(1)}, u32[]{:S(2)}) copy-start(bf16[16,4096]{1,0:T(8,128)(2,1)S(1)} %collective-permute-done) | copy-start | bytes 393220
  28.3 21.1 %all-to-all-start = ((bf16[32,24,128]{2,1,0:T(8,128)(2,1)}), bf16[32,24,128]{2,1,0:T(8,128)(2,1)S(1)}, u32[]{:S(2)}, u32[]{:S(2)}) async-start(bf16[32,24,128]{2,1,0:T(8,128)(2,1)} %pad_maximum_fusion.2), calls=%async_computation | async-start | bytes 393216 | tf_op jit(solution)/shard_map/all_to_all | solution.py:101
  50.1 4.8 %collective-permute-start.3 = (bf16[32,16,128]{2,1,0:T(8,128)(2,1)}, bf16[32,16,128]{2,1,0:T(8,128)(2,1)}, u32[]{:S(2)}, u32[]{:S(2)}) collective-permute-start(bf16[32,16,128]{2,1,0:T(8,128)(2,1)} %slice.54), channel_id=1, source_target_pairs={{0,4},{4,0},{1,5},{5,1},{2,6},{6,2},{3,7},{7,3},{8,12},{12,8},{9,1... | collective-permute-start | bytes 393224 | tf_op jit(solution)/shard_map/ppermute | solution.py:40
  54.8 11.3 %collective-permute-start.5 = (f32[8,128]{1,0:T(8,128)S(1)}, f32[8,128]{1,0:T(8,128)S(1)}, u32[]{:S(2)}, u32[]{:S(2)}) collective-permute-start(f32[8,128]{1,0:T(8,128)S(1)} %convert_reduce_fusion.3), channel_id=1, source_target_pairs={{0,4},{4,0},{1,5},{5,1},{2,6},{6,2},{3,7},{7,3},{8,12},{12,8},{9,1... | collective-permute-start | bytes 12296 | tf_op jit(solution)/shard_map/ppermute | solution.py:40
  60.8 3.3 %copy-start.13 = (bf16[16,4096]{1,0:T(8,128)(2,1)S(1)}, bf16[16,4096]{1,0:T(8,128)(2,1)}, u32[]{:S(2)}) copy-start(bf16[16,4096]{1,0:T(8,128)(2,1)} %copy-done.12) | copy-start | bytes 393220
  60.8 10.9 %copy-start.8 = (f32[4,4]{1,0:T(4,128)S(1)}, f32[4,4]{1,0:T(4,128)}, u32[]{:S(2)}) copy-start(f32[4,4]{1,0:T(4,128)} %param.15) | copy-start | bytes 196
  60.8 12.1 %copy-start.2 = (f32[4,512,16]{1,2,0:T(8,128)S(1)}, f32[4,512,16]{1,2,0:T(8,128)}, u32[]{:S(2)}) copy-start(f32[4,512,16]{1,2,0:T(8,128)} %param.13) | copy-start | bytes 393220
  63.1 1.0 copy-start.5
  64.1 9.4 %copy-start.1 = (f32[4]{0:T(128)S(1)}, f32[4]{0:T(128)}, u32[]{:S(2)}) copy-start(f32[4]{0:T(128)} %param.14) | copy-start | bytes 52
  64.1 10.1 %copy-start.11 = (s32[128]{0:T(128)S(1)}, s32[128]{0:T(128)}, u32[]{:S(2)}) copy-start(s32[128]{0:T(128)} %copy-done.10) | copy-start | bytes 1540
  65.6 1.4 %collective-permute-start.4 = (f32[32,128]{1,0:T(8,128)S(1)}, f32[32,128]{1,0:T(8,128)S(1)}, u32[]{:S(2)}, u32[]{:S(2)}) collective-permute-start(f32[32,128]{1,0:T(8,128)S(1)} %dynamic-slice_bitcast_fusion), channel_id=1, source_target_pairs={{0,4},{4,0},{1,5},{5,1},{2,6},{6,2},{3,7},{7,3},{8,12},{12,8},{9,1... | collective-permute-start | bytes 49160 | tf_op jit(solution)/shard_map/ppermute | solution.py:40
  67.8 17.0 %all-to-all-start.1 = ((bf16[32,40,128]{2,1,0:T(8,128)(2,1)}), bf16[32,40,128]{2,1,0:T(8,128)(2,1)S(1)}, u32[]{:S(2)}, u32[]{:S(2)}) async-start(bf16[32,40,128]{2,1,0:T(8,128)(2,1)} %broadcast_in_dim.37), calls=%async_computation.1 | async-start | bytes 655360 | tf_op jit(solution)/shard_map/all_to_all | solution.py:150
  73.5 17.6 %copy-start.6 = (bf16[128,4096]{1,0:T(8,128)(2,1)S(1)}, bf16[128,4096]{1,0:T(8,128)(2,1)}, u32[]{:S(2)}) copy-start(bf16[128,4096]{1,0:T(8,128)(2,1)} %copy-done.5) | copy-start | bytes 3145732
  84.8 5.7 %collective-permute-start.6 = (f32[32,128]{1,0:T(8,128)S(1)}, f32[32,128]{1,0:T(8,128)S(1)}, u32[]{:S(2)}, u32[]{:S(2)}) collective-permute-start(f32[32,128]{1,0:T(8,128)S(1)} %convert_reduce_fusion.2), channel_id=1, source_target_pairs={{0,4},{4,0},{1,5},{5,1},{2,6},{6,2},{3,7},{7,3},{8,12},{12,8},{9,1... | collective-permute-start | bytes 49160 | tf_op jit(solution)/shard_map/ppermute | solution.py:40
  87.4 13.9 %copy-start.7 = (f32[1,4096,16]{1,2,0:T(8,128)S(1)}, f32[1,4096,16]{1,2,0:T(8,128)}, u32[]{:S(2)}) copy-start(f32[1,4096,16]{1,2,0:T(8,128)} %param.11) | copy-start | bytes 786436
  91.4 5.2 %collective-permute-start.7 = (bf16[16,4096]{1,0:T(8,128)(2,1)S(1)}, bf16[16,4096]{1,0:T(8,128)(2,1)S(1)}, u32[]{:S(2)}, u32[]{:S(2)}) collective-permute-start(bf16[16,4096]{1,0:T(8,128)(2,1)S(1)} %get-tuple-element.74), channel_id=1, source_target_pairs={{0,3},{1,0},{2,1},{3,2},{4,7},{5,4},{6,5},{7,6},{8,11},{9,8},{10,9... | collective-permute-start | bytes 393224 | tf_op jit(solution)/shard_map/ppermute | solution.py:175
  91.5 6.7 %collective-permute-start.8 = (bf16[16,4096]{1,0:T(8,128)(2,1)S(1)}, bf16[16,4096]{1,0:T(8,128)(2,1)S(1)}, u32[]{:S(2)}, u32[]{:S(2)}) collective-permute-start(bf16[16,4096]{1,0:T(8,128)(2,1)S(1)} %get-tuple-element.76), channel_id=1, source_target_pairs={{0,2},{1,3},{2,0},{3,1},{4,6},{5,7},{6,4},{7,5},{8,10},{9,11},{10,... | collective-permute-start | bytes 393224 | tf_op jit(solution)/shard_map/ppermute | solution.py:175
  93.6 7.6 %collective-permute-start.9 = (bf16[16,4096]{1,0:T(8,128)(2,1)S(1)}, bf16[16,4096]{1,0:T(8,128)(2,1)S(1)}, u32[]{:S(2)}, u32[]{:S(2)}) collective-permute-start(bf16[16,4096]{1,0:T(8,128)(2,1)S(1)} %get-tuple-element.75), channel_id=1, source_target_pairs={{0,1},{1,2},{2,3},{3,0},{4,5},{5,6},{6,7},{7,4},{8,9},{9,10},{10,1... | collective-permute-start | bytes 393224 | tf_op jit(solution)/shard_map/ppermute | solution.py:175

commit v3 on v0

v3 whole, which is shorter than its diff:
```python
import functools
import math

import jax
import jax.numpy as jnp
from jax import lax
from jax.experimental import pallas as pl
from jax.experimental.pallas import tpu as pltpu
from jax.sharding import Mesh
from jax.sharding import PartitionSpec as P

LENGTH = 0.5
STEP_SIZE = 0.5
SLOTS = 8
BLOCK = 512
SIN_TURNS = (
    6.283185160088695,
    -41.34165503124932,
    81.60100406363227,
    -76.54978208799582,
    39.53670460277009,
)
POINT_AXES = ("z", "y", "core")
CHIP_AXES = ("z", "y")
BF16 = jnp.bfloat16
F32 = jnp.float32
NT = (((1,), (1,)), ((), ()))


def dot(a, b):
    return jnp.dot(a, b, preferred_element_type=F32)


def dot_nt(a, b):
    return lax.dot_general(a, b, NT, preferred_element_type=F32)


def cos_turns(turns, scale):
    rest = turns - jnp.round(turns)
    quarter = 0.25 - jnp.abs(rest)
    square = quarter * quarter
    poly = F32(SIN_TURNS[-1] * scale)
    for coefficient in SIN_TURNS[-2::-1]:
        poly = poly * square + F32(coefficient * scale)
    return poly * quarter


def split(value):
    high = value.astype(BF16)
    return high, (value - high.astype(F32)).astype(BF16)


def place_of_device():
    chip = lax.axis_index("z") * lax.axis_size("y") + lax.axis_index("y")
    return lax.axis_index("out"), lax.axis_index("core"), chip


def whole(shape):
    return pl.BlockSpec(shape, lambda i: (0,) * len(shape))


def features_kernel(index_ref, points_ref, freq_ref, phase_ref, feats_ref, sent_ref, local_ref, rows_ref):
    step = pl.program_id(0)
    out, core, chip = place_of_device()
    block = points_ref.shape[0]
    own = feats_ref.shape[1]
    n_out = freq_ref.shape[1] // own
    shard_rows = block * pl.num_programs(0)
    minibatch = index_ref.shape[1]

    @pl.when(step == 0)
    def _():
        base = (chip * 2 + core) * shard_rows
        index = index_ref[...]
        key = index * minibatch + lax.broadcasted_iota(jnp.int32, index.shape, 1)
        key_column = jnp.transpose(jnp.broadcast_to(key, (8, minibatch)))[:, :1]
        rank = jnp.sum((key_column < key).astype(jnp.int32), 0, keepdims=True)
        before = jnp.sum((index < base).astype(jnp.int32), 1, keepdims=True)
        first = (before - out + (n_out - 1)) // n_out
        inside = (index >= base) & (index < base + shard_rows) & (lax.rem(rank - out + n_out, n_out) == 0)
        slot = jnp.where(inside, (rank - out) // n_out - first, -1)
        here = slot == lax.broadcasted_iota(jnp.int32, (2 * SLOTS, minibatch), 0)
        local = jnp.sum(jnp.where(here, index - base + 1, 0), 1, keepdims=True) - 1
        local_ref[...] = jnp.broadcast_to(local, local_ref.shape)
        rows_ref[...] = jnp.zeros_like(rows_ref)

    points = points_ref[...]
    at = pl.multiple_of(out * own, own)
    phase = phase_ref[:, pl.ds(at, own)] * (0.5 / math.pi)
    turns = dot(points, freq_ref[:, pl.ds(at, own)]) * (0.5 / math.pi) + phase
    feats_ref[...] = cos_turns(turns, math.sqrt(2.0 / freq_ref.shape[1])).astype(BF16)
    pick = local_ref[:, :1] - step * block == lax.broadcasted_iota(jnp.int32, (2 * SLOTS, block), 1)
    rows_ref[...] += dot(pick.astype(F32).astype(BF16), points)

    @pl.when(step == pl.num_programs(0) - 1)
    def _():
        half = rows_ref.shape[1] // 2
        rows = rows_ref[...]
        sent_ref[...] = jnp.concatenate([rows[:SLOTS, :half], rows[:SLOTS, half:]], 0).astype(BF16)


def project_kernel(n_out, *refs):
    weight_refs, (feats_ref, sent_ref, pack_ref, sum_ref) = refs[:n_out], refs[n_out:]
    step = pl.program_id(0)

    @pl.when(step == 0)
    def _():
        sum_ref[...] = jnp.zeros_like(sum_ref)

    weights = jnp.concatenate([ref[...] for ref in weight_refs], 0)
    sum_ref[...] += dot(weights, feats_ref[...])

    @pl.when(step == pl.num_programs(0) - 1)
    def _():
        across = sum_ref.shape[1] // 128
        for at in range(pack_ref.shape[0]):
            r, c = divmod(at, across)
            high, low = split(sum_ref[8 * r : 8 * r + 8, 128 * c : 128 * c + 128])
            pack_ref[at, :16] = sent_ref[...]
            pack_ref[at, 16:] = jnp.concatenate([high.astype(F32), low.astype(F32)], 0).astype(BF16)


def gram_kernel(n_out, direct, *refs):
    weight_refs = refs[:n_out]
    at_ref, own_ref, other_ref, points_ref, norm_ref = refs[n_out : n_out + 5]
    kern_ref, kept_ref, given_ref, tile_ref, rows_ref, row_norm_ref, sum_ref = refs[n_out + 5 :]
    step = pl.program_id(0)

    @pl.when(step == 0)
    def _():
        peers, height, lanes = own_ref.shape
        if direct:
            rows = at_ref[...].astype(F32)
        else:
            columns = lax.broadcasted_iota(jnp.int32, (rows_ref.shape[0], peers * height), 1)
            halves = []
            for half in range(2):
                part = 0.0
                for source, held in enumerate((own_ref, other_ref)):
                    pick = (at_ref[source][:, :1] + half * SLOTS == columns).astype(F32).astype(BF16)
                    part = part + dot(pick, held[...].reshape(peers * height, lanes))
                halves.append(part)
            rows = jnp.concatenate(halves, 1)
        rows_ref[...] = rows.astype(BF16)
        row_norm_ref[...] = jnp.broadcast_to(jnp.sum(rows * rows, 1, keepdims=True), row_norm_ref.shape)
        sum_ref[...] = jnp.zeros_like(sum_ref)
        tile = jnp.sum(own_ref[:, 16:].astype(F32), 0) + jnp.sum(other_ref[:, 16:].astype(F32), 0)
        tile_ref[...] = tile[:8] + tile[8:]

    inner = dot_nt(rows_ref[...], points_ref[...])
    squared = row_norm_ref[:, :1] + norm_ref[...] - 2.0 * inner
    scaled_square = (5.0 / (LENGTH * LENGTH)) * jnp.maximum(squared, 0.0)
    scaled_r = scaled_square * lax.rsqrt(jnp.maximum(scaled_square, 1e-30))
    kern = (1.0 + scaled_r + scaled_square * (1.0 / 3.0)) * jnp.exp(-scaled_r)
    kern = kern.astype(BF16)
    kern_ref[...] = kern
    weights = jnp.concatenate([ref[...] for ref in weight_refs], 0)
    sum_ref[...] += dot_nt(weights, kern)

    @pl.when(step == pl.num_programs(0) - 1)
    def _():
        half = kept_ref.shape[0]
        core = lax.axis_index("core")
        lower, upper = sum_ref[:half], sum_ref[half:]
        kept_ref[...] = jnp.where(core == 0, lower, upper)
        given_ref[...] = jnp.where(core == 0, upper, lower)


def pack_kernel(kept_ref, came_ref, tile_ref, pack_ref):
    half = kept_ref.shape[0]
    high, low = split(tile_ref[...])
    value = jnp.concatenate([kept_ref[...] + came_ref[...], high.astype(F32), low.astype(F32)], 0).astype(BF16)
    pack_ref[...] = jnp.broadcast_to(value[None], pack_ref.shape)


def step_kernel(n_out, ratio, *refs):
    coregion_ref, noise_ref, targets_ref, own_ref, other_ref, feats_ref, kern_ref, rep_ref = refs[:8]
    base_ref, part_refs, (mixed_ref, weighted_ref) = refs[8], refs[9 : 8 + n_out], refs[8 + n_out :]
    draws = rep_ref.shape[0]
    half = n_out * draws // 2

    @pl.when(pl.program_id(0) == 0)
    def _():
        out, core, _ = place_of_device()
        order = [lax.rem(out - k + n_out, n_out) for k in range(n_out)]
        mixer = [[coregion_ref[a, b] for b in order] for a in order]

        def mix(values):
            return [sum(c * v for c, v in zip(line, values)) for line in mixer]

        own = jnp.sum(own_ref[:, :half].astype(F32), 0)
        other = jnp.sum(other_ref[:, :half].astype(F32), 0)
        total = jnp.concatenate([jnp.where(core == 0, own, other), jnp.where(core == 0, other, own)], 0)
        fitted = mix([total[draws * k : draws * (k + 1)] for k in range(n_out)])
        scaled = [
            (fitted[k] - targets_ref[draws * k : draws * (k + 1)]) / noise_ref[order[k]] for k in range(n_out)
        ]
        weighted = jnp.concatenate(mix(scaled), 0).astype(BF16)
        weighted_ref[...] = (weighted.astype(F32) * ratio).astype(BF16)
        across = mixed_ref.shape[1] // 128
        tiles = [own_ref[p, half:].astype(F32) for p in range(own_ref.shape[0])]
        tiles = [tile[:8] + tile[8:] for tile in tiles]
        lines = [
            jnp.concatenate(tiles[across * r : across * (r + 1)], 1) for r in range(n_out * draws // 8)
        ]
        each = draws // 8
        projected = [jnp.concatenate(lines[each * k : each * (k + 1)], 0) for k in range(n_out)]
        mixed_ref[...] = jnp.concatenate(mix(projected), 0).astype(BF16)

    gradient = dot(weighted_ref[...], kern_ref[...]) + dot_nt(mixed_ref[...], feats_ref[...])
    change = -STEP_SIZE * gradient
    base_ref[...] = rep_ref[...] + change[:draws]
    for k, ref in enumerate(part_refs, 1):
        ref[...] = change[draws * k : draws * (k + 1)].astype(BF16)


def swap_core(value):
    return lax.ppermute(value, "core", [(0, 1), (1, 0)])


def params():
    return pltpu.CompilerParams(dimension_semantics=("arbitrary",), vmem_limit_bytes=32 * 1024 * 1024)


def shards(points, rep_weights, batch_index, targets, noise_var, coregion, frequencies, phases):
    highest = lax.Precision.HIGHEST
    n_out = lax.axis_size("out")
    n_chips = lax.axis_size("z") * lax.axis_size("y")
    n_pts = 2 * n_chips
    rows, width = points.shape
    draws = rep_weights.shape[2]
    minibatch = batch_index.shape[0]
    own_rows = minibatch // n_out
    own_features = frequencies.shape[1] // n_out
    cols = n_out * draws
    steps = rows // BLOCK
    out, core, chip = place_of_device()
    shard = chip * 2 + core
    ratio = (rows * n_pts) / minibatch

    own_weights = rep_weights[0].T
    low = own_weights.astype(BF16)
    weights = [low]
    for k in range(1, n_out):
        weights.append(lax.ppermute(low, "out", [(i, (i + k) % n_out) for i in range(n_out)]))
    weight_specs = [pl.BlockSpec((draws, BLOCK), lambda i: (0, i))] * n_out
    point_spec = pl.BlockSpec((BLOCK, width), lambda i: (i, 0))
    feat_spec = pl.BlockSpec((BLOCK, own_features), lambda i: (i, 0))
    kern_spec = pl.BlockSpec((own_rows, BLOCK), lambda i: (0, i))
    draw_spec = pl.BlockSpec((draws, BLOCK), lambda i: (0, i))

    feats, sent_rows = pl.pallas_call(
        features_kernel,
        grid=(steps,),
        out_shape=(
            jax.ShapeDtypeStruct((rows, own_features), BF16),
            jax.ShapeDtypeStruct((2 * SLOTS, width // 2), BF16),
        ),
        in_specs=[
            whole((1, minibatch)),
            point_spec,
            whole(frequencies.shape),
            whole((1, phases.shape[0])),
        ],
        out_specs=(feat_spec, whole((2 * SLOTS, width // 2))),
        scratch_shapes=[pltpu.VMEM((2 * SLOTS, 128), jnp.int32), pltpu.VMEM((2 * SLOTS, width), F32)],
        compiler_params=params(),
        name="features",
    )(batch_index[None], points, frequencies, phases[None])

    pack = pl.pallas_call(
        functools.partial(project_kernel, n_out),
        grid=(steps,),
        out_shape=jax.ShapeDtypeStruct((n_chips, 32, 128), BF16),
        in_specs=[*weight_specs, feat_spec, whole((2 * SLOTS, width // 2))],
        out_specs=whole((n_chips, 32, 128)),
        scratch_shapes=[pltpu.VMEM((cols, own_features), F32)],
        compiler_params=params(),
        name="project",
    )(*weights, feats, sent_rows)
    got = lax.all_to_all(pack, CHIP_AXES, 0, 0)
    got_other = swap_core(got)

    key = batch_index * minibatch + lax.iota(jnp.int32, minibatch)
    rank = jnp.sum((key[None, :] < key[:, None]).astype(jnp.int32), 1)
    own_rank = lax.iota(jnp.int32, own_rows) * n_out + out
    chosen = own_rank[:, None] == rank[None, :]
    own_index = jnp.sum(jnp.where(chosen, batch_index[None, :], 0), 1)
    own_shard = own_index // rows
    starts = jnp.sum((own_index[None, :] < (own_shard * rows)[:, None]).astype(jnp.int32), 1)
    slot = lax.iota(jnp.int32, own_rows) - starts
    same_shard = (batch_index // rows)[None, :] == (batch_index // rows)[:, None]
    most = jnp.max(jnp.sum(same_shard.astype(jnp.int32), 1))
    overflow = most > SLOTS * n_out
    at = (own_shard // 2) * 32 + slot
    own_core = (own_shard % 2) == core
    at = jnp.stack([jnp.where(own_core, at, -64), jnp.where(own_core, -64, at)])
    at = jnp.broadcast_to(at[:, :, None], (2, own_rows, 128))
    col_norm = jnp.sum(jnp.square(points.astype(F32)), 1)[None]
    order = lax.rem(out - lax.iota(jnp.int32, n_out) + n_out, n_out)
    own_targets = jnp.einsum("im,qms->qsi", chosen.astype(F32), targets, precision=highest)[order]
    own_targets = own_targets.reshape(cols, own_rows)

    def gram(direct, where):
        return pl.pallas_call(
            functools.partial(gram_kernel, n_out, direct),
            grid=(steps,),
            out_shape=(
                jax.ShapeDtypeStruct((own_rows, rows), BF16),
                jax.ShapeDtypeStruct((cols // 2, own_rows), F32),
                jax.ShapeDtypeStruct((cols // 2, own_rows), F32),
                jax.ShapeDtypeStruct((8, 128), F32),
            ),
            in_specs=[
                *weight_specs,
                whole(where.shape),
                whole(got.shape),
                whole(got.shape),
                point_spec,
                pl.BlockSpec((1, BLOCK), lambda i: (0, i)),
            ],
            out_specs=(
                kern_spec,
                whole((cols // 2, own_rows)),
                whole((cols // 2, own_rows)),
                whole((8, 128)),
            ),
            scratch_shapes=[
                pltpu.VMEM((own_rows, width), BF16),
                pltpu.VMEM((own_rows, 128), F32),
                pltpu.VMEM((cols, own_rows), F32),
            ],
            compiler_params=params(),
            name="gram_fetched" if direct else "gram",
        )(*weights, where, got, got_other, points, col_norm)

    def fetch():
        local = own_index - shard * rows
        inside = (local >= 0) & (local < rows)
        picked = jnp.where(inside[:, None], points[jnp.clip(local, 0, rows - 1)].astype(F32), 0.0)
        return gram(True, lax.psum(picked, POINT_AXES).astype(BF16))

    kern, kept, given, tile = lax.cond(overflow, fetch, lambda: gram(False, at))

    pack = pl.pallas_call(
        pack_kernel,
        out_shape=jax.ShapeDtypeStruct((n_chips, cols // 2 + 16, 128), BF16),
        name="pack",
    )(kept, swap_core(given), tile)
    got = lax.all_to_all(pack, CHIP_AXES, 0, 0)
    got_other = swap_core(got)

    base, *parts = pl.pallas_call(
        functools.partial(step_kernel, n_out, ratio),
        grid=(steps,),
        out_shape=[jax.ShapeDtypeStruct((draws, rows), F32)]
        + [jax.ShapeDtypeStruct((draws, rows), BF16)] * (n_out - 1),
        in_specs=[
            pl.BlockSpec(memory_space=pltpu.SMEM),
            pl.BlockSpec(memory_space=pltpu.SMEM),
            whole(own_targets.shape),
            whole(got.shape),
            whole(got.shape),
            feat_spec,
            kern_spec,
            draw_spec,
        ],
        out_specs=[draw_spec] * n_out,
        scratch_shapes=[pltpu.VMEM((cols, own_features), BF16), pltpu.VMEM((cols, own_rows), BF16)],
        compiler_params=params(),
        name="step",
    )(coregion, noise_var, own_targets, got, got_other, feats, kern, own_weights)
    total = base
    for k, part in enumerate(parts, 1):
        part = lax.ppermute(part, "out", [(i, (i - k) % n_out) for i in range(n_out)])
        total = total + part.astype(F32)
    return total.T[None]


def solution(mesh):
    fine = Mesh(mesh.devices.reshape(8, 4, 2, 4), ("z", "y", "core", "out"))
    in_specs = (P(POINT_AXES, None), P("out", POINT_AXES, None), P(), P(), P(), P(), P(), P())
    out_specs = P("out", POINT_AXES, None)
    return jax.shard_map(shards, mesh=fine, in_specs=in_specs, out_specs=out_specs, check_vma=False)
```

time: 711 us -> 103 us (0.14); the launches traced: 701 us -> 102 us
  blocking collectives: 518 us -> 18.4 us
  matrix products: 166 us -> 1.02 us
  Pallas kernels: 0 us -> 24.8 us
  starting transfers between devices: 0 us -> 24.6 us
  waiting for transfers between devices: 0 us -> 19 us
    psum x2 -> x0, blocking collectives: 499 us -> none  [the longest x1 253 us: shards(): batch_rows = lax.psum(picked, 'pts').astype(jnp.bfloat16)]
    dot_general x23 -> x0, matrix products: 166 us -> none  [the longest x8 129 us: feature_map(): jnp.dot(slab, freq_cols, preferred_element_type=jnp.float32) + phase_cols]
    pallas_call x0 -> x5, Pallas kernels: none -> 24.8 us  [the longest x1 8.23 us: shards(): pl.pallas_call(features_kernel, grid=(steps,), out_shape=(jax.ShapeDtypeS...]
    all_gather x2 -> x0, blocking collectives: 19.3 us -> none  [the longest x1 10.2 us: shards(): lax.all_gather(totals[None].astype(jnp.bfloat16), 'out', axis=0, tiled=True)]
    all_to_all x0 -> x1, blocking collectives: none -> 18.4 us  [shards(): got = lax.all_to_all(pack, CHIP_AXES, 0, 0)]
    ppermute x0 -> x9, starting transfers between devices: none -> 13.4 us  [the longest x3 5.72 us: shards(): lax.ppermute(low, 'out', [(i, (i + k) % n_out) for i in range(n_out)])]
    all_to_all x0 -> x1, starting transfers between devices: none -> 11.2 us  [shards(): got = lax.all_to_all(pack, CHIP_AXES, 0, 0)]
    all_to_all x0 -> x1, waiting for transfers between devices: none -> 9.93 us  [shards(): got = lax.all_to_all(pack, CHIP_AXES, 0, 0)]
  transfers between devices with their start and end apart: 0 -> 10, of which waited for: 0 -> 5; matrix products, arithmetic and copies ran while one was open for 0% -> 5% of each run, Pallas kernels for 0% -> 8%
where the time goes in v3:
time: 103 us; the launch traced here: 102 us
  Pallas kernels  24.8 us (24%)
  starting transfers between devices  24.6 us (24%)
  waiting for transfers between devices  19 us (18%)
  blocking collectives  18.4 us (18%)
  local copies, waits for them, and re-layouts  8.01 us (8%)
  other arithmetic  5.21 us (5%)
    all_to_all x1, blocking collectives, shards(): got = lax.all_to_all(pack, CHIP_AXES, 0, 0)  18.4 us
    all_to_all x1, starting transfers between devices, shards(): got = lax.all_to_all(pack, CHIP_AXES, 0, 0)  11.2 us
    all_to_all x1, waiting for transfers between devices, shards(): got = lax.all_to_all(pack, CHIP_AXES, 0, 0)  9.93 us
    pallas_call x1, Pallas kernels, shards(): pl.pallas_call(features_kernel, grid=(steps,), out_shape=(jax.ShapeDtypeS...  8.23 us
    ppermute x3, waiting for transfers between devices, shards(): lax.ppermute(part, 'out', [(i, (i - k) % n_out) for i in range(n_out)])  7.66 us
    unnamed x26, local copies, waits for them, and re-layouts  7.36 us
    pallas_call x1, Pallas kernels, gram(): pl.pallas_call(functools.partial(gram_kernel, n_out, direct), grid=(steps...  6.77 us
    ppermute x3, starting transfers between devices, shards(): lax.ppermute(low, 'out', [(i, (i + k) % n_out) for i in range(n_out)])  5.72 us
  transfers between devices with their start and end apart: 10, of which 5 were waited for; matrix products, arithmetic and copies ran while one was open for 5% of the time, Pallas kernels for 8%

profile of v3, /device:TPU:1, one launch (start us, length us, event | category | flops | bytes accessed | tf_op | source)
XLA Modules:
  0.0 101.9 jit_solution(15032745665489916549)
XLA Ops:
  0.0 1.0 bitcast_convert_fusion.refs_0_
  1.0 2.1 %collective-permute-start = (bf16[16,4096]{1,0:T(8,128)(2,1)S(1)}, bf16[16,4096]{1,0:T(8,128)(2,1)S(1)}, u32[]{:S(2)}, u32[]{:S(2)}) collective-permute-start(bf16[16,4096]{1,0:T(8,128)(2,1)S(1)} %bitcast_convert_fusion.refs_0_), channel_id=1, source_target_pairs={{0,1},{1,2},{2,3},{3,0},{4,5},{5,6},{6,7},{7,4},{8,9},{9,10},{10,1... | collective-permute-start | bytes 393224 | tf_op jit(solution)/shard_map/ppermute | solution.py:245
  3.1 2.5 %collective-permute-start.1 = (bf16[16,4096]{1,0:T(8,128)(2,1)S(1)}, bf16[16,4096]{1,0:T(8,128)(2,1)S(1)}, u32[]{:S(2)}, u32[]{:S(2)}) collective-permute-start(bf16[16,4096]{1,0:T(8,128)(2,1)S(1)} %bitcast_convert_fusion.refs_0_), channel_id=1, source_target_pairs={{0,2},{1,3},{2,0},{3,1},{4,6},{5,7},{6,4},{7,5},{8,10},{9,11},{10,... | collective-permute-start | bytes 393224 | tf_op jit(solution)/shard_map/ppermute | solution.py:245
  5.6 1.2 %collective-permute-start.2 = (bf16[16,4096]{1,0:T(8,128)(2,1)S(1)}, bf16[16,4096]{1,0:T(8,128)(2,1)S(1)}, u32[]{:S(2)}, u32[]{:S(2)}) collective-permute-start(bf16[16,4096]{1,0:T(8,128)(2,1)S(1)} %bitcast_convert_fusion.refs_0_), channel_id=1, source_target_pairs={{0,3},{1,0},{2,1},{3,2},{4,7},{5,4},{6,5},{7,6},{8,11},{9,8},{10,9... | collective-permute-start | bytes 393224 | tf_op jit(solution)/shard_map/ppermute | solution.py:245
  6.7 0.7 add_select_fusion
  7.7 1.2 %copy-done.4 = bf16[256,2048]{1,0:T(8,128)(2,1)S(1)} copy-done((bf16[256,2048]{1,0:T(8,128)(2,1)S(1)}, bf16[256,2048]{1,0:T(8,128)(2,1)}, u32[]{:S(2)}) %copy-start.4) | copy-done | bytes 1048600
  8.9 0.7 copy-done.5
  9.6 0.7 copy-done.6
  10.3 8.2 %features.1 = (bf16[4096,512]{1,0:T(8,128)(2,1)S(1)}, bf16[16,128]{1,0:T(8,128)(2,1)S(1)}) custom-call(s32[1,512]{1,0:T(1,128)S(1)} %bitcast.56, bf16[4096,256]{1,0:T(8,128)(2,1)} %points_ref.1, bf16[256,2048]{1,0:T(8,128)(2,1)S(1)} %copy-done.4, f32[1,2048]{1,0:T(1,128)S(1)} %bitcast.57), custom_call_target="tpu_custom_call" | custom-call | tf_op jit(solution)/shard_map/features/pallas_call | solution.py:252
  18.8 2.7 %project.1 = bf16[32,32,128]{2,1,0:T(8,128)(2,1)} custom-call(bf16[16,4096]{1,0:T(8,128)(2,1)S(1)} %bitcast_convert_fusion.refs_0_, bf16[16,4096]{1,0:T(8,128)(2,1)S(1)} %collective-permute-done.refs_1_, bf16[16,4096]{1,0:T(8,128)(2,1)S(1)} %collective-permute-done.1.refs_2_, bf16[16,4096]{1,0:T(8,128)(2,1)S(1)} %collective-permute-done.2.refs_3_, ...), custom_call_target="tpu_custom_call" | custom-call | tf_op jit(solution)/shard_map/project/pallas_call | solution.py:271
  21.4 1.9 %copy-done.1 = bf16[4096,512]{1,0:T(8,128)(2,1)} copy-done((bf16[4096,512]{1,0:T(8,128)(2,1)}, bf16[4096,512]{1,0:T(8,128)(2,1)S(1)}, u32[]{:S(2)}) %copy-start.1) | copy-done | bytes 4194328
  23.4 11.2 %all-to-all-start = ((bf16[32,32,128]{2,1,0:T(8,128)(2,1)}), bf16[32,32,128]{2,1,0:T(8,128)(2,1)S(1)}, u32[]{:S(2)}, u32[]{:S(2)}) async-start(bf16[32,32,128]{2,1,0:T(8,128)(2,1)} %project.1), calls=%async_computation | async-start | bytes 524288 | tf_op jit(solution)/shard_map/all_to_all | solution.py:281
  35.1 9.9 %all-to-all-done = bf16[32,32,128]{2,1,0:T(8,128)(2,1)S(1)} async-done(((bf16[32,32,128]{2,1,0:T(8,128)(2,1)}), bf16[32,32,128]{2,1,0:T(8,128)(2,1)S(1)}, u32[]{:S(2)}, u32[]{:S(2)}) %all-to-all-start) | async-done | bytes 262176 | tf_op jit(solution)/shard_map/all_to_all | solution.py:281
  45.0 3.8 %collective-permute-start.3 = (bf16[32,32,128]{2,1,0:T(8,128)(2,1)S(1)}, bf16[32,32,128]{2,1,0:T(8,128)(2,1)S(1)}, u32[]{:S(2)}, u32[]{:S(2)}) collective-permute-start(bf16[32,32,128]{2,1,0:T(8,128)(2,1)S(1)} %all-to-all-done), channel_id=1, source_target_pairs={{0,4},{4,0},{1,5},{5,1},{2,6},{6,2},{3,7},{7,3},{8,12},{12,8},{9,1... | collective-permute-start | bytes 786440 | tf_op jit(solution)/shard_map/ppermute | solution.py:218
  48.7 0.6 reduce_max.9
  50.0 1.2 %multiply_reduce_fusion = f32[4096]{0:T(1024)} fusion(bf16[4096,256]{1,0:T(8,128)(2,1)S(1)} %copy-done.9), kind=kLoop, calls=%fused_computation.6 | loop fusion | flops 3141632 | bytes 2113536 | tf_op jit(solution)/shard_map/reduce_sum | solution.py:299
  51.3 6.9 %conditional.1 = ((bf16[128,4096]{1,0:T(8,128)(2,1)}, f32[32,128]{1,0:T(8,128)}, f32[32,128]{1,0:T(8,128)}, f32[8,128]{1,0:T(8,128)S(1)})) conditional(s32[]{:T(128)} %convert_element_type.36, (s32[2,128]{1,0:T(2,128)S(1)}, bf16[16,4096]{1,0:T(8,128)(2,1)S(1)}, bf16[16,4096]{1,0:T(8,128)(2,1)S(1)}, bf16[16,4096]{1,0:T(8,128)(2,1)S(1)}, ...), branch_computations={%region_6.7_spmd, %region_7.9_spmd} | conditional | flops 100485 | bytes 1579880 | solution.py:343
  51.4 6.8 %gram.1 = (bf16[128,4096]{1,0:T(8,128)(2,1)}, f32[32,128]{1,0:T(8,128)}, f32[32,128]{1,0:T(8,128)}, f32[8,128]{1,0:T(8,128)S(1)}) custom-call(bf16[16,4096]{1,0:T(8,128)(2,1)S(1)} %get-tuple-element.54.refs_0_, bf16[16,4096]{1,0:T(8,128)(2,1)S(1)} %get-tuple-element.55.refs_1_, bf16[16,4096]{1,0:T(8,128)(2,1)S(1)} %get-tuple-element.56.refs_2_, ...), custom_call_target="tpu_custom_call" | custom-call | tf_op jit(solution)/shard_map/cond/branch_0_fun/gram/pallas_call | solution.py:305
  58.2 1.4 %collective-permute-done.4.came_ref = f32[32,128]{1,0:T(8,128)S(1)} collective-permute-done((f32[32,128]{1,0:T(8,128)}, f32[32,128]{1,0:T(8,128)S(1)}, u32[]{:S(2)}, u32[]{:S(2)}) %collective-permute-start.4) | collective-permute-done | bytes 16416 | tf_op jit(solution)/shard_map/ppermute | solution.py:218
  59.6 0.6 copy-done.11
  60.2 1.5 %pack.1 = bf16[32,48,128]{2,1,0:T(8,128)(2,1)} custom-call(f32[32,128]{1,0:T(8,128)} %get-tuple-element.87.kept_ref, f32[32,128]{1,0:T(8,128)} %copy-done.11, f32[8,128]{1,0:T(8,128)S(1)} %get-tuple-element.89.tile_ref), custom_call_target="tpu_custom_call" | custom-call | tf_op jit(solution)/shard_map/pack/pallas_call | solution.py:345
  61.7 18.4 %all_to_all.10.refs_3_ = bf16[32,48,128]{2,1,0:T(8,128)(2,1)S(1)} all-to-all(bf16[32,48,128]{2,1,0:T(8,128)(2,1)} %pack.1), channel_id=1, replica_groups=mesh['z'=8,'y'=4,'core'=2,'out'=4] {'z','y'}, dimensions={0} | all-to-all | bytes 786432 | tf_op jit(solution)/shard_map/all_to_all | solution.py:350
  80.1 1.7 %collective-permute-start.5 = (bf16[32,48,128]{2,1,0:T(8,128)(2,1)S(1)}, bf16[32,48,128]{2,1,0:T(8,128)(2,1)S(1)}, u32[]{:S(2)}, u32[]{:S(2)}) collective-permute-start(bf16[32,48,128]{2,1,0:T(8,128)(2,1)S(1)} %all_to_all.10.refs_3_), channel_id=1, source_target_pairs={{0,4},{4,0},{1,5},{5,1},{2,6},{6,2},{3,7},{7,3},{8,12},{12,8},{9,1... | collective-permute-start | bytes 1179656 | tf_op jit(solution)/shard_map/ppermute | solution.py:218
  81.8 1.0 fusion
  82.8 0.6 gather_fusion.1
  83.5 2.2 %copy-done.2 = bf16[4096,512]{1,0:T(8,128)(2,1)S(1)} copy-done((bf16[4096,512]{1,0:T(8,128)(2,1)S(1)}, bf16[4096,512]{1,0:T(8,128)(2,1)}, u32[]{:S(2)}) %copy-start.2) | copy-done | bytes 4194328
  85.6 5.6 %step.1 = (f32[16,4096]{1,0:T(8,128)S(1)}, bf16[16,4096]{1,0:T(8,128)(2,1)S(1)}, bf16[16,4096]{1,0:T(8,128)(2,1)S(1)}, bf16[16,4096]{1,0:T(8,128)(2,1)S(1)}) custom-call(f32[4,4]{1,0:T(4,128)S(1)} %copy-done.7, f32[4]{0:T(128)S(1)} %copy-done.8, f32[64,128]{1,0:T(8,128)S(1)} %bitcast.55, bf16[32,48,128]{2,1,0:T(8,128)(2,1)S(1)} %all_to_all.10.refs_3_, ...), custom_call_target="tpu_custom_call" | custom-call | tf_op jit(solution)/shard_map/step/pallas_call | solution.py:353
  91.4 2.1 %collective-permute-start.7 = (bf16[16,4096]{1,0:T(8,128)(2,1)S(1)}, bf16[16,4096]{1,0:T(8,128)(2,1)S(1)}, u32[]{:S(2)}, u32[]{:S(2)}) collective-permute-start(bf16[16,4096]{1,0:T(8,128)(2,1)S(1)} %get-tuple-element.93), channel_id=1, source_target_pairs={{0,2},{1,3},{2,0},{3,1},{4,6},{5,7},{6,4},{7,5},{8,10},{9,11},{10,... | collective-permute-start | bytes 393224 | tf_op jit(solution)/shard_map/ppermute | solution.py:375
  93.4 3.0 %collective-permute-done.6 = bf16[16,4096]{1,0:T(8,128)(2,1)S(1)} collective-permute-done((bf16[16,4096]{1,0:T(8,128)(2,1)S(1)}, bf16[16,4096]{1,0:T(8,128)(2,1)S(1)}, u32[]{:S(2)}, u32[]{:S(2)}) %collective-permute-start.6) | collective-permute-done | bytes 131104 | tf_op jit(solution)/shard_map/ppermute | solution.py:375
  96.4 1.6 %collective-permute-done.7 = bf16[16,4096]{1,0:T(8,128)(2,1)S(1)} collective-permute-done((bf16[16,4096]{1,0:T(8,128)(2,1)S(1)}, bf16[16,4096]{1,0:T(8,128)(2,1)S(1)}, u32[]{:S(2)}, u32[]{:S(2)}) %collective-permute-start.7) | collective-permute-done | bytes 131104 | tf_op jit(solution)/shard_map/ppermute | solution.py:375
  98.0 3.1 %collective-permute-done.8 = bf16[16,4096]{1,0:T(8,128)(2,1)S(1)} collective-permute-done((bf16[16,4096]{1,0:T(8,128)(2,1)S(1)}, bf16[16,4096]{1,0:T(8,128)(2,1)S(1)}, u32[]{:S(2)}, u32[]{:S(2)}) %collective-permute-start.8) | collective-permute-done | bytes 131104 | tf_op jit(solution)/shard_map/ppermute | solution.py:375
  101.1 0.8 add_bitcast_fusion
  (39 shorter events, 1.2 us)
Async XLA Ops:
  0.0 81.8 %copy-start = (f32[4,512,16]{1,2,0:T(8,128)S(1)}, f32[4,512,16]{1,2,0:T(8,128)}, u32[]{:S(2)}) copy-start(f32[4,512,16]{1,2,0:T(8,128)} %param.13) | copy-start | bytes 393220
  1.0 17.7 %collective-permute-start = (bf16[16,4096]{1,0:T(8,128)(2,1)S(1)}, bf16[16,4096]{1,0:T(8,128)(2,1)S(1)}, u32[]{:S(2)}, u32[]{:S(2)}) collective-permute-start(bf16[16,4096]{1,0:T(8,128)(2,1)S(1)} %bitcast_convert_fusion.refs_0_), channel_id=1, source_target_pairs={{0,1},{1,2},{2,3},{3,0},{4,5},{5,6},{6,7},{7,4},{8,9},{9,10},{10,1... | collective-permute-start | bytes 393224 | tf_op jit(solution)/shard_map/ppermute | solution.py:245
  3.1 15.6 %collective-permute-start.1 = (bf16[16,4096]{1,0:T(8,128)(2,1)S(1)}, bf16[16,4096]{1,0:T(8,128)(2,1)S(1)}, u32[]{:S(2)}, u32[]{:S(2)}) collective-permute-start(bf16[16,4096]{1,0:T(8,128)(2,1)S(1)} %bitcast_convert_fusion.refs_0_), channel_id=1, source_target_pairs={{0,2},{1,3},{2,0},{3,1},{4,6},{5,7},{6,4},{7,5},{8,10},{9,11},{10,... | collective-permute-start | bytes 393224 | tf_op jit(solution)/shard_map/ppermute | solution.py:245
  5.6 13.2 %collective-permute-start.2 = (bf16[16,4096]{1,0:T(8,128)(2,1)S(1)}, bf16[16,4096]{1,0:T(8,128)(2,1)S(1)}, u32[]{:S(2)}, u32[]{:S(2)}) collective-permute-start(bf16[16,4096]{1,0:T(8,128)(2,1)S(1)} %bitcast_convert_fusion.refs_0_), channel_id=1, source_target_pairs={{0,3},{1,0},{2,1},{3,2},{4,7},{5,4},{6,5},{7,6},{8,11},{9,8},{10,9... | collective-permute-start | bytes 393224 | tf_op jit(solution)/shard_map/ppermute | solution.py:245
  7.7 15.7 %copy-start.12 = (s32[128]{0:T(128)}, s32[128]{0:T(128)S(1)}, u32[]{:S(2)}) copy-start(s32[128]{0:T(128)S(1)} %multiply_add_fusion) | copy-start | bytes 1540
  7.7 1.2 %copy-start.4 = (bf16[256,2048]{1,0:T(8,128)(2,1)S(1)}, bf16[256,2048]{1,0:T(8,128)(2,1)}, u32[]{:S(2)}) copy-start(bf16[256,2048]{1,0:T(8,128)(2,1)} %freq_ref.1) | copy-start | bytes 3145732
  8.9 0.7 copy-start.5
  9.6 0.7 copy-start.6
  10.3 39.7 %copy-start.9 = (bf16[4096,256]{1,0:T(8,128)(2,1)S(1)}, bf16[4096,256]{1,0:T(8,128)(2,1)}, u32[]{:S(2)}) copy-start(bf16[4096,256]{1,0:T(8,128)(2,1)} %points_ref.1) | copy-start | bytes 6291460
  18.7 32.6 %copy-start.13 = (s32[128]{0:T(128)}, s32[128]{0:T(128)S(1)}, u32[]{:S(2)}) copy-start(s32[128]{0:T(128)S(1)} %fusion.2) | copy-start | bytes 1540
  21.4 2.0 %copy-start.1 = (bf16[4096,512]{1,0:T(8,128)(2,1)}, bf16[4096,512]{1,0:T(8,128)(2,1)S(1)}, u32[]{:S(2)}) copy-start(bf16[4096,512]{1,0:T(8,128)(2,1)S(1)} %get-tuple-element.85.refs_4_.refs_5_) | copy-start | bytes 12582916
  23.4 21.6 %all-to-all-start = ((bf16[32,32,128]{2,1,0:T(8,128)(2,1)}), bf16[32,32,128]{2,1,0:T(8,128)(2,1)S(1)}, u32[]{:S(2)}, u32[]{:S(2)}) async-start(bf16[32,32,128]{2,1,0:T(8,128)(2,1)} %project.1), calls=%async_computation | async-start | bytes 524288 | tf_op jit(solution)/shard_map/all_to_all | solution.py:281
  45.0 6.3 %collective-permute-start.3 = (bf16[32,32,128]{2,1,0:T(8,128)(2,1)S(1)}, bf16[32,32,128]{2,1,0:T(8,128)(2,1)S(1)}, u32[]{:S(2)}, u32[]{:S(2)}) collective-permute-start(bf16[32,32,128]{2,1,0:T(8,128)(2,1)S(1)} %all-to-all-done), channel_id=1, source_target_pairs={{0,4},{4,0},{1,5},{5,1},{2,6},{6,2},{3,7},{7,3},{8,12},{12,8},{9,1... | collective-permute-start | bytes 786440 | tf_op jit(solution)/shard_map/ppermute | solution.py:218
  51.3 32.2 %copy-start.3 = (f32[1,4096,16]{1,2,0:T(8,128)S(1)}, f32[1,4096,16]{1,2,0:T(8,128)}, u32[]{:S(2)}) copy-start(f32[1,4096,16]{1,2,0:T(8,128)} %param.11) | copy-start | bytes 786436
  51.3 32.2 %copy-start.7 = (f32[4,4]{1,0:T(4,128)S(1)}, f32[4,4]{1,0:T(4,128)}, u32[]{:S(2)}) copy-start(f32[4,4]{1,0:T(4,128)} %refs_0_.1) | copy-start | bytes 196
  51.3 32.2 %copy-start.8 = (f32[4]{0:T(128)S(1)}, f32[4]{0:T(128)}, u32[]{:S(2)}) copy-start(f32[4]{0:T(128)} %refs_1_.1) | copy-start | bytes 52
  58.2 1.4 %collective-permute-start.4 = (f32[32,128]{1,0:T(8,128)}, f32[32,128]{1,0:T(8,128)S(1)}, u32[]{:S(2)}, u32[]{:S(2)}) collective-permute-start(f32[32,128]{1,0:T(8,128)} %get-tuple-element.88), channel_id=1, source_target_pairs={{0,4},{4,0},{1,5},{5,1},{2,6},{6,2},{3,7},{7,3},{8,12},{12,8},{9,1... | collective-permute-start | bytes 49160 | tf_op jit(solution)/shard_map/ppermute | solution.py:218
  59.6 0.6 copy-start.11
  80.1 3.3 %collective-permute-start.5 = (bf16[32,48,128]{2,1,0:T(8,128)(2,1)S(1)}, bf16[32,48,128]{2,1,0:T(8,128)(2,1)S(1)}, u32[]{:S(2)}, u32[]{:S(2)}) collective-permute-start(bf16[32,48,128]{2,1,0:T(8,128)(2,1)S(1)} %all_to_all.10.refs_3_), channel_id=1, source_target_pairs={{0,4},{4,0},{1,5},{5,1},{2,6},{6,2},{3,7},{7,3},{8,12},{12,8},{9,1... | collective-permute-start | bytes 1179656 | tf_op jit(solution)/shard_map/ppermute | solution.py:218
  83.4 2.2 %copy-start.2 = (bf16[4096,512]{1,0:T(8,128)(2,1)S(1)}, bf16[4096,512]{1,0:T(8,128)(2,1)}, u32[]{:S(2)}) copy-start(bf16[4096,512]{1,0:T(8,128)(2,1)} %copy-done.1) | copy-start | bytes 12582916
  91.3 5.1 %collective-permute-start.6 = (bf16[16,4096]{1,0:T(8,128)(2,1)S(1)}, bf16[16,4096]{1,0:T(8,128)(2,1)S(1)}, u32[]{:S(2)}, u32[]{:S(2)}) collective-permute-start(bf16[16,4096]{1,0:T(8,128)(2,1)S(1)} %get-tuple-element.92), channel_id=1, source_target_pairs={{0,3},{1,0},{2,1},{3,2},{4,7},{5,4},{6,5},{7,6},{8,11},{9,8},{10,9... | collective-permute-start | bytes 393224 | tf_op jit(solution)/shard_map/ppermute | solution.py:375
  91.4 6.7 %collective-permute-start.7 = (bf16[16,4096]{1,0:T(8,128)(2,1)S(1)}, bf16[16,4096]{1,0:T(8,128)(2,1)S(1)}, u32[]{:S(2)}, u32[]{:S(2)}) collective-permute-start(bf16[16,4096]{1,0:T(8,128)(2,1)S(1)} %get-tuple-element.93), channel_id=1, source_target_pairs={{0,2},{1,3},{2,0},{3,1},{4,6},{5,7},{6,4},{7,5},{8,10},{9,11},{10,... | collective-permute-start | bytes 393224 | tf_op jit(solution)/shard_map/ppermute | solution.py:375
  93.4 7.7 %collective-permute-start.8 = (bf16[16,4096]{1,0:T(8,128)(2,1)S(1)}, bf16[16,4096]{1,0:T(8,128)(2,1)S(1)}, u32[]{:S(2)}, u32[]{:S(2)}) collective-permute-start(bf16[16,4096]{1,0:T(8,128)(2,1)S(1)} %get-tuple-element.94), channel_id=1, source_target_pairs={{0,1},{1,2},{2,3},{3,0},{4,5},{5,6},{6,7},{7,4},{8,9},{9,10},{10,1... | collective-permute-start | bytes 393224 | tf_op jit(solution)/shard_map/ppermute | solution.py:375

commit v4 on v3

--- a/solution.py
+++ b/solution.py
@@ -12,7 +12,10 @@
 LENGTH = 0.5
 STEP_SIZE = 0.5
 SLOTS = 8
-BLOCK = 512
+CHUNK = 512
+FEATURES_BLOCK = 1024
+GRAM_BLOCK = 2048
+STEP_BLOCK = 2048
 SIN_TURNS = (
     6.283185160088695,
     -41.34165503124932,
@@ -59,13 +62,23 @@
     return pl.BlockSpec(shape, lambda i: (0,) * len(shape))
 
 
-def features_kernel(index_ref, points_ref, freq_ref, phase_ref, feats_ref, sent_ref, local_ref, rows_ref):
+def features_of(points, freq_ref, phase_ref, at, own):
+    phase = phase_ref[:, pl.ds(at, own)] * (0.5 / math.pi)
+    turns = dot(points, freq_ref[:, pl.ds(at, own)]) * (0.5 / math.pi) + phase
+    return cos_turns(turns, math.sqrt(2.0 / freq_ref.shape[1])).astype(BF16)
+
+
+def picked_rows(local, first, points):
+    columns = lax.broadcasted_iota(jnp.int32, (2 * SLOTS, points.shape[0]), 1)
+    return dot((local[:, :1] - first == columns).astype(F32).astype(BF16), points)
+
+
+def features_kernel(shard_rows, index_ref, points_ref, freq_ref, phase_ref, feats_ref, local_ref, rows_ref):
     step = pl.program_id(0)
     out, core, chip = place_of_device()
     block = points_ref.shape[0]
     own = feats_ref.shape[1]
     n_out = freq_ref.shape[1] // own
-    shard_rows = block * pl.num_programs(0)
     minibatch = index_ref.shape[1]
 
     @pl.when(step == 0)
@@ -85,38 +98,45 @@
         rows_ref[...] = jnp.zeros_like(rows_ref)
 
     points = points_ref[...]
-    at = pl.multiple_of(out * own, own)
-    phase = phase_ref[:, pl.ds(at, own)] * (0.5 / math.pi)
-    turns = dot(points, freq_ref[:, pl.ds(at, own)]) * (0.5 / math.pi) + phase
-    feats_ref[...] = cos_turns(turns, math.sqrt(2.0 / freq_ref.shape[1])).astype(BF16)
-    pick = local_ref[:, :1] - step * block == lax.broadcasted_iota(jnp.int32, (2 * SLOTS, block), 1)
-    rows_ref[...] += dot(pick.astype(F32).astype(BF16), points)
-
-    @pl.when(step == pl.num_programs(0) - 1)
+    feats_ref[...] = features_of(points, freq_ref, phase_ref, pl.multiple_of(out * own, own), own)
+    rows_ref[...] += picked_rows(local_ref[...], step * block, points)
+
+
+def project_kernel(n_out, *refs):
+    weight_refs = refs[:n_out]
+    points_ref, freq_ref, phase_ref, local_ref, early_ref, earlier_ref = refs[n_out : n_out + 6]
+    feats_ref, pack_ref, sum_ref, rows_ref = refs[n_out + 6 :]
+    step = pl.program_id(0)
+    steps = pl.num_programs(0)
+    block = points_ref.shape[0]
+    own = feats_ref.shape[1]
+
+    @pl.when(step == 0)
+    def _():
+        sum_ref[...] = jnp.zeros_like(sum_ref)
+        rows_ref[...] = earlier_ref[...]
+
+    def weights(at):
+        here = pl.ds(pl.multiple_of(at * block, block), block)
+        return jnp.concatenate([ref[:, here] for ref in weight_refs], 0)
+
+    points = points_ref[...]
+    at = pl.multiple_of(lax.axis_index("out") * own, own)
+    feats = features_of(points, freq_ref, phase_ref, at, own)
+    feats_ref[...] = feats
+    rows_ref[...] += picked_rows(local_ref[...], (step + steps) * block, points)
+    sum_ref[...] += dot(weights(step), early_ref[...]) + dot(weights(step + steps), feats)
+
+    @pl.when(step == steps - 1)
     def _():
         half = rows_ref.shape[1] // 2
         rows = rows_ref[...]
-        sent_ref[...] = jnp.concatenate([rows[:SLOTS, :half], rows[:SLOTS, half:]], 0).astype(BF16)
-
-
-def project_kernel(n_out, *refs):
-    weight_refs, (feats_ref, sent_ref, pack_ref, sum_ref) = refs[:n_out], refs[n_out:]
-    step = pl.program_id(0)
-
-    @pl.when(step == 0)
-    def _():
-        sum_ref[...] = jnp.zeros_like(sum_ref)
-
-    weights = jnp.concatenate([ref[...] for ref in weight_refs], 0)
-    sum_ref[...] += dot(weights, feats_ref[...])
-
-    @pl.when(step == pl.num_programs(0) - 1)
-    def _():
-        across = sum_ref.shape[1] // 128
+        rows = jnp.concatenate([rows[:SLOTS, :half], rows[:SLOTS, half:]], 0).astype(BF16)
+        across = own // 128
         for at in range(pack_ref.shape[0]):
             r, c = divmod(at, across)
             high, low = split(sum_ref[8 * r : 8 * r + 8, 128 * c : 128 * c + 128])
-            pack_ref[at, :16] = sent_ref[...]
+            pack_ref[at, :16] = rows
             pack_ref[at, 16:] = jnp.concatenate([high.astype(F32), low.astype(F32)], 0).astype(BF16)
 
 
@@ -145,17 +165,22 @@
         row_norm_ref[...] = jnp.broadcast_to(jnp.sum(rows * rows, 1, keepdims=True), row_norm_ref.shape)
         sum_ref[...] = jnp.zeros_like(sum_ref)
         tile = jnp.sum(own_ref[:, 16:].astype(F32), 0) + jnp.sum(other_ref[:, 16:].astype(F32), 0)
-        tile_ref[...] = tile[:8] + tile[8:]
-
-    inner = dot_nt(rows_ref[...], points_ref[...])
-    squared = row_norm_ref[:, :1] + norm_ref[...] - 2.0 * inner
-    scaled_square = (5.0 / (LENGTH * LENGTH)) * jnp.maximum(squared, 0.0)
-    scaled_r = scaled_square * lax.rsqrt(jnp.maximum(scaled_square, 1e-30))
-    kern = (1.0 + scaled_r + scaled_square * (1.0 / 3.0)) * jnp.exp(-scaled_r)
-    kern = kern.astype(BF16)
-    kern_ref[...] = kern
-    weights = jnp.concatenate([ref[...] for ref in weight_refs], 0)
-    sum_ref[...] += dot_nt(weights, kern)
+        high, low = split(tile[:8] + tile[8:])
+        tile_ref[...] = jnp.concatenate([high.astype(F32), low.astype(F32)], 0).astype(BF16)
+
+    total = 0.0
+    for at in range(0, points_ref.shape[0], CHUNK):
+        here = pl.ds(at, CHUNK)
+        inner = dot_nt(rows_ref[...], points_ref[here, :])
+        squared = row_norm_ref[:, :1] + norm_ref[:, here] - 2.0 * inner
+        scaled_square = (5.0 / (LENGTH * LENGTH)) * jnp.maximum(squared, 0.0)
+        scaled_r = scaled_square * lax.rsqrt(jnp.maximum(scaled_square, 1e-30))
+        kern = (1.0 + scaled_r + scaled_square * (1.0 / 3.0)) * jnp.exp(-scaled_r)
+        kern = kern.astype(BF16)
+        kern_ref[:, here] = kern
+        weights = jnp.concatenate([ref[:, here] for ref in weight_refs], 0)
+        total = total + dot_nt(weights, kern)
+    sum_ref[...] += total
 
     @pl.when(step == pl.num_programs(0) - 1)
     def _():
@@ -166,17 +191,10 @@
         given_ref[...] = jnp.where(core == 0, upper, lower)
 
 
-def pack_kernel(kept_ref, came_ref, tile_ref, pack_ref):
-    half = kept_ref.shape[0]
-    high, low = split(tile_ref[...])
-    value = jnp.concatenate([kept_ref[...] + came_ref[...], high.astype(F32), low.astype(F32)], 0).astype(BF16)
-    pack_ref[...] = jnp.broadcast_to(value[None], pack_ref.shape)
-
-
 def step_kernel(n_out, ratio, *refs):
-    coregion_ref, noise_ref, targets_ref, own_ref, other_ref, feats_ref, kern_ref, rep_ref = refs[:8]
-    base_ref, part_refs, (mixed_ref, weighted_ref) = refs[8], refs[9 : 8 + n_out], refs[8 + n_out :]
-    draws = rep_ref.shape[0]
+    coregion_ref, noise_ref, targets_ref, own_ref, other_ref, feats_ref, kern_ref = refs[:7]
+    base_ref, part_refs, (mixed_ref, weighted_ref) = refs[7], refs[8 : 7 + n_out], refs[7 + n_out :]
+    draws = base_ref.shape[0]
     half = n_out * draws // 2
 
     @pl.when(pl.program_id(0) == 0)
@@ -209,7 +227,7 @@
 
     gradient = dot(weighted_ref[...], kern_ref[...]) + dot_nt(mixed_ref[...], feats_ref[...])
     change = -STEP_SIZE * gradient
-    base_ref[...] = rep_ref[...] + change[:draws]
+    base_ref[...] = change[:draws]
     for k, ref in enumerate(part_refs, 1):
         ref[...] = change[draws * k : draws * (k + 1)].astype(BF16)
 
@@ -218,8 +236,8 @@
     return lax.ppermute(value, "core", [(0, 1), (1, 0)])
 
 
-def params():
-    return pltpu.CompilerParams(dimension_semantics=("arbitrary",), vmem_limit_bytes=32 * 1024 * 1024)
+def params(limit=None):
+    return pltpu.CompilerParams(dimension_semantics=("arbitrary",), vmem_limit_bytes=limit)
 
 
 def shards(points, rep_weights, batch_index, targets, noise_var, coregion, frequencies, phases):
@@ -233,7 +251,6 @@
     own_rows = minibatch // n_out
     own_features = frequencies.shape[1] // n_out
     cols = n_out * draws
-    steps = rows // BLOCK
     out, core, chip = place_of_device()
     shard = chip * 2 + core
     ratio = (rows * n_pts) / minibatch
@@ -243,43 +260,59 @@
     weights = [low]
     for k in range(1, n_out):
         weights.append(lax.ppermute(low, "out", [(i, (i + k) % n_out) for i in range(n_out)]))
-    weight_specs = [pl.BlockSpec((draws, BLOCK), lambda i: (0, i))] * n_out
-    point_spec = pl.BlockSpec((BLOCK, width), lambda i: (i, 0))
-    feat_spec = pl.BlockSpec((BLOCK, own_features), lambda i: (i, 0))
-    kern_spec = pl.BlockSpec((own_rows, BLOCK), lambda i: (0, i))
-    draw_spec = pl.BlockSpec((draws, BLOCK), lambda i: (0, i))
-
-    feats, sent_rows = pl.pallas_call(
-        features_kernel,
-        grid=(steps,),
+    weight_specs = lambda block: [pl.BlockSpec((draws, block), lambda i: (0, i))] * n_out
+    point_spec = lambda block: pl.BlockSpec((block, width), lambda i: (i, 0))
+    feat_spec = lambda block: pl.BlockSpec((block, own_features), lambda i: (i, 0))
+    kern_spec = lambda block: pl.BlockSpec((own_rows, block), lambda i: (0, i))
+    draw_spec = lambda block: pl.BlockSpec((draws, block), lambda i: (0, i))
+
+    early = rows // 2 // FEATURES_BLOCK
+    feats, local, picked = pl.pallas_call(
+        functools.partial(features_kernel, rows),
+        grid=(early,),
         out_shape=(
             jax.ShapeDtypeStruct((rows, own_features), BF16),
-            jax.ShapeDtypeStruct((2 * SLOTS, width // 2), BF16),
+            jax.ShapeDtypeStruct((2 * SLOTS, 128), jnp.int32),
+            jax.ShapeDtypeStruct((2 * SLOTS, width), F32),
         ),
         in_specs=[
             whole((1, minibatch)),
-            point_spec,
+            point_spec(FEATURES_BLOCK),
             whole(frequencies.shape),
             whole((1, phases.shape[0])),
         ],
-        out_specs=(feat_spec, whole((2 * SLOTS, width // 2))),
-        scratch_shapes=[pltpu.VMEM((2 * SLOTS, 128), jnp.int32), pltpu.VMEM((2 * SLOTS, width), F32)],
+        out_specs=(feat_spec(FEATURES_BLOCK), whole((2 * SLOTS, 128)), whole((2 * SLOTS, width))),
         compiler_params=params(),
         name="features",
     )(batch_index[None], points, frequencies, phases[None])
 
-    pack = pl.pallas_call(
+    feats, pack = pl.pallas_call(
         functools.partial(project_kernel, n_out),
-        grid=(steps,),
-        out_shape=jax.ShapeDtypeStruct((n_chips, 32, 128), BF16),
-        in_specs=[*weight_specs, feat_spec, whole((2 * SLOTS, width // 2))],
-        out_specs=whole((n_chips, 32, 128)),
-        scratch_shapes=[pltpu.VMEM((cols, own_features), F32)],
+        grid=(early,),
+        out_shape=(
+            jax.ShapeDtypeStruct((rows, own_features), BF16),
+            jax.ShapeDtypeStruct((n_chips, 32, 128), BF16),
+        ),
+        in_specs=[whole((draws, rows))] * n_out
+        + [
+            pl.BlockSpec((FEATURES_BLOCK, width), lambda i: (i + early, 0)),
+            whole(frequencies.shape),
+            whole((1, phases.shape[0])),
+            whole((2 * SLOTS, 128)),
+            feat_spec(FEATURES_BLOCK),
+            whole((2 * SLOTS, width)),
+        ],
+        out_specs=(
+            pl.BlockSpec((FEATURES_BLOCK, own_features), lambda i: (i + early, 0)),
+            whole((n_chips, 32, 128)),
+        ),
+        scratch_shapes=[pltpu.VMEM((cols, own_features), F32), pltpu.VMEM((2 * SLOTS, width), F32)],
+        input_output_aliases={n_out + 4: 0},
         compiler_params=params(),
         name="project",
-    )(*weights, feats, sent_rows)
+    )(*weights, points, frequencies, phases[None], local, feats, picked)
     got = lax.all_to_all(pack, CHIP_AXES, 0, 0)
-    got_other = swap_core(got)
+    batch_index, points_now, targets, _ = lax.optimization_barrier((batch_index, points, targets, pack))
 
     key = batch_index * minibatch + lax.iota(jnp.int32, minibatch)
     rank = jnp.sum((key[None, :] < key[:, None]).astype(jnp.int32), 1)
@@ -296,41 +329,45 @@
     own_core = (own_shard % 2) == core
     at = jnp.stack([jnp.where(own_core, at, -64), jnp.where(own_core, -64, at)])
     at = jnp.broadcast_to(at[:, :, None], (2, own_rows, 128))
-    col_norm = jnp.sum(jnp.square(points.astype(F32)), 1)[None]
+    col_norm = jnp.sum(jnp.square(points_now.astype(F32)), 1)[None]
     order = lax.rem(out - lax.iota(jnp.int32, n_out) + n_out, n_out)
     own_targets = jnp.einsum("im,qms->qsi", chosen.astype(F32), targets, precision=highest)[order]
     own_targets = own_targets.reshape(cols, own_rows)
+    got, at, overflow, own_index, col_norm, own_targets = lax.optimization_barrier(
+        (got, at, overflow, own_index, col_norm, own_targets)
+    )
+    got_other = swap_core(got)
 
     def gram(direct, where):
         return pl.pallas_call(
             functools.partial(gram_kernel, n_out, direct),
-            grid=(steps,),
+            grid=(rows // GRAM_BLOCK,),
             out_shape=(
                 jax.ShapeDtypeStruct((own_rows, rows), BF16),
                 jax.ShapeDtypeStruct((cols // 2, own_rows), F32),
                 jax.ShapeDtypeStruct((cols // 2, own_rows), F32),
-                jax.ShapeDtypeStruct((8, 128), F32),
+                jax.ShapeDtypeStruct((16, 128), BF16),
             ),
             in_specs=[
-                *weight_specs,
+                *weight_specs(GRAM_BLOCK),
                 whole(where.shape),
                 whole(got.shape),
                 whole(got.shape),
-                point_spec,
-                pl.BlockSpec((1, BLOCK), lambda i: (0, i)),
+                point_spec(GRAM_BLOCK),
+                pl.BlockSpec((1, GRAM_BLOCK), lambda i: (0, i)),
             ],
             out_specs=(
-                kern_spec,
+                kern_spec(GRAM_BLOCK),
                 whole((cols // 2, own_rows)),
                 whole((cols // 2, own_rows)),
-                whole((8, 128)),
+                whole((16, 128)),
             ),
             scratch_shapes=[
                 pltpu.VMEM((own_rows, width), BF16),
                 pltpu.VMEM((own_rows, 128), F32),
                 pltpu.VMEM((cols, own_rows), F32),
             ],
-            compiler_params=params(),
+            compiler_params=params(24 * 1024 * 1024),
             name="gram_fetched" if direct else "gram",
         )(*weights, where, got, got_other, points, col_norm)
 
@@ -342,17 +379,14 @@
 
     kern, kept, given, tile = lax.cond(overflow, fetch, lambda: gram(False, at))
 
-    pack = pl.pallas_call(
-        pack_kernel,
-        out_shape=jax.ShapeDtypeStruct((n_chips, cols // 2 + 16, 128), BF16),
-        name="pack",
-    )(kept, swap_core(given), tile)
+    pack = jnp.concatenate([(kept + swap_core(given)).astype(BF16), tile], 0)
+    pack = jnp.broadcast_to(pack[None], (n_chips, *pack.shape))
     got = lax.all_to_all(pack, CHIP_AXES, 0, 0)
     got_other = swap_core(got)
 
     base, *parts = pl.pallas_call(
         functools.partial(step_kernel, n_out, ratio),
-        grid=(steps,),
+        grid=(rows // STEP_BLOCK,),
         out_shape=[jax.ShapeDtypeStruct((draws, rows), F32)]
         + [jax.ShapeDtypeStruct((draws, rows), BF16)] * (n_out - 1),
         in_specs=[
@@ -361,16 +395,15 @@
             whole(own_targets.shape),
             whole(got.shape),
             whole(got.shape),
-            feat_spec,
-            kern_spec,
-            draw_spec,
+            feat_spec(STEP_BLOCK),
+            kern_spec(STEP_BLOCK),
         ],
-        out_specs=[draw_spec] * n_out,
+        out_specs=[draw_spec(STEP_BLOCK)] * n_out,
         scratch_shapes=[pltpu.VMEM((cols, own_features), BF16), pltpu.VMEM((cols, own_rows), BF16)],
-        compiler_params=params(),
+        compiler_params=params(24 * 1024 * 1024),
         name="step",
-    )(coregion, noise_var, own_targets, got, got_other, feats, kern, own_weights)
-    total = base
+    )(coregion, noise_var, own_targets, got, got_other, feats, kern)
+    total = own_weights + base
     for k, part in enumerate(parts, 1):
         part = lax.ppermute(part, "out", [(i, (i - k) % n_out) for i in range(n_out)])
         total = total + part.astype(F32)

time: 103 us -> 88.6 us (0.86)
  Pallas kernels: 24.8 us -> 18.9 us
  local copies, waits for them, and re-layouts: 8.01 us -> 2.91 us
  blocking collectives: 18.4 us -> 17.1 us
  other arithmetic: 5.21 us -> 4.08 us
  starting transfers between devices: 24.6 us -> 25.7 us
    pallas_call x5 -> x4, Pallas kernels: 24.8 us -> 18.9 us  [the longest x1 6.1 us: shards(): pl.pallas_call(functools.partial(project_kernel, n_out), grid=(early,), o...]
    unnamed x26 -> x14, local copies, waits for them, and re-layouts: 7.36 us -> 2.21 us
    all_to_all x1, waiting for transfers between devices: 9.93 us -> 6.65 us  [shards(): got = lax.all_to_all(pack, CHIP_AXES, 0, 0)]
    ppermute x3, waiting for transfers between devices: 1.39 us -> 3.35 us  [swap_core(): return lax.ppermute(value, 'core', [(0, 1), (1, 0)])]
    all_to_all x1, blocking collectives: 18.4 us -> 17.1 us  [shards(): got = lax.all_to_all(pack, CHIP_AXES, 0, 0)]
    ppermute x3, starting transfers between devices: 5.48 us -> 6.53 us  [swap_core(): return lax.ppermute(value, 'core', [(0, 1), (1, 0)])]
  transfers between devices with their start and end apart: 10 -> 10, of which waited for: 5 -> 7; matrix products, arithmetic and copies ran while one was open for 5% -> 3% of each run, Pallas kernels for 8% -> 6%
where the time goes in v4:
time: 88.6 us; the launch traced here: 88.3 us
  starting transfers between devices  25.7 us (29%)
  Pallas kernels  18.9 us (21%)
  waiting for transfers between devices  18.6 us (21%)
  blocking collectives  17.1 us (19%)
  other arithmetic  4.08 us (5%)
  local copies, waits for them, and re-layouts  2.91 us (3%)
    all_to_all x1, blocking collectives, shards(): got = lax.all_to_all(pack, CHIP_AXES, 0, 0)  17.1 us
    all_to_all x1, starting transfers between devices, shards(): got = lax.all_to_all(pack, CHIP_AXES, 0, 0)  11.2 us
    ppermute x3, waiting for transfers between devices, shards(): lax.ppermute(part, 'out', [(i, (i - k) % n_out) for i in range(n_out)])  8.56 us
    all_to_all x1, waiting for transfers between devices, shards(): got = lax.all_to_all(pack, CHIP_AXES, 0, 0)  6.65 us
    ppermute x3, starting transfers between devices, swap_core(): return lax.ppermute(value, 'core', [(0, 1), (1, 0)])  6.53 us
    pallas_call x1, Pallas kernels, shards(): pl.pallas_call(functools.partial(project_kernel, n_out), grid=(early,), o...  6.1 us
    ppermute x3, starting transfers between devices, shards(): lax.ppermute(low, 'out', [(i, (i + k) % n_out) for i in range(n_out)])  5.72 us
    pallas_call x1, Pallas kernels, shards(): pl.pallas_call(functools.partial(features_kernel, rows), grid=(early,), o...  5.56 us
  transfers between devices with their start and end apart: 10, of which 7 were waited for; matrix products, arithmetic and copies ran while one was open for 3% of the time, Pallas kernels for 6%

profile of v4, /device:TPU:1, one launch (start us, length us, event | category | flops | bytes accessed | tf_op | source)
XLA Modules:
  0.0 88.3 jit_solution(17077931147687758664)
XLA Ops:
  0.0 1.1 %bitcast_convert_fusion.refs_0_ = bf16[16,4096]{1,0:T(8,128)(2,1)S(1)} fusion(f32[1,4096,16]{1,2,0:T(8,128)} %param.11), kind=kLoop, calls=%fused_computation.13 | loop fusion | flops 65536 | bytes 393216 | tf_op jit(solution)/shard_map/convert_element_type | solution.py:259
  1.1 2.1 %collective-permute-start = (bf16[16,4096]{1,0:T(8,128)(2,1)S(1)}, bf16[16,4096]{1,0:T(8,128)(2,1)S(1)}, u32[]{:S(2)}, u32[]{:S(2)}) collective-permute-start(bf16[16,4096]{1,0:T(8,128)(2,1)S(1)} %bitcast_convert_fusion.refs_0_), channel_id=1, source_target_pairs={{0,1},{1,2},{2,3},{3,0},{4,5},{5,6},{6,7},{7,4},{8,9},{9,10},{10,1... | collective-permute-start | bytes 393224 | tf_op jit(solution)/shard_map/ppermute | solution.py:262
  3.2 2.5 %collective-permute-start.1 = (bf16[16,4096]{1,0:T(8,128)(2,1)S(1)}, bf16[16,4096]{1,0:T(8,128)(2,1)S(1)}, u32[]{:S(2)}, u32[]{:S(2)}) collective-permute-start(bf16[16,4096]{1,0:T(8,128)(2,1)S(1)} %bitcast_convert_fusion.refs_0_), channel_id=1, source_target_pairs={{0,2},{1,3},{2,0},{3,1},{4,6},{5,7},{6,4},{7,5},{8,10},{9,11},{10,... | collective-permute-start | bytes 393224 | tf_op jit(solution)/shard_map/ppermute | solution.py:262
  5.7 1.2 %collective-permute-start.2 = (bf16[16,4096]{1,0:T(8,128)(2,1)S(1)}, bf16[16,4096]{1,0:T(8,128)(2,1)S(1)}, u32[]{:S(2)}, u32[]{:S(2)}) collective-permute-start(bf16[16,4096]{1,0:T(8,128)(2,1)S(1)} %bitcast_convert_fusion.refs_0_), channel_id=1, source_target_pairs={{0,3},{1,0},{2,1},{3,2},{4,7},{5,4},{6,5},{7,6},{8,11},{9,8},{10,9... | collective-permute-start | bytes 393224 | tf_op jit(solution)/shard_map/ppermute | solution.py:262
  6.9 5.6 %features.1 = (bf16[4096,512]{1,0:T(8,128)(2,1)}, s32[16,128]{1,0:T(8,128)}, f32[16,256]{1,0:T(8,128)}) custom-call(s32[1,512]{1,0:T(1,128)} %bitcast.64, bf16[4096,256]{1,0:T(8,128)(2,1)} %refs_4_.1, bf16[256,2048]{1,0:T(8,128)(2,1)} %refs_5_.1, f32[1,2048]{1,0:T(1,128)} %bitcast.62), custom_call_target="tpu_custom_call" | custom-call | tf_op jit(solution)/shard_map/features/pallas_call | solution.py:270
  12.5 6.1 %project.1 = (bf16[4096,512]{1,0:T(8,128)(2,1)}, bf16[32,32,128]{2,1,0:T(8,128)(2,1)}) custom-call(bf16[16,4096]{1,0:T(8,128)(2,1)S(1)} %bitcast_convert_fusion.refs_0_, bf16[16,4096]{1,0:T(8,128)(2,1)S(1)} %collective-permute-done.refs_1_, bf16[16,4096]{1,0:T(8,128)(2,1)S(1)} %collective-permute-done.1.refs_2_, ...), custom_call_target="tpu_custom_call", output_to_operand_aliasing={{0}: (8, {})} | custom-call | tf_op jit(solution)/shard_map/project/pallas_call | solution.py:289
  18.6 11.2 %all-to-all-start = ((bf16[32,32,128]{2,1,0:T(8,128)(2,1)}), bf16[32,32,128]{2,1,0:T(8,128)(2,1)S(1)}, u32[]{:S(2)}, u32[]{:S(2)}) async-start(bf16[32,32,128]{2,1,0:T(8,128)(2,1)} %get-tuple-element.99), calls=%async_computation | async-start | bytes 524288 | tf_op jit(solution)/shard_map/all_to_all | solution.py:314
  29.8 0.2 convert_reduce_fusion.1
  30.1 0.2 fusion
  30.5 0.3 fusion.5
  30.8 0.3 convert_reduce_fusion
  31.1 0.6 gather_fusion.1
  31.6 0.6 reduce_max.9
  32.9 0.6 multiply_reduce_fusion
  33.6 6.7 %all-to-all-done = bf16[32,32,128]{2,1,0:T(8,128)(2,1)S(1)} async-done(((bf16[32,32,128]{2,1,0:T(8,128)(2,1)}), bf16[32,32,128]{2,1,0:T(8,128)(2,1)S(1)}, u32[]{:S(2)}, u32[]{:S(2)}) %all-to-all-start) | async-done | bytes 262176 | tf_op jit(solution)/shard_map/all_to_all | solution.py:314
  40.3 3.8 %collective-permute-start.3 = (bf16[32,32,128]{2,1,0:T(8,128)(2,1)S(1)}, bf16[32,32,128]{2,1,0:T(8,128)(2,1)S(1)}, u32[]{:S(2)}, u32[]{:S(2)}) collective-permute-start(bf16[32,32,128]{2,1,0:T(8,128)(2,1)S(1)} %all-to-all-done), channel_id=1, source_target_pairs={{0,4},{4,0},{1,5},{5,1},{2,6},{6,2},{3,7},{7,3},{8,12},{12,8},{9,1... | collective-permute-start | bytes 786440 | tf_op jit(solution)/shard_map/ppermute | solution.py:236
  44.1 1.2 %collective-permute-done.3 = bf16[32,32,128]{2,1,0:T(8,128)(2,1)S(1)} collective-permute-done((bf16[32,32,128]{2,1,0:T(8,128)(2,1)S(1)}, bf16[32,32,128]{2,1,0:T(8,128)(2,1)S(1)}, u32[]{:S(2)}, u32[]{:S(2)}) %collective-permute-start.3) | collective-permute-done | bytes 262176 | tf_op jit(solution)/shard_map/ppermute | solution.py:236
  45.3 4.2 %conditional.1 = ((bf16[128,4096]{1,0:T(8,128)(2,1)}, f32[32,128]{1,0:T(8,128)S(1)}, f32[32,128]{1,0:T(8,128)S(1)}, bf16[16,128]{1,0:T(8,128)(2,1)S(1)})) conditional(s32[]{:T(128)} %convert_element_type.42, (bf16[16,4096]{1,0:T(8,128)(2,1)S(1)}, bf16[16,4096]{1,0:T(8,128)(2,1)S(1)}, bf16[16,4096]{1,0:T(8,128)(2,1)S(1)}, ...), branch_computations={%region_6.7_spmd, %region_7.9_spmd} | conditional | flops 100485 | bytes 531276 | solution.py:380
  45.3 4.2 %gram.1 = (bf16[128,4096]{1,0:T(8,128)(2,1)}, f32[32,128]{1,0:T(8,128)S(1)}, f32[32,128]{1,0:T(8,128)S(1)}, bf16[16,128]{1,0:T(8,128)(2,1)S(1)}) custom-call(bf16[16,4096]{1,0:T(8,128)(2,1)S(1)} %get-tuple-element.53.refs_0_, bf16[16,4096]{1,0:T(8,128)(2,1)S(1)} %get-tuple-element.54.refs_1_, bf16[16,4096]{1,0:T(8,128)(2,1)S(1)} %get-tuple-element.55.refs_2_, ...), custom_call_target="tpu_custom_call" | custom-call | tf_op jit(solution)/shard_map/cond/branch_0_fun/gram/pallas_call | solution.py:342
  49.5 0.4 collective-permute-start.4
  49.9 0.8 collective-permute-done.4
  50.8 17.1 %all_to_all.10.refs_3_ = bf16[32,48,128]{2,1,0:T(8,128)(2,1)S(1)} all-to-all(bf16[32,48,128]{2,1,0:T(8,128)(2,1)S(1)} %broadcast_in_dim.76), channel_id=1, replica_groups=mesh['z'=8,'y'=4,'core'=2,'out'=4] {'z','y'}, dimensions={0} | all-to-all | bytes 786432 | tf_op jit(solution)/shard_map/all_to_all | solution.py:384
  67.9 2.3 %collective-permute-start.5 = (bf16[32,48,128]{2,1,0:T(8,128)(2,1)S(1)}, bf16[32,48,128]{2,1,0:T(8,128)(2,1)S(1)}, u32[]{:S(2)}, u32[]{:S(2)}) collective-permute-start(bf16[32,48,128]{2,1,0:T(8,128)(2,1)S(1)} %all_to_all.10.refs_3_), channel_id=1, source_target_pairs={{0,4},{4,0},{1,5},{5,1},{2,6},{6,2},{3,7},{7,3},{8,12},{12,8},{9,1... | collective-permute-start | bytes 1179656 | tf_op jit(solution)/shard_map/ppermute | solution.py:236
  70.2 1.3 %collective-permute-done.5.refs_4_ = bf16[32,48,128]{2,1,0:T(8,128)(2,1)S(1)} collective-permute-done((bf16[32,48,128]{2,1,0:T(8,128)(2,1)S(1)}, bf16[32,48,128]{2,1,0:T(8,128)(2,1)S(1)}, u32[]{:S(2)}, u32[]{:S(2)}) %collective-permute-start.5) | collective-permute-done | bytes 393248 | tf_op jit(solution)/shard_map/ppermute | solution.py:236
  71.6 2.2 %copy-done.1 = bf16[4096,512]{1,0:T(8,128)(2,1)S(1)} copy-done((bf16[4096,512]{1,0:T(8,128)(2,1)S(1)}, bf16[4096,512]{1,0:T(8,128)(2,1)}, u32[]{:S(2)}) %copy-start.1) | copy-done | bytes 4194328
  73.8 3.0 %step.1 = (f32[16,4096]{1,0:T(8,128)S(1)}, bf16[16,4096]{1,0:T(8,128)(2,1)S(1)}, bf16[16,4096]{1,0:T(8,128)(2,1)S(1)}, bf16[16,4096]{1,0:T(8,128)(2,1)S(1)}) custom-call(f32[4,4]{1,0:T(4,128)S(1)} %copy-done.2, f32[4]{0:T(128)S(1)} %copy-done.3, f32[64,128]{1,0:T(8,128)S(1)} %bitcast.59, bf16[32,48,128]{2,1,0:T(8,128)(2,1)S(1)} %all_to_all.10.refs_3_, ...), custom_call_target="tpu_custom_call" | custom-call | tf_op jit(solution)/shard_map/step/pallas_call | solution.py:387
  76.8 1.2 %collective-permute-start.6 = (bf16[16,4096]{1,0:T(8,128)(2,1)S(1)}, bf16[16,4096]{1,0:T(8,128)(2,1)S(1)}, u32[]{:S(2)}, u32[]{:S(2)}) collective-permute-start(bf16[16,4096]{1,0:T(8,128)(2,1)S(1)} %get-tuple-element.115), channel_id=1, source_target_pairs={{0,3},{1,0},{2,1},{3,2},{4,7},{5,4},{6,5},{7,6},{8,11},{9,8},{10,9... | collective-permute-start | bytes 393224 | tf_op jit(solution)/shard_map/ppermute | solution.py:408
  78.0 1.0 %collective-permute-start.7 = (bf16[16,4096]{1,0:T(8,128)(2,1)S(1)}, bf16[16,4096]{1,0:T(8,128)(2,1)S(1)}, u32[]{:S(2)}, u32[]{:S(2)}) collective-permute-start(bf16[16,4096]{1,0:T(8,128)(2,1)S(1)} %get-tuple-element.116), channel_id=1, source_target_pairs={{0,2},{1,3},{2,0},{3,1},{4,6},{5,7},{6,4},{7,5},{8,10},{9,11},{10,... | collective-permute-start | bytes 393224 | tf_op jit(solution)/shard_map/ppermute | solution.py:408
  79.0 2.6 %collective-permute-done.6 = bf16[16,4096]{1,0:T(8,128)(2,1)S(1)} collective-permute-done((bf16[16,4096]{1,0:T(8,128)(2,1)S(1)}, bf16[16,4096]{1,0:T(8,128)(2,1)S(1)}, u32[]{:S(2)}, u32[]{:S(2)}) %collective-permute-start.6) | collective-permute-done | bytes 131104 | tf_op jit(solution)/shard_map/ppermute | solution.py:408
  81.6 2.3 %collective-permute-done.7 = bf16[16,4096]{1,0:T(8,128)(2,1)S(1)} collective-permute-done((bf16[16,4096]{1,0:T(8,128)(2,1)S(1)}, bf16[16,4096]{1,0:T(8,128)(2,1)S(1)}, u32[]{:S(2)}, u32[]{:S(2)}) %collective-permute-start.7) | collective-permute-done | bytes 131104 | tf_op jit(solution)/shard_map/ppermute | solution.py:408
  83.9 3.7 %collective-permute-done.8 = bf16[16,4096]{1,0:T(8,128)(2,1)S(1)} collective-permute-done((bf16[16,4096]{1,0:T(8,128)(2,1)S(1)}, bf16[16,4096]{1,0:T(8,128)(2,1)S(1)}, u32[]{:S(2)}, u32[]{:S(2)}) %collective-permute-start.8) | collective-permute-done | bytes 131104 | tf_op jit(solution)/shard_map/ppermute | solution.py:408
  87.6 0.8 fusion.4
  (29 shorter events, 0.4 us)
Async XLA Ops:
  0.0 30.5 %copy-start = (f32[4,512,16]{1,2,0:T(8,128)S(1)}, f32[4,512,16]{1,2,0:T(8,128)}, u32[]{:S(2)}) copy-start(f32[4,512,16]{1,2,0:T(8,128)} %param.13) | copy-start | bytes 393220
  0.0 12.5 %copy-start.4 = (bf16[4096,256]{1,0:T(8,128)(2,1)S(1)}, bf16[4096,256]{1,0:T(8,128)(2,1)}, u32[]{:S(2)}) copy-start(bf16[4096,256]{1,0:T(8,128)(2,1)} %refs_4_.1) | copy-start | bytes 6291460
  1.1 11.3 %collective-permute-start = (bf16[16,4096]{1,0:T(8,128)(2,1)S(1)}, bf16[16,4096]{1,0:T(8,128)(2,1)S(1)}, u32[]{:S(2)}, u32[]{:S(2)}) collective-permute-start(bf16[16,4096]{1,0:T(8,128)(2,1)S(1)} %bitcast_convert_fusion.refs_0_), channel_id=1, source_target_pairs={{0,1},{1,2},{2,3},{3,0},{4,5},{5,6},{6,7},{7,4},{8,9},{9,10},{10,1... | collective-permute-start | bytes 393224 | tf_op jit(solution)/shard_map/ppermute | solution.py:262
  3.2 9.2 %collective-permute-start.1 = (bf16[16,4096]{1,0:T(8,128)(2,1)S(1)}, bf16[16,4096]{1,0:T(8,128)(2,1)S(1)}, u32[]{:S(2)}, u32[]{:S(2)}) collective-permute-start(bf16[16,4096]{1,0:T(8,128)(2,1)S(1)} %bitcast_convert_fusion.refs_0_), channel_id=1, source_target_pairs={{0,2},{1,3},{2,0},{3,1},{4,6},{5,7},{6,4},{7,5},{8,10},{9,11},{10,... | collective-permute-start | bytes 393224 | tf_op jit(solution)/shard_map/ppermute | solution.py:262
  5.7 6.8 %collective-permute-start.2 = (bf16[16,4096]{1,0:T(8,128)(2,1)S(1)}, bf16[16,4096]{1,0:T(8,128)(2,1)S(1)}, u32[]{:S(2)}, u32[]{:S(2)}) collective-permute-start(bf16[16,4096]{1,0:T(8,128)(2,1)S(1)} %bitcast_convert_fusion.refs_0_), channel_id=1, source_target_pairs={{0,3},{1,0},{2,1},{3,2},{4,7},{5,4},{6,5},{7,6},{8,11},{9,8},{10,9... | collective-permute-start | bytes 393224 | tf_op jit(solution)/shard_map/ppermute | solution.py:262
  12.5 17.3 %copy-start.6 = (s32[512]{0:T(512)S(1)}, s32[512]{0:T(512)}, u32[]{:S(2)}) copy-start(s32[512]{0:T(512)} %param.12) | copy-start | bytes 6148
  18.6 21.6 %all-to-all-start = ((bf16[32,32,128]{2,1,0:T(8,128)(2,1)}), bf16[32,32,128]{2,1,0:T(8,128)(2,1)S(1)}, u32[]{:S(2)}, u32[]{:S(2)}) async-start(bf16[32,32,128]{2,1,0:T(8,128)(2,1)} %get-tuple-element.99), calls=%async_computation | async-start | bytes 524288 | tf_op jit(solution)/shard_map/all_to_all | solution.py:314
  40.3 5.0 %collective-permute-start.3 = (bf16[32,32,128]{2,1,0:T(8,128)(2,1)S(1)}, bf16[32,32,128]{2,1,0:T(8,128)(2,1)S(1)}, u32[]{:S(2)}, u32[]{:S(2)}) collective-permute-start(bf16[32,32,128]{2,1,0:T(8,128)(2,1)S(1)} %all-to-all-done), channel_id=1, source_target_pairs={{0,4},{4,0},{1,5},{5,1},{2,6},{6,2},{3,7},{7,3},{8,12},{12,8},{9,1... | collective-permute-start | bytes 786440 | tf_op jit(solution)/shard_map/ppermute | solution.py:236
  45.3 26.3 %copy-start.2 = (f32[4,4]{1,0:T(4,128)S(1)}, f32[4,4]{1,0:T(4,128)}, u32[]{:S(2)}) copy-start(f32[4,4]{1,0:T(4,128)} %refs_0_.1) | copy-start | bytes 196
  45.3 26.3 %copy-start.3 = (f32[4]{0:T(128)S(1)}, f32[4]{0:T(128)}, u32[]{:S(2)}) copy-start(f32[4]{0:T(128)} %refs_1_.1) | copy-start | bytes 52
  49.5 38.0 %copy-start.5 = (f32[1,4096,16]{1,2,0:T(8,128)S(1)}, f32[1,4096,16]{1,2,0:T(8,128)}, u32[]{:S(2)}) copy-start(f32[1,4096,16]{1,2,0:T(8,128)} %param.11) | copy-start | bytes 786436
  49.5 1.2 %collective-permute-start.4 = (f32[32,128]{1,0:T(8,128)S(1)}, f32[32,128]{1,0:T(8,128)S(1)}, u32[]{:S(2)}, u32[]{:S(2)}) collective-permute-start(f32[32,128]{1,0:T(8,128)S(1)} %get-tuple-element.110), channel_id=1, source_target_pairs={{0,4},{4,0},{1,5},{5,1},{2,6},{6,2},{3,7},{7,3},{8,12},{12,8},{9,1... | collective-permute-start | bytes 49160 | tf_op jit(solution)/shard_map/ppermute | solution.py:236
  67.9 3.7 %collective-permute-start.5 = (bf16[32,48,128]{2,1,0:T(8,128)(2,1)S(1)}, bf16[32,48,128]{2,1,0:T(8,128)(2,1)S(1)}, u32[]{:S(2)}, u32[]{:S(2)}) collective-permute-start(bf16[32,48,128]{2,1,0:T(8,128)(2,1)S(1)} %all_to_all.10.refs_3_), channel_id=1, source_target_pairs={{0,4},{4,0},{1,5},{5,1},{2,6},{6,2},{3,7},{7,3},{8,12},{12,8},{9,1... | collective-permute-start | bytes 1179656 | tf_op jit(solution)/shard_map/ppermute | solution.py:236
  71.6 2.2 %copy-start.1 = (bf16[4096,512]{1,0:T(8,128)(2,1)S(1)}, bf16[4096,512]{1,0:T(8,128)(2,1)}, u32[]{:S(2)}) copy-start(bf16[4096,512]{1,0:T(8,128)(2,1)} %get-tuple-element.112.refs_5_) | copy-start | bytes 12582916
  76.8 4.8 %collective-permute-start.6 = (bf16[16,4096]{1,0:T(8,128)(2,1)S(1)}, bf16[16,4096]{1,0:T(8,128)(2,1)S(1)}, u32[]{:S(2)}, u32[]{:S(2)}) collective-permute-start(bf16[16,4096]{1,0:T(8,128)(2,1)S(1)} %get-tuple-element.115), channel_id=1, source_target_pairs={{0,3},{1,0},{2,1},{3,2},{4,7},{5,4},{6,5},{7,6},{8,11},{9,8},{10,9... | collective-permute-start | bytes 393224 | tf_op jit(solution)/shard_map/ppermute | solution.py:408
  78.0 5.9 %collective-permute-start.7 = (bf16[16,4096]{1,0:T(8,128)(2,1)S(1)}, bf16[16,4096]{1,0:T(8,128)(2,1)S(1)}, u32[]{:S(2)}, u32[]{:S(2)}) collective-permute-start(bf16[16,4096]{1,0:T(8,128)(2,1)S(1)} %get-tuple-element.116), channel_id=1, source_target_pairs={{0,2},{1,3},{2,0},{3,1},{4,6},{5,7},{6,4},{7,5},{8,10},{9,11},{10,... | collective-permute-start | bytes 393224 | tf_op jit(solution)/shard_map/ppermute | solution.py:408
  79.0 8.6 %collective-permute-start.8 = (bf16[16,4096]{1,0:T(8,128)(2,1)S(1)}, bf16[16,4096]{1,0:T(8,128)(2,1)S(1)}, u32[]{:S(2)}, u32[]{:S(2)}) collective-permute-start(bf16[16,4096]{1,0:T(8,128)(2,1)S(1)} %get-tuple-element.117), channel_id=1, source_target_pairs={{0,1},{1,2},{2,3},{3,0},{4,5},{5,6},{6,7},{7,4},{8,9},{9,10},{10,1... | collective-permute-start | bytes 393224 | tf_op jit(solution)/shard_map/ppermute | solution.py:408

commit v5 on v4

--- a/solution.py
+++ b/solution.py
@@ -16,6 +16,7 @@
 FEATURES_BLOCK = 1024
 GRAM_BLOCK = 2048
 STEP_BLOCK = 2048
+SMALL_VMEM = 24 * 1024 * 1024
 SIN_TURNS = (
     6.283185160088695,
     -41.34165503124932,
@@ -73,12 +74,13 @@
     return dot((local[:, :1] - first == columns).astype(F32).astype(BF16), points)
 
 
-def features_kernel(shard_rows, index_ref, points_ref, freq_ref, phase_ref, feats_ref, local_ref, rows_ref):
+def features_kernel(index_ref, points_ref, freq_ref, phase_ref, feats_ref, held_ref, sent_ref, local_ref, rows_ref):
     step = pl.program_id(0)
     out, core, chip = place_of_device()
     block = points_ref.shape[0]
     own = feats_ref.shape[1]
     n_out = freq_ref.shape[1] // own
+    shard_rows = held_ref.shape[0]
     minibatch = index_ref.shape[1]
 
     @pl.when(step == 0)
@@ -98,46 +100,31 @@
         rows_ref[...] = jnp.zeros_like(rows_ref)
 
     points = points_ref[...]
-    feats_ref[...] = features_of(points, freq_ref, phase_ref, pl.multiple_of(out * own, own), own)
-    rows_ref[...] += picked_rows(local_ref[...], step * block, points)
-
-
-def project_kernel(n_out, *refs):
-    weight_refs = refs[:n_out]
-    points_ref, freq_ref, phase_ref, local_ref, early_ref, earlier_ref = refs[n_out : n_out + 6]
-    feats_ref, pack_ref, sum_ref, rows_ref = refs[n_out + 6 :]
-    step = pl.program_id(0)
-    steps = pl.num_programs(0)
-    block = points_ref.shape[0]
-    own = feats_ref.shape[1]
-
-    @pl.when(step == 0)
-    def _():
-        sum_ref[...] = jnp.zeros_like(sum_ref)
-        rows_ref[...] = earlier_ref[...]
-
-    def weights(at):
-        here = pl.ds(pl.multiple_of(at * block, block), block)
-        return jnp.concatenate([ref[:, here] for ref in weight_refs], 0)
-
-    points = points_ref[...]
-    at = pl.multiple_of(lax.axis_index("out") * own, own)
-    feats = features_of(points, freq_ref, phase_ref, at, own)
+    at = pl.multiple_of(out * own, own)
+    phase = phase_ref[:, pl.ds(at, own)] * (0.5 / math.pi)
+    turns = dot(points, freq_ref[:, pl.ds(at, own)]) * (0.5 / math.pi) + phase
+    feats = cos_turns(turns, math.sqrt(2.0 / freq_ref.shape[1])).astype(BF16)
     feats_ref[...] = feats
-    rows_ref[...] += picked_rows(local_ref[...], (step + steps) * block, points)
-    sum_ref[...] += dot(weights(step), early_ref[...]) + dot(weights(step + steps), feats)
-
-    @pl.when(step == steps - 1)
+    held_ref[pl.ds(pl.multiple_of(step * block, block), block), :] = feats
+    columns = lax.broadcasted_iota(jnp.int32, (2 * SLOTS, block), 1)
+    rows_ref[...] += dot((local_ref[:, :1] - step * block == columns).astype(F32).astype(BF16), points)
+
+    @pl.when(step == pl.num_programs(0) - 1)
     def _():
         half = rows_ref.shape[1] // 2
         rows = rows_ref[...]
-        rows = jnp.concatenate([rows[:SLOTS, :half], rows[:SLOTS, half:]], 0).astype(BF16)
-        across = own // 128
-        for at in range(pack_ref.shape[0]):
-            r, c = divmod(at, across)
-            high, low = split(sum_ref[8 * r : 8 * r + 8, 128 * c : 128 * c + 128])
-            pack_ref[at, :16] = rows
-            pack_ref[at, 16:] = jnp.concatenate([high.astype(F32), low.astype(F32)], 0).astype(BF16)
+        sent_ref[...] = jnp.concatenate([rows[:SLOTS, :half], rows[:SLOTS, half:]], 0).astype(BF16)
+
+
+def project_kernel(n_out, *refs):
+    weight_refs, (feats_ref, sent_ref, pack_ref) = refs[:n_out], refs[n_out:]
+    total = dot(jnp.concatenate([ref[...] for ref in weight_refs], 0), feats_ref[...])
+    across = total.shape[1] // 128
+    for at in range(pack_ref.shape[0]):
+        r, c = divmod(at, across)
+        high, low = split(total[8 * r : 8 * r + 8, 128 * c : 128 * c + 128])
+        pack_ref[at, :16] = sent_ref[...]
+        pack_ref[at, 16:] = jnp.concatenate([high.astype(F32), low.astype(F32)], 0).astype(BF16)
 
 
 def gram_kernel(n_out, direct, *refs):
@@ -232,6 +219,10 @@
         ref[...] = change[draws * k : draws * (k + 1)].astype(BF16)
 
 
+def in_hbm(value):
+    return pltpu.with_memory_space_constraint(value, pltpu.HBM)
+
+
 def swap_core(value):
     return lax.ppermute(value, "core", [(0, 1), (1, 0)])
 
@@ -266,14 +257,13 @@
     kern_spec = lambda block: pl.BlockSpec((own_rows, block), lambda i: (0, i))
     draw_spec = lambda block: pl.BlockSpec((draws, block), lambda i: (0, i))
 
-    early = rows // 2 // FEATURES_BLOCK
-    feats, local, picked = pl.pallas_call(
-        functools.partial(features_kernel, rows),
-        grid=(early,),
+    feats, held, sent_rows = pl.pallas_call(
+        features_kernel,
+        grid=(rows // FEATURES_BLOCK,),
         out_shape=(
-            jax.ShapeDtypeStruct((rows, own_features), BF16),
-            jax.ShapeDtypeStruct((2 * SLOTS, 128), jnp.int32),
-            jax.ShapeDtypeStruct((2 * SLOTS, width), F32),
+            pltpu.HBM((rows, own_features), BF16),
+            pltpu.VMEM((rows, own_features), BF16),
+            jax.ShapeDtypeStruct((2 * SLOTS, width // 2), BF16),
         ),
         in_specs=[
             whole((1, minibatch)),
@@ -281,36 +271,25 @@
             whole(frequencies.shape),
             whole((1, phases.shape[0])),
         ],
-        out_specs=(feat_spec(FEATURES_BLOCK), whole((2 * SLOTS, 128)), whole((2 * SLOTS, width))),
-        compiler_params=params(),
+        out_specs=(
+            feat_spec(FEATURES_BLOCK),
+            pl.BlockSpec(memory_space=pltpu.VMEM),
+            whole((2 * SLOTS, width // 2)),
+        ),
+        scratch_shapes=[pltpu.VMEM((2 * SLOTS, 128), jnp.int32), pltpu.VMEM((2 * SLOTS, width), F32)],
+        compiler_params=params(SMALL_VMEM),
         name="features",
-    )(batch_index[None], points, frequencies, phases[None])
-
-    feats, pack = pl.pallas_call(
+    )(in_hbm(batch_index[None]), in_hbm(points), in_hbm(frequencies), in_hbm(phases[None]))
+
+    in_vmem = pl.BlockSpec(memory_space=pltpu.VMEM)
+    pack = pl.pallas_call(
         functools.partial(project_kernel, n_out),
-        grid=(early,),
-        out_shape=(
-            jax.ShapeDtypeStruct((rows, own_features), BF16),
-            jax.ShapeDtypeStruct((n_chips, 32, 128), BF16),
-        ),
-        in_specs=[whole((draws, rows))] * n_out
-        + [
-            pl.BlockSpec((FEATURES_BLOCK, width), lambda i: (i + early, 0)),
-            whole(frequencies.shape),
-            whole((1, phases.shape[0])),
-            whole((2 * SLOTS, 128)),
-            feat_spec(FEATURES_BLOCK),
-            whole((2 * SLOTS, width)),
-        ],
-        out_specs=(
-            pl.BlockSpec((FEATURES_BLOCK, own_features), lambda i: (i + early, 0)),
-            whole((n_chips, 32, 128)),
-        ),
-        scratch_shapes=[pltpu.VMEM((cols, own_features), F32), pltpu.VMEM((2 * SLOTS, width), F32)],
-        input_output_aliases={n_out + 4: 0},
-        compiler_params=params(),
+        out_shape=jax.ShapeDtypeStruct((n_chips, 32, 128), BF16),
+        in_specs=[in_vmem] * (n_out + 2),
+        out_specs=in_vmem,
+        compiler_params=pltpu.CompilerParams(vmem_limit_bytes=SMALL_VMEM),
         name="project",
-    )(*weights, points, frequencies, phases[None], local, feats, picked)
+    )(*weights, pltpu.with_memory_space_constraint(held, pltpu.VMEM), sent_rows)
     got = lax.all_to_all(pack, CHIP_AXES, 0, 0)
     batch_index, points_now, targets, _ = lax.optimization_barrier((batch_index, points, targets, pack))
 
@@ -367,7 +346,7 @@
                 pltpu.VMEM((own_rows, 128), F32),
                 pltpu.VMEM((cols, own_rows), F32),
             ],
-            compiler_params=params(24 * 1024 * 1024),
+            compiler_params=params(SMALL_VMEM),
             name="gram_fetched" if direct else "gram",
         )(*weights, where, got, got_other, points, col_norm)
 
@@ -400,9 +379,9 @@
         ],
         out_specs=[draw_spec(STEP_BLOCK)] * n_out,
         scratch_shapes=[pltpu.VMEM((cols, own_features), BF16), pltpu.VMEM((cols, own_rows), BF16)],
-        compiler_params=params(24 * 1024 * 1024),
+        compiler_params=params(SMALL_VMEM),
         name="step",
-    )(coregion, noise_var, own_targets, got, got_other, feats, kern)
+    )(coregion, noise_var, own_targets, got, got_other, in_hbm(feats), in_hbm(kern))
     total = own_weights + base
     for k, part in enumerate(parts, 1):
         part = lax.ppermute(part, "out", [(i, (i - k) % n_out) for i in range(n_out)])

time: 88.6 us -> 84 us (0.948)
  local copies, waits for them, and re-layouts: 2.91 us -> 0.72 us
  waiting for transfers between devices: 18.6 us -> 17.3 us
  Pallas kernels: 18.9 us -> 17.8 us
    unnamed x14 -> x12, local copies, waits for them, and re-layouts: 2.21 us -> 0.03 us
    pallas_call x2, Pallas kernels: 11.7 us -> 9.94 us  [the longest x1 8.4 us: shards(): pl.pallas_call(features_kernel, grid=(rows // FEATURES_BLOCK,), out_shape...]
    ppermute x3, waiting for transfers between devices: 8.56 us -> 7.21 us  [shards(): lax.ppermute(part, 'out', [(i, (i - k) % n_out) for i in range(n_out)])]
  transfers between devices with their start and end apart: 10 -> 10, of which waited for: 7 -> 7; matrix products, arithmetic and copies ran while one was open for 3% -> 4% of each run, Pallas kernels for 6% -> 10%
where the time goes in v5:
time: 84 us; the launch traced here: 83.7 us
  starting transfers between devices  25.7 us (31%)
  Pallas kernels  17.8 us (21%)
  waiting for transfers between devices  17.3 us (21%)
  blocking collectives  17 us (20%)
  other arithmetic  4.04 us (5%)
  between operations  0.86 us (1%)
    all_to_all x1, blocking collectives, shards(): got = lax.all_to_all(pack, CHIP_AXES, 0, 0)  17 us
    all_to_all x1, starting transfers between devices, shards(): got = lax.all_to_all(pack, CHIP_AXES, 0, 0)  11.2 us
    pallas_call x1, Pallas kernels, shards(): pl.pallas_call(features_kernel, grid=(rows // FEATURES_BLOCK,), out_shape...  8.4 us
    ppermute x3, waiting for transfers between devices, shards(): lax.ppermute(part, 'out', [(i, (i - k) % n_out) for i in range(n_out)])  7.21 us
    ppermute x3, starting transfers between devices, swap_core(): return lax.ppermute(value, 'core', [(0, 1), (1, 0)])  6.59 us
    all_to_all x1, waiting for transfers between devices, shards(): got = lax.all_to_all(pack, CHIP_AXES, 0, 0)  6.52 us
    ppermute x3, starting transfers between devices, shards(): lax.ppermute(low, 'out', [(i, (i + k) % n_out) for i in range(n_out)])  5.72 us
    pallas_call x1, Pallas kernels, gram(): pl.pallas_call(functools.partial(gram_kernel, n_out, direct), grid=(rows...  4.21 us
  transfers between devices with their start and end apart: 10, of which 7 were waited for; matrix products, arithmetic and copies ran while one was open for 4% of the time, Pallas kernels for 10%

profile of v5, /device:TPU:1, one launch (start us, length us, event | category | flops | bytes accessed | tf_op | source)
XLA Modules:
  0.0 83.7 jit_solution(1555298844011939314)
XLA Ops:
  0.0 1.0 %bitcast_convert_fusion.refs_0_ = bf16[16,4096]{1,0:T(8,128)(2,1)S(1)} fusion(f32[1,4096,16]{1,2,0:T(8,128)} %param.11), kind=kLoop, calls=%fused_computation.13 | loop fusion | flops 65536 | bytes 393216 | tf_op jit(solution)/shard_map/convert_element_type | solution.py:250
  1.0 2.1 %collective-permute-start = (bf16[16,4096]{1,0:T(8,128)(2,1)S(1)}, bf16[16,4096]{1,0:T(8,128)(2,1)S(1)}, u32[]{:S(2)}, u32[]{:S(2)}) collective-permute-start(bf16[16,4096]{1,0:T(8,128)(2,1)S(1)} %bitcast_convert_fusion.refs_0_), channel_id=1, source_target_pairs={{0,1},{1,2},{2,3},{3,0},{4,5},{5,6},{6,7},{7,4},{8,9},{9,10},{10,1... | collective-permute-start | bytes 393224 | tf_op jit(solution)/shard_map/ppermute | solution.py:253
  3.1 2.5 %collective-permute-start.1 = (bf16[16,4096]{1,0:T(8,128)(2,1)S(1)}, bf16[16,4096]{1,0:T(8,128)(2,1)S(1)}, u32[]{:S(2)}, u32[]{:S(2)}) collective-permute-start(bf16[16,4096]{1,0:T(8,128)(2,1)S(1)} %bitcast_convert_fusion.refs_0_), channel_id=1, source_target_pairs={{0,2},{1,3},{2,0},{3,1},{4,6},{5,7},{6,4},{7,5},{8,10},{9,11},{10,... | collective-permute-start | bytes 393224 | tf_op jit(solution)/shard_map/ppermute | solution.py:253
  5.6 1.2 %collective-permute-start.2 = (bf16[16,4096]{1,0:T(8,128)(2,1)S(1)}, bf16[16,4096]{1,0:T(8,128)(2,1)S(1)}, u32[]{:S(2)}, u32[]{:S(2)}) collective-permute-start(bf16[16,4096]{1,0:T(8,128)(2,1)S(1)} %bitcast_convert_fusion.refs_0_), channel_id=1, source_target_pairs={{0,3},{1,0},{2,1},{3,2},{4,7},{5,4},{6,5},{7,6},{8,11},{9,8},{10,9... | collective-permute-start | bytes 393224 | tf_op jit(solution)/shard_map/ppermute | solution.py:253
  6.8 8.4 %features.1 = (bf16[4096,512]{1,0:T(8,128)(2,1)}, bf16[4096,512]{1,0:T(8,128)(2,1)S(1)}, bf16[16,128]{1,0:T(8,128)(2,1)S(1)}) custom-call(s32[1,512]{1,0:T(1,128)} %bitcast.62, bf16[4096,256]{1,0:T(8,128)(2,1)} %points_ref.1, bf16[256,2048]{1,0:T(8,128)(2,1)} %freq_ref.1, f32[1,2048]{1,0:T(1,128)} %bitcast.63), custom_call_target="tpu_custom_call" | custom-call | tf_op jit(solution)/shard_map/features/pallas_call | solution.py:260
  15.2 1.5 %project.1 = bf16[32,32,128]{2,1,0:T(8,128)(2,1)} custom-call(bf16[16,4096]{1,0:T(8,128)(2,1)S(1)} %bitcast_convert_fusion.refs_0_, bf16[16,4096]{1,0:T(8,128)(2,1)S(1)} %collective-permute-done.refs_1_, bf16[16,4096]{1,0:T(8,128)(2,1)S(1)} %collective-permute-done.1.refs_2_, bf16[16,4096]{1,0:T(8,128)(2,1)S(1)} %collective-permute-done.2.refs_3_, ...), custom_call_target="tpu_custom_call" | custom-call | tf_op jit(solution)/shard_map/project/pallas_call | solution.py:285
  16.8 11.2 %all-to-all-start = ((bf16[32,32,128]{2,1,0:T(8,128)(2,1)}), bf16[32,32,128]{2,1,0:T(8,128)(2,1)S(1)}, u32[]{:S(2)}, u32[]{:S(2)}) async-start(bf16[32,32,128]{2,1,0:T(8,128)(2,1)} %project.1), calls=%async_computation | async-start | bytes 524288 | tf_op jit(solution)/shard_map/all_to_all | solution.py:293
  28.0 0.2 convert_reduce_fusion.1
  28.2 0.2 fusion
  28.4 0.2 convert_reduce_fusion.2
  28.6 0.3 fusion.5
  29.0 0.3 convert_reduce_fusion
  29.2 0.6 gather_fusion.1
  29.8 0.7 reduce_max.9
  31.2 0.6 multiply_reduce_fusion
  31.9 6.5 %all-to-all-done = bf16[32,32,128]{2,1,0:T(8,128)(2,1)S(1)} async-done(((bf16[32,32,128]{2,1,0:T(8,128)(2,1)}), bf16[32,32,128]{2,1,0:T(8,128)(2,1)S(1)}, u32[]{:S(2)}, u32[]{:S(2)}) %all-to-all-start) | async-done | bytes 262176 | tf_op jit(solution)/shard_map/all_to_all | solution.py:293
  38.4 0.1 broadcast_in_dim.73
  38.5 3.8 %collective-permute-start.3 = (bf16[32,32,128]{2,1,0:T(8,128)(2,1)S(1)}, bf16[32,32,128]{2,1,0:T(8,128)(2,1)S(1)}, u32[]{:S(2)}, u32[]{:S(2)}) collective-permute-start(bf16[32,32,128]{2,1,0:T(8,128)(2,1)S(1)} %all-to-all-done), channel_id=1, source_target_pairs={{0,4},{4,0},{1,5},{5,1},{2,6},{6,2},{3,7},{7,3},{8,12},{12,8},{9,1... | collective-permute-start | bytes 786440 | tf_op jit(solution)/shard_map/ppermute | solution.py:227
  42.3 1.2 %collective-permute-done.3 = bf16[32,32,128]{2,1,0:T(8,128)(2,1)S(1)} collective-permute-done((bf16[32,32,128]{2,1,0:T(8,128)(2,1)S(1)}, bf16[32,32,128]{2,1,0:T(8,128)(2,1)S(1)}, u32[]{:S(2)}, u32[]{:S(2)}) %collective-permute-start.3) | collective-permute-done | bytes 262176 | tf_op jit(solution)/shard_map/ppermute | solution.py:227
  43.5 4.2 %conditional.1 = ((bf16[128,4096]{1,0:T(8,128)(2,1)}, f32[32,128]{1,0:T(8,128)S(1)}, f32[32,128]{1,0:T(8,128)}, bf16[16,128]{1,0:T(8,128)(2,1)S(1)})) conditional(s32[]{:T(128)} %convert_element_type.42, (bf16[16,4096]{1,0:T(8,128)(2,1)S(1)}, bf16[16,4096]{1,0:T(8,128)(2,1)S(1)}, bf16[16,4096]{1,0:T(8,128)(2,1)S(1)}, bf16[16,4096]{1,0:T(8,128)(2,1)S(1)}, ...), branch_computations={%region_6.7_spmd, %region_7.9_spmd} | conditional | flops 100485 | bytes 531276 | solution.py:359
  43.5 4.2 %gram.1 = (bf16[128,4096]{1,0:T(8,128)(2,1)}, f32[32,128]{1,0:T(8,128)S(1)}, f32[32,128]{1,0:T(8,128)}, bf16[16,128]{1,0:T(8,128)(2,1)S(1)}) custom-call(bf16[16,4096]{1,0:T(8,128)(2,1)S(1)} %get-tuple-element.53.refs_0_, bf16[16,4096]{1,0:T(8,128)(2,1)S(1)} %get-tuple-element.54.refs_1_, bf16[16,4096]{1,0:T(8,128)(2,1)S(1)} %get-tuple-element.55.refs_2_, ...), custom_call_target="tpu_custom_call" | custom-call | tf_op jit(solution)/shard_map/cond/branch_0_fun/gram/pallas_call | solution.py:321
  47.7 0.4 collective-permute-start.4
  48.1 1.0 %collective-permute-done.4 = f32[32,128]{1,0:T(8,128)S(1)} collective-permute-done((f32[32,128]{1,0:T(8,128)}, f32[32,128]{1,0:T(8,128)S(1)}, u32[]{:S(2)}, u32[]{:S(2)}) %collective-permute-start.4) | collective-permute-done | bytes 16416 | tf_op jit(solution)/shard_map/ppermute | solution.py:227
  49.2 17.0 %all_to_all.10.refs_3_ = bf16[32,48,128]{2,1,0:T(8,128)(2,1)S(1)} all-to-all(bf16[32,48,128]{2,1,0:T(8,128)(2,1)S(1)} %broadcast_in_dim.75), channel_id=1, replica_groups=mesh['z'=8,'y'=4,'core'=2,'out'=4] {'z','y'}, dimensions={0} | all-to-all | bytes 786432 | tf_op jit(solution)/shard_map/all_to_all | solution.py:363
  66.2 2.4 %collective-permute-start.5 = (bf16[32,48,128]{2,1,0:T(8,128)(2,1)S(1)}, bf16[32,48,128]{2,1,0:T(8,128)(2,1)S(1)}, u32[]{:S(2)}, u32[]{:S(2)}) collective-permute-start(bf16[32,48,128]{2,1,0:T(8,128)(2,1)S(1)} %all_to_all.10.refs_3_), channel_id=1, source_target_pairs={{0,4},{4,0},{1,5},{5,1},{2,6},{6,2},{3,7},{7,3},{8,12},{12,8},{9,1... | collective-permute-start | bytes 1179656 | tf_op jit(solution)/shard_map/ppermute | solution.py:227
  68.5 1.3 %collective-permute-done.5.refs_4_ = bf16[32,48,128]{2,1,0:T(8,128)(2,1)S(1)} collective-permute-done((bf16[32,48,128]{2,1,0:T(8,128)(2,1)S(1)}, bf16[32,48,128]{2,1,0:T(8,128)(2,1)S(1)}, u32[]{:S(2)}, u32[]{:S(2)}) %collective-permute-start.5) | collective-permute-done | bytes 393248 | tf_op jit(solution)/shard_map/ppermute | solution.py:227
  69.9 3.7 %step.1 = (f32[16,4096]{1,0:T(8,128)S(1)}, bf16[16,4096]{1,0:T(8,128)(2,1)S(1)}, bf16[16,4096]{1,0:T(8,128)(2,1)S(1)}, bf16[16,4096]{1,0:T(8,128)(2,1)S(1)}) custom-call(f32[4,4]{1,0:T(4,128)S(1)} %copy-done.1, f32[4]{0:T(128)S(1)} %copy-done.2, f32[64,128]{1,0:T(8,128)S(1)} %bitcast.59, bf16[32,48,128]{2,1,0:T(8,128)(2,1)S(1)} %all_to_all.10.refs_3_, ...), custom_call_target="tpu_custom_call" | custom-call | tf_op jit(solution)/shard_map/step/pallas_call | solution.py:366
  73.7 2.1 %collective-permute-start.7 = (bf16[16,4096]{1,0:T(8,128)(2,1)S(1)}, bf16[16,4096]{1,0:T(8,128)(2,1)S(1)}, u32[]{:S(2)}, u32[]{:S(2)}) collective-permute-start(bf16[16,4096]{1,0:T(8,128)(2,1)S(1)} %get-tuple-element.112), channel_id=1, source_target_pairs={{0,2},{1,3},{2,0},{3,1},{4,6},{5,7},{6,4},{7,5},{8,10},{9,11},{10,... | collective-permute-start | bytes 393224 | tf_op jit(solution)/shard_map/ppermute | solution.py:387
  75.7 2.6 %collective-permute-done.6 = bf16[16,4096]{1,0:T(8,128)(2,1)S(1)} collective-permute-done((bf16[16,4096]{1,0:T(8,128)(2,1)S(1)}, bf16[16,4096]{1,0:T(8,128)(2,1)S(1)}, u32[]{:S(2)}, u32[]{:S(2)}) %collective-permute-start.6) | collective-permute-done | bytes 131104 | tf_op jit(solution)/shard_map/ppermute | solution.py:387
  78.4 1.4 %collective-permute-done.7 = bf16[16,4096]{1,0:T(8,128)(2,1)S(1)} collective-permute-done((bf16[16,4096]{1,0:T(8,128)(2,1)S(1)}, bf16[16,4096]{1,0:T(8,128)(2,1)S(1)}, u32[]{:S(2)}, u32[]{:S(2)}) %collective-permute-start.7) | collective-permute-done | bytes 131104 | tf_op jit(solution)/shard_map/ppermute | solution.py:387
  79.8 3.2 %collective-permute-done.8 = bf16[16,4096]{1,0:T(8,128)(2,1)S(1)} collective-permute-done((bf16[16,4096]{1,0:T(8,128)(2,1)S(1)}, bf16[16,4096]{1,0:T(8,128)(2,1)S(1)}, u32[]{:S(2)}, u32[]{:S(2)}) %collective-permute-start.8) | collective-permute-done | bytes 131104 | tf_op jit(solution)/shard_map/ppermute | solution.py:387
  83.0 0.8 fusion.4
  (27 shorter events, 0.3 us)
Async XLA Ops:
  0.0 28.6 %copy-start = (f32[4,512,16]{1,2,0:T(8,128)S(1)}, f32[4,512,16]{1,2,0:T(8,128)}, u32[]{:S(2)}) copy-start(f32[4,512,16]{1,2,0:T(8,128)} %param.13) | copy-start | bytes 393220
  1.0 14.2 %collective-permute-start = (bf16[16,4096]{1,0:T(8,128)(2,1)S(1)}, bf16[16,4096]{1,0:T(8,128)(2,1)S(1)}, u32[]{:S(2)}, u32[]{:S(2)}) collective-permute-start(bf16[16,4096]{1,0:T(8,128)(2,1)S(1)} %bitcast_convert_fusion.refs_0_), channel_id=1, source_target_pairs={{0,1},{1,2},{2,3},{3,0},{4,5},{5,6},{6,7},{7,4},{8,9},{9,10},{10,1... | collective-permute-start | bytes 393224 | tf_op jit(solution)/shard_map/ppermute | solution.py:253
  3.1 12.1 %collective-permute-start.1 = (bf16[16,4096]{1,0:T(8,128)(2,1)S(1)}, bf16[16,4096]{1,0:T(8,128)(2,1)S(1)}, u32[]{:S(2)}, u32[]{:S(2)}) collective-permute-start(bf16[16,4096]{1,0:T(8,128)(2,1)S(1)} %bitcast_convert_fusion.refs_0_), channel_id=1, source_target_pairs={{0,2},{1,3},{2,0},{3,1},{4,6},{5,7},{6,4},{7,5},{8,10},{9,11},{10,... | collective-permute-start | bytes 393224 | tf_op jit(solution)/shard_map/ppermute | solution.py:253
  5.6 9.6 %collective-permute-start.2 = (bf16[16,4096]{1,0:T(8,128)(2,1)S(1)}, bf16[16,4096]{1,0:T(8,128)(2,1)S(1)}, u32[]{:S(2)}, u32[]{:S(2)}) collective-permute-start(bf16[16,4096]{1,0:T(8,128)(2,1)S(1)} %bitcast_convert_fusion.refs_0_), channel_id=1, source_target_pairs={{0,3},{1,0},{2,1},{3,2},{4,7},{5,4},{6,5},{7,6},{8,11},{9,8},{10,9... | collective-permute-start | bytes 393224 | tf_op jit(solution)/shard_map/ppermute | solution.py:253
  6.7 21.2 %copy-start.5 = (s32[512]{0:T(512)S(1)}, s32[512]{0:T(512)}, u32[]{:S(2)}) copy-start(s32[512]{0:T(512)} %param.12) | copy-start | bytes 6148
  6.8 24.5 %copy-start.3 = (bf16[4096,256]{1,0:T(8,128)(2,1)S(1)}, bf16[4096,256]{1,0:T(8,128)(2,1)}, u32[]{:S(2)}) copy-start(bf16[4096,256]{1,0:T(8,128)(2,1)} %points_ref.1) | copy-start | bytes 6291460
  16.8 21.6 %all-to-all-start = ((bf16[32,32,128]{2,1,0:T(8,128)(2,1)}), bf16[32,32,128]{2,1,0:T(8,128)(2,1)S(1)}, u32[]{:S(2)}, u32[]{:S(2)}) async-start(bf16[32,32,128]{2,1,0:T(8,128)(2,1)} %project.1), calls=%async_computation | async-start | bytes 524288 | tf_op jit(solution)/shard_map/all_to_all | solution.py:293
  38.5 5.0 %collective-permute-start.3 = (bf16[32,32,128]{2,1,0:T(8,128)(2,1)S(1)}, bf16[32,32,128]{2,1,0:T(8,128)(2,1)S(1)}, u32[]{:S(2)}, u32[]{:S(2)}) collective-permute-start(bf16[32,32,128]{2,1,0:T(8,128)(2,1)S(1)} %all-to-all-done), channel_id=1, source_target_pairs={{0,4},{4,0},{1,5},{5,1},{2,6},{6,2},{3,7},{7,3},{8,12},{12,8},{9,1... | collective-permute-start | bytes 786440 | tf_op jit(solution)/shard_map/ppermute | solution.py:227
  43.5 26.4 %copy-start.1 = (f32[4,4]{1,0:T(4,128)S(1)}, f32[4,4]{1,0:T(4,128)}, u32[]{:S(2)}) copy-start(f32[4,4]{1,0:T(4,128)} %refs_0_.1) | copy-start | bytes 196
  43.5 26.4 %copy-start.2 = (f32[4]{0:T(128)S(1)}, f32[4]{0:T(128)}, u32[]{:S(2)}) copy-start(f32[4]{0:T(128)} %refs_1_.1) | copy-start | bytes 52
  47.7 35.3 %copy-start.4 = (f32[1,4096,16]{1,2,0:T(8,128)S(1)}, f32[1,4096,16]{1,2,0:T(8,128)}, u32[]{:S(2)}) copy-start(f32[1,4096,16]{1,2,0:T(8,128)} %param.11) | copy-start | bytes 786436
  47.7 1.4 %collective-permute-start.4 = (f32[32,128]{1,0:T(8,128)}, f32[32,128]{1,0:T(8,128)S(1)}, u32[]{:S(2)}, u32[]{:S(2)}) collective-permute-start(f32[32,128]{1,0:T(8,128)} %get-tuple-element.106), channel_id=1, source_target_pairs={{0,4},{4,0},{1,5},{5,1},{2,6},{6,2},{3,7},{7,3},{8,12},{12,8},{9,1... | collective-permute-start | bytes 49160 | tf_op jit(solution)/shard_map/ppermute | solution.py:227
  66.2 3.7 %collective-permute-start.5 = (bf16[32,48,128]{2,1,0:T(8,128)(2,1)S(1)}, bf16[32,48,128]{2,1,0:T(8,128)(2,1)S(1)}, u32[]{:S(2)}, u32[]{:S(2)}) collective-permute-start(bf16[32,48,128]{2,1,0:T(8,128)(2,1)S(1)} %all_to_all.10.refs_3_), channel_id=1, source_target_pairs={{0,4},{4,0},{1,5},{5,1},{2,6},{6,2},{3,7},{7,3},{8,12},{12,8},{9,1... | collective-permute-start | bytes 1179656 | tf_op jit(solution)/shard_map/ppermute | solution.py:227
  73.6 4.8 %collective-permute-start.6 = (bf16[16,4096]{1,0:T(8,128)(2,1)S(1)}, bf16[16,4096]{1,0:T(8,128)(2,1)S(1)}, u32[]{:S(2)}, u32[]{:S(2)}) collective-permute-start(bf16[16,4096]{1,0:T(8,128)(2,1)S(1)} %get-tuple-element.111), channel_id=1, source_target_pairs={{0,3},{1,0},{2,1},{3,2},{4,7},{5,4},{6,5},{7,6},{8,11},{9,8},{10,9... | collective-permute-start | bytes 393224 | tf_op jit(solution)/shard_map/ppermute | solution.py:387
  73.7 6.1 %collective-permute-start.7 = (bf16[16,4096]{1,0:T(8,128)(2,1)S(1)}, bf16[16,4096]{1,0:T(8,128)(2,1)S(1)}, u32[]{:S(2)}, u32[]{:S(2)}) collective-permute-start(bf16[16,4096]{1,0:T(8,128)(2,1)S(1)} %get-tuple-element.112), channel_id=1, source_target_pairs={{0,2},{1,3},{2,0},{3,1},{4,6},{5,7},{6,4},{7,5},{8,10},{9,11},{10,... | collective-permute-start | bytes 393224 | tf_op jit(solution)/shard_map/ppermute | solution.py:387
  75.7 7.2 %collective-permute-start.8 = (bf16[16,4096]{1,0:T(8,128)(2,1)S(1)}, bf16[16,4096]{1,0:T(8,128)(2,1)S(1)}, u32[]{:S(2)}, u32[]{:S(2)}) collective-permute-start(bf16[16,4096]{1,0:T(8,128)(2,1)S(1)} %get-tuple-element.113), channel_id=1, source_target_pairs={{0,1},{1,2},{2,3},{3,0},{4,5},{5,6},{6,7},{7,4},{8,9},{9,10},{10,1... | collective-permute-start | bytes 393224 | tf_op jit(solution)/shard_map/ppermute | solution.py:387

commit v6 on v5

--- a/solution.py
+++ b/solution.py
@@ -12,9 +12,8 @@
 LENGTH = 0.5
 STEP_SIZE = 0.5
 SLOTS = 8
-CHUNK = 512
+CHUNK = 1024
 FEATURES_BLOCK = 1024
-GRAM_BLOCK = 2048
 STEP_BLOCK = 2048
 SMALL_VMEM = 24 * 1024 * 1024
 SIN_TURNS = (
@@ -152,8 +151,7 @@
         row_norm_ref[...] = jnp.broadcast_to(jnp.sum(rows * rows, 1, keepdims=True), row_norm_ref.shape)
         sum_ref[...] = jnp.zeros_like(sum_ref)
         tile = jnp.sum(own_ref[:, 16:].astype(F32), 0) + jnp.sum(other_ref[:, 16:].astype(F32), 0)
-        high, low = split(tile[:8] + tile[8:])
-        tile_ref[...] = jnp.concatenate([high.astype(F32), low.astype(F32)], 0).astype(BF16)
+        tile_ref[...] = tile[:8] + tile[8:]
 
     total = 0.0
     for at in range(0, points_ref.shape[0], CHUNK):
@@ -193,8 +191,9 @@
         def mix(values):
             return [sum(c * v for c, v in zip(line, values)) for line in mixer]
 
-        own = jnp.sum(own_ref[:, :half].astype(F32), 0)
-        other = jnp.sum(other_ref[:, :half].astype(F32), 0)
+        got = [own_ref[p].astype(F32) for p in range(own_ref.shape[0])]
+        own = sum(block[:half] for block in got)
+        other = sum(other_ref[p].astype(F32)[:half] for p in range(other_ref.shape[0]))
         total = jnp.concatenate([jnp.where(core == 0, own, other), jnp.where(core == 0, other, own)], 0)
         fitted = mix([total[draws * k : draws * (k + 1)] for k in range(n_out)])
         scaled = [
@@ -203,8 +202,7 @@
         weighted = jnp.concatenate(mix(scaled), 0).astype(BF16)
         weighted_ref[...] = (weighted.astype(F32) * ratio).astype(BF16)
         across = mixed_ref.shape[1] // 128
-        tiles = [own_ref[p, half:].astype(F32) for p in range(own_ref.shape[0])]
-        tiles = [tile[:8] + tile[8:] for tile in tiles]
+        tiles = [block[half:] for block in got]
         lines = [
             jnp.concatenate(tiles[across * r : across * (r + 1)], 1) for r in range(n_out * draws // 8)
         ]
@@ -221,6 +219,10 @@
 
 def in_hbm(value):
     return pltpu.with_memory_space_constraint(value, pltpu.HBM)
+
+
+def far_first(n_out):
+    return sorted(range(1, n_out), key=lambda k: -min(k, n_out - k))
 
 
 def swap_core(value):
@@ -248,9 +250,9 @@
 
     own_weights = rep_weights[0].T
     low = own_weights.astype(BF16)
-    weights = [low]
-    for k in range(1, n_out):
-        weights.append(lax.ppermute(low, "out", [(i, (i + k) % n_out) for i in range(n_out)]))
+    weights = [low] * n_out
+    for k in far_first(n_out):
+        weights[k] = lax.ppermute(low, "out", [(i, (i + k) % n_out) for i in range(n_out)])
     weight_specs = lambda block: [pl.BlockSpec((draws, block), lambda i: (0, i))] * n_out
     point_spec = lambda block: pl.BlockSpec((block, width), lambda i: (i, 0))
     feat_spec = lambda block: pl.BlockSpec((block, own_features), lambda i: (i, 0))
@@ -320,26 +322,19 @@
     def gram(direct, where):
         return pl.pallas_call(
             functools.partial(gram_kernel, n_out, direct),
-            grid=(rows // GRAM_BLOCK,),
+            grid=(1,),
             out_shape=(
                 jax.ShapeDtypeStruct((own_rows, rows), BF16),
                 jax.ShapeDtypeStruct((cols // 2, own_rows), F32),
                 jax.ShapeDtypeStruct((cols // 2, own_rows), F32),
-                jax.ShapeDtypeStruct((16, 128), BF16),
+                jax.ShapeDtypeStruct((8, 128), F32),
             ),
-            in_specs=[
-                *weight_specs(GRAM_BLOCK),
-                whole(where.shape),
-                whole(got.shape),
-                whole(got.shape),
-                point_spec(GRAM_BLOCK),
-                pl.BlockSpec((1, GRAM_BLOCK), lambda i: (0, i)),
-            ],
+            in_specs=[pl.BlockSpec(memory_space=pltpu.VMEM)] * (n_out + 5),
             out_specs=(
-                kern_spec(GRAM_BLOCK),
-                whole((cols // 2, own_rows)),
-                whole((cols // 2, own_rows)),
-                whole((16, 128)),
+                pl.BlockSpec(memory_space=pltpu.VMEM),
+                pl.BlockSpec(memory_space=pltpu.VMEM),
+                pl.BlockSpec(memory_space=pltpu.VMEM),
+                pl.BlockSpec(memory_space=pltpu.VMEM),
             ),
             scratch_shapes=[
                 pltpu.VMEM((own_rows, width), BF16),
@@ -348,7 +343,7 @@
             ],
             compiler_params=params(SMALL_VMEM),
             name="gram_fetched" if direct else "gram",
-        )(*weights, where, got, got_other, points, col_norm)
+        )(*weights, where, got, got_other, pltpu.with_memory_space_constraint(points, pltpu.VMEM), col_norm)
 
     def fetch():
         local = own_index - shard * rows
@@ -358,7 +353,7 @@
 
     kern, kept, given, tile = lax.cond(overflow, fetch, lambda: gram(False, at))
 
-    pack = jnp.concatenate([(kept + swap_core(given)).astype(BF16), tile], 0)
+    pack = jnp.concatenate([kept + swap_core(given), tile], 0).astype(BF16)
     pack = jnp.broadcast_to(pack[None], (n_chips, *pack.shape))
     got = lax.all_to_all(pack, CHIP_AXES, 0, 0)
     got_other = swap_core(got)
@@ -383,8 +378,8 @@
         name="step",
     )(coregion, noise_var, own_targets, got, got_other, in_hbm(feats), in_hbm(kern))
     total = own_weights + base
-    for k, part in enumerate(parts, 1):
-        part = lax.ppermute(part, "out", [(i, (i - k) % n_out) for i in range(n_out)])
+    for k in far_first(n_out):
+        part = lax.ppermute(parts[k - 1], "out", [(i, (i - k) % n_out) for i in range(n_out)])
         total = total + part.astype(F32)
     return total.T[None]
 

time: 84 us -> 81.4 us (0.969)
  Pallas kernels: 17.8 us -> 16.6 us
  blocking collectives: 17 us -> 15.8 us
    pallas_call x1, Pallas kernels: 4.21 us -> 2.96 us  [gram(): pl.pallas_call(functools.partial(gram_kernel, n_out, direct), grid=(1,),...]
    all_to_all x1, blocking collectives: 17 us -> 15.8 us  [shards(): got = lax.all_to_all(pack, CHIP_AXES, 0, 0)]
where the time goes in v6:
time: 81.4 us; the launch traced here: 81.1 us
  starting transfers between devices  26.3 us (32%)
  Pallas kernels  16.6 us (20%)
  waiting for transfers between devices  16.5 us (20%)
  blocking collectives  15.8 us (19%)
  other arithmetic  4.04 us (5%)
  between operations  0.85 us (1%)
    all_to_all x1, blocking collectives, shards(): got = lax.all_to_all(pack, CHIP_AXES, 0, 0)  15.8 us
    all_to_all x1, starting transfers between devices, shards(): got = lax.all_to_all(pack, CHIP_AXES, 0, 0)  11.2 us
    pallas_call x1, Pallas kernels, shards(): pl.pallas_call(features_kernel, grid=(rows // FEATURES_BLOCK,), out_shape...  8.4 us
    ppermute x3, starting transfers between devices, swap_core(): return lax.ppermute(value, 'core', [(0, 1), (1, 0)])  6.61 us
    all_to_all x1, waiting for transfers between devices, shards(): got = lax.all_to_all(pack, CHIP_AXES, 0, 0)  6.52 us
    ppermute x3, waiting for transfers between devices, shards(): lax.ppermute(parts[k - 1], 'out', [(i, (i - k) % n_out) for i in range(n_...  6.48 us
    ppermute x3, starting transfers between devices, shards(): lax.ppermute(low, 'out', [(i, (i + k) % n_out) for i in range(n_out)])  5.72 us
    pallas_call x1, Pallas kernels, shards(): pl.pallas_call(functools.partial(step_kernel, n_out, ratio), grid=(rows /...  3.65 us
  transfers between devices with their start and end apart: 10, of which 7 were waited for; matrix products, arithmetic and copies ran while one was open for 4% of the time, Pallas kernels for 10%

profile of v6, /device:TPU:1, one launch (start us, length us, event | category | flops | bytes accessed | tf_op | source)
XLA Modules:
  0.0 81.1 jit_solution(974580739042804064)
XLA Ops:
  0.0 1.0 %bitcast_convert_fusion.refs_0_ = bf16[16,4096]{1,0:T(8,128)(2,1)S(1)} fusion(f32[1,4096,16]{1,2,0:T(8,128)} %param.11), kind=kLoop, calls=%fused_computation.13 | loop fusion | flops 65536 | bytes 393216 | tf_op jit(solution)/shard_map/convert_element_type | solution.py:252
  1.0 2.1 %collective-permute-start = (bf16[16,4096]{1,0:T(8,128)(2,1)S(1)}, bf16[16,4096]{1,0:T(8,128)(2,1)S(1)}, u32[]{:S(2)}, u32[]{:S(2)}) collective-permute-start(bf16[16,4096]{1,0:T(8,128)(2,1)S(1)} %bitcast_convert_fusion.refs_0_), channel_id=1, source_target_pairs={{0,1},{1,2},{2,3},{3,0},{4,5},{5,6},{6,7},{7,4},{8,9},{9,10},{10,1... | collective-permute-start | bytes 393224 | tf_op jit(solution)/shard_map/ppermute | solution.py:255
  3.1 2.5 %collective-permute-start.1 = (bf16[16,4096]{1,0:T(8,128)(2,1)S(1)}, bf16[16,4096]{1,0:T(8,128)(2,1)S(1)}, u32[]{:S(2)}, u32[]{:S(2)}) collective-permute-start(bf16[16,4096]{1,0:T(8,128)(2,1)S(1)} %bitcast_convert_fusion.refs_0_), channel_id=1, source_target_pairs={{0,2},{1,3},{2,0},{3,1},{4,6},{5,7},{6,4},{7,5},{8,10},{9,11},{10,... | collective-permute-start | bytes 393224 | tf_op jit(solution)/shard_map/ppermute | solution.py:255
  5.6 1.2 %collective-permute-start.2 = (bf16[16,4096]{1,0:T(8,128)(2,1)S(1)}, bf16[16,4096]{1,0:T(8,128)(2,1)S(1)}, u32[]{:S(2)}, u32[]{:S(2)}) collective-permute-start(bf16[16,4096]{1,0:T(8,128)(2,1)S(1)} %bitcast_convert_fusion.refs_0_), channel_id=1, source_target_pairs={{0,3},{1,0},{2,1},{3,2},{4,7},{5,4},{6,5},{7,6},{8,11},{9,8},{10,9... | collective-permute-start | bytes 393224 | tf_op jit(solution)/shard_map/ppermute | solution.py:255
  6.8 8.4 %features.1 = (bf16[4096,512]{1,0:T(8,128)(2,1)}, bf16[4096,512]{1,0:T(8,128)(2,1)S(1)}, bf16[16,128]{1,0:T(8,128)(2,1)S(1)}) custom-call(s32[1,512]{1,0:T(1,128)} %bitcast.62, bf16[4096,256]{1,0:T(8,128)(2,1)} %points_ref.1, bf16[256,2048]{1,0:T(8,128)(2,1)} %freq_ref.1, f32[1,2048]{1,0:T(1,128)} %bitcast.63), custom_call_target="tpu_custom_call" | custom-call | tf_op jit(solution)/shard_map/features/pallas_call | solution.py:262
  15.2 1.5 %project.1 = bf16[32,32,128]{2,1,0:T(8,128)(2,1)} custom-call(bf16[16,4096]{1,0:T(8,128)(2,1)S(1)} %bitcast_convert_fusion.refs_0_, bf16[16,4096]{1,0:T(8,128)(2,1)S(1)} %collective-permute-done.refs_1_, bf16[16,4096]{1,0:T(8,128)(2,1)S(1)} %collective-permute-done.1.refs_2_, bf16[16,4096]{1,0:T(8,128)(2,1)S(1)} %collective-permute-done.2.refs_3_, ...), custom_call_target="tpu_custom_call" | custom-call | tf_op jit(solution)/shard_map/project/pallas_call | solution.py:287
  16.8 11.2 %all-to-all-start = ((bf16[32,32,128]{2,1,0:T(8,128)(2,1)}), bf16[32,32,128]{2,1,0:T(8,128)(2,1)S(1)}, u32[]{:S(2)}, u32[]{:S(2)}) async-start(bf16[32,32,128]{2,1,0:T(8,128)(2,1)} %project.1), calls=%async_computation | async-start | bytes 524288 | tf_op jit(solution)/shard_map/all_to_all | solution.py:295
  28.0 0.2 convert_reduce_fusion.1
  28.2 0.2 fusion
  28.4 0.2 convert_reduce_fusion.2
  28.6 0.3 fusion.5
  29.0 0.3 convert_reduce_fusion
  29.2 0.6 gather_fusion.1
  29.8 0.7 reduce_max.9
  31.2 0.6 multiply_reduce_fusion
  31.9 6.5 %all-to-all-done = bf16[32,32,128]{2,1,0:T(8,128)(2,1)S(1)} async-done(((bf16[32,32,128]{2,1,0:T(8,128)(2,1)}), bf16[32,32,128]{2,1,0:T(8,128)(2,1)S(1)}, u32[]{:S(2)}, u32[]{:S(2)}) %all-to-all-start) | async-done | bytes 262176 | tf_op jit(solution)/shard_map/all_to_all | solution.py:295
  38.5 3.8 %collective-permute-start.3 = (bf16[32,32,128]{2,1,0:T(8,128)(2,1)S(1)}, bf16[32,32,128]{2,1,0:T(8,128)(2,1)S(1)}, u32[]{:S(2)}, u32[]{:S(2)}) collective-permute-start(bf16[32,32,128]{2,1,0:T(8,128)(2,1)S(1)} %all-to-all-done), channel_id=1, source_target_pairs={{0,4},{4,0},{1,5},{5,1},{2,6},{6,2},{3,7},{7,3},{8,12},{12,8},{9,1... | collective-permute-start | bytes 786440 | tf_op jit(solution)/shard_map/ppermute | solution.py:229
  42.3 1.2 %collective-permute-done.3 = bf16[32,32,128]{2,1,0:T(8,128)(2,1)S(1)} collective-permute-done((bf16[32,32,128]{2,1,0:T(8,128)(2,1)S(1)}, bf16[32,32,128]{2,1,0:T(8,128)(2,1)S(1)}, u32[]{:S(2)}, u32[]{:S(2)}) %collective-permute-start.3) | collective-permute-done | bytes 262176 | tf_op jit(solution)/shard_map/ppermute | solution.py:229
  43.5 3.0 %conditional.1 = ((bf16[128,4096]{1,0:T(8,128)(2,1)}, f32[32,128]{1,0:T(8,128)S(1)}, f32[32,128]{1,0:T(8,128)}, f32[8,128]{1,0:T(8,128)S(1)})) conditional(s32[]{:T(128)} %convert_element_type.44, (bf16[16,4096]{1,0:T(8,128)(2,1)S(1)}, bf16[16,4096]{1,0:T(8,128)(2,1)S(1)}, bf16[16,4096]{1,0:T(8,128)(2,1)S(1)}, bf16[16,4096]{1,0:T(8,128)(2,1)S(1)}, ...), branch_computations={%region_6.7_spmd, %region_7.9_spmd} | conditional | flops 100485 | bytes 531276 | solution.py:354
  43.5 3.0 %gram.1 = (bf16[128,4096]{1,0:T(8,128)(2,1)}, f32[32,128]{1,0:T(8,128)S(1)}, f32[32,128]{1,0:T(8,128)}, f32[8,128]{1,0:T(8,128)S(1)}) custom-call(bf16[16,4096]{1,0:T(8,128)(2,1)S(1)} %get-tuple-element.67.refs_0_, bf16[16,4096]{1,0:T(8,128)(2,1)S(1)} %get-tuple-element.68.refs_1_, bf16[16,4096]{1,0:T(8,128)(2,1)S(1)} %get-tuple-element.69.refs_2_, ...), custom_call_target="tpu_custom_call" | custom-call | tf_op jit(solution)/shard_map/cond/branch_0_fun/gram/pallas_call | solution.py:323
  46.4 0.4 collective-permute-start.4
  46.8 1.0 %collective-permute-done.4 = f32[32,128]{1,0:T(8,128)S(1)} collective-permute-done((f32[32,128]{1,0:T(8,128)}, f32[32,128]{1,0:T(8,128)S(1)}, u32[]{:S(2)}, u32[]{:S(2)}) %collective-permute-start.4) | collective-permute-done | bytes 16416 | tf_op jit(solution)/shard_map/ppermute | solution.py:229
  47.9 15.8 %all_to_all.10.refs_3_ = bf16[32,40,128]{2,1,0:T(8,128)(2,1)S(1)} all-to-all(bf16[32,40,128]{2,1,0:T(8,128)(2,1)S(1)} %broadcast_in_dim.75), channel_id=1, replica_groups=mesh['z'=8,'y'=4,'core'=2,'out'=4] {'z','y'}, dimensions={0} | all-to-all | bytes 655360 | tf_op jit(solution)/shard_map/all_to_all | solution.py:358
  63.8 2.4 %collective-permute-start.5 = (bf16[32,40,128]{2,1,0:T(8,128)(2,1)S(1)}, bf16[32,40,128]{2,1,0:T(8,128)(2,1)S(1)}, u32[]{:S(2)}, u32[]{:S(2)}) collective-permute-start(bf16[32,40,128]{2,1,0:T(8,128)(2,1)S(1)} %all_to_all.10.refs_3_), channel_id=1, source_target_pairs={{0,4},{4,0},{1,5},{5,1},{2,6},{6,2},{3,7},{7,3},{8,12},{12,8},{9,1... | collective-permute-start | bytes 983048 | tf_op jit(solution)/shard_map/ppermute | solution.py:229
  66.2 1.3 %collective-permute-done.5.refs_4_ = bf16[32,40,128]{2,1,0:T(8,128)(2,1)S(1)} collective-permute-done((bf16[32,40,128]{2,1,0:T(8,128)(2,1)S(1)}, bf16[32,40,128]{2,1,0:T(8,128)(2,1)S(1)}, u32[]{:S(2)}, u32[]{:S(2)}) %collective-permute-start.5) | collective-permute-done | bytes 327712 | tf_op jit(solution)/shard_map/ppermute | solution.py:229
  67.4 3.7 %step.1 = (f32[16,4096]{1,0:T(8,128)S(1)}, bf16[16,4096]{1,0:T(8,128)(2,1)S(1)}, bf16[16,4096]{1,0:T(8,128)(2,1)S(1)}, bf16[16,4096]{1,0:T(8,128)(2,1)S(1)}) custom-call(f32[4,4]{1,0:T(4,128)S(1)} %copy-done.2, f32[4]{0:T(128)S(1)} %copy-done.3, f32[64,128]{1,0:T(8,128)S(1)} %bitcast.59, bf16[32,40,128]{2,1,0:T(8,128)(2,1)S(1)} %all_to_all.10.refs_3_, ...), custom_call_target="tpu_custom_call" | custom-call | tf_op jit(solution)/shard_map/step/pallas_call | solution.py:361
  71.1 0.3 collective-permute-start.6
  71.4 2.5 %collective-permute-start.7 = (bf16[16,4096]{1,0:T(8,128)(2,1)S(1)}, bf16[16,4096]{1,0:T(8,128)(2,1)S(1)}, u32[]{:S(2)}, u32[]{:S(2)}) collective-permute-start(bf16[16,4096]{1,0:T(8,128)(2,1)S(1)} %get-tuple-element.126), channel_id=1, source_target_pairs={{0,3},{1,0},{2,1},{3,2},{4,7},{5,4},{6,5},{7,6},{8,11},{9,8},{10,9... | collective-permute-start | bytes 393224 | tf_op jit(solution)/shard_map/ppermute | solution.py:382
  73.9 3.5 %collective-permute-done.6 = bf16[16,4096]{1,0:T(8,128)(2,1)S(1)} collective-permute-done((bf16[16,4096]{1,0:T(8,128)(2,1)S(1)}, bf16[16,4096]{1,0:T(8,128)(2,1)S(1)}, u32[]{:S(2)}, u32[]{:S(2)}) %collective-permute-start.6) | collective-permute-done | bytes 131104 | tf_op jit(solution)/shard_map/ppermute | solution.py:382
  77.4 0.4 collective-permute-done.7
  77.8 2.6 %collective-permute-done.8 = bf16[16,4096]{1,0:T(8,128)(2,1)S(1)} collective-permute-done((bf16[16,4096]{1,0:T(8,128)(2,1)S(1)}, bf16[16,4096]{1,0:T(8,128)(2,1)S(1)}, u32[]{:S(2)}, u32[]{:S(2)}) %collective-permute-start.8) | collective-permute-done | bytes 131104 | tf_op jit(solution)/shard_map/ppermute | solution.py:382
  80.4 0.8 fusion.4
  (28 shorter events, 0.3 us)
Async XLA Ops:
  0.0 28.6 %copy-start = (f32[4,512,16]{1,2,0:T(8,128)S(1)}, f32[4,512,16]{1,2,0:T(8,128)}, u32[]{:S(2)}) copy-start(f32[4,512,16]{1,2,0:T(8,128)} %param.13) | copy-start | bytes 393220
  1.0 14.2 %collective-permute-start = (bf16[16,4096]{1,0:T(8,128)(2,1)S(1)}, bf16[16,4096]{1,0:T(8,128)(2,1)S(1)}, u32[]{:S(2)}, u32[]{:S(2)}) collective-permute-start(bf16[16,4096]{1,0:T(8,128)(2,1)S(1)} %bitcast_convert_fusion.refs_0_), channel_id=1, source_target_pairs={{0,1},{1,2},{2,3},{3,0},{4,5},{5,6},{6,7},{7,4},{8,9},{9,10},{10,1... | collective-permute-start | bytes 393224 | tf_op jit(solution)/shard_map/ppermute | solution.py:255
  3.1 12.1 %collective-permute-start.1 = (bf16[16,4096]{1,0:T(8,128)(2,1)S(1)}, bf16[16,4096]{1,0:T(8,128)(2,1)S(1)}, u32[]{:S(2)}, u32[]{:S(2)}) collective-permute-start(bf16[16,4096]{1,0:T(8,128)(2,1)S(1)} %bitcast_convert_fusion.refs_0_), channel_id=1, source_target_pairs={{0,2},{1,3},{2,0},{3,1},{4,6},{5,7},{6,4},{7,5},{8,10},{9,11},{10,... | collective-permute-start | bytes 393224 | tf_op jit(solution)/shard_map/ppermute | solution.py:255
  5.6 9.6 %collective-permute-start.2 = (bf16[16,4096]{1,0:T(8,128)(2,1)S(1)}, bf16[16,4096]{1,0:T(8,128)(2,1)S(1)}, u32[]{:S(2)}, u32[]{:S(2)}) collective-permute-start(bf16[16,4096]{1,0:T(8,128)(2,1)S(1)} %bitcast_convert_fusion.refs_0_), channel_id=1, source_target_pairs={{0,3},{1,0},{2,1},{3,2},{4,7},{5,4},{6,5},{7,6},{8,11},{9,8},{10,9... | collective-permute-start | bytes 393224 | tf_op jit(solution)/shard_map/ppermute | solution.py:255
  6.7 21.2 %copy-start.5 = (s32[512]{0:T(512)S(1)}, s32[512]{0:T(512)}, u32[]{:S(2)}) copy-start(s32[512]{0:T(512)} %param.12) | copy-start | bytes 6148
  6.8 24.5 %copy-start.1 = (bf16[4096,256]{1,0:T(8,128)(2,1)S(1)}, bf16[4096,256]{1,0:T(8,128)(2,1)}, u32[]{:S(2)}) copy-start(bf16[4096,256]{1,0:T(8,128)(2,1)} %points_ref.1) | copy-start | bytes 6291460
  16.8 21.6 %all-to-all-start = ((bf16[32,32,128]{2,1,0:T(8,128)(2,1)}), bf16[32,32,128]{2,1,0:T(8,128)(2,1)S(1)}, u32[]{:S(2)}, u32[]{:S(2)}) async-start(bf16[32,32,128]{2,1,0:T(8,128)(2,1)} %project.1), calls=%async_computation | async-start | bytes 524288 | tf_op jit(solution)/shard_map/all_to_all | solution.py:295
  38.5 5.0 %collective-permute-start.3 = (bf16[32,32,128]{2,1,0:T(8,128)(2,1)S(1)}, bf16[32,32,128]{2,1,0:T(8,128)(2,1)S(1)}, u32[]{:S(2)}, u32[]{:S(2)}) collective-permute-start(bf16[32,32,128]{2,1,0:T(8,128)(2,1)S(1)} %all-to-all-done), channel_id=1, source_target_pairs={{0,4},{4,0},{1,5},{5,1},{2,6},{6,2},{3,7},{7,3},{8,12},{12,8},{9,1... | collective-permute-start | bytes 786440 | tf_op jit(solution)/shard_map/ppermute | solution.py:229
  43.5 23.9 %copy-start.2 = (f32[4,4]{1,0:T(4,128)S(1)}, f32[4,4]{1,0:T(4,128)}, u32[]{:S(2)}) copy-start(f32[4,4]{1,0:T(4,128)} %refs_0_.1) | copy-start | bytes 196
  43.5 23.9 %copy-start.3 = (f32[4]{0:T(128)S(1)}, f32[4]{0:T(128)}, u32[]{:S(2)}) copy-start(f32[4]{0:T(128)} %refs_1_.1) | copy-start | bytes 52
  46.4 33.9 %copy-start.4 = (f32[1,4096,16]{1,2,0:T(8,128)S(1)}, f32[1,4096,16]{1,2,0:T(8,128)}, u32[]{:S(2)}) copy-start(f32[1,4096,16]{1,2,0:T(8,128)} %param.11) | copy-start | bytes 786436
  46.4 1.4 %collective-permute-start.4 = (f32[32,128]{1,0:T(8,128)}, f32[32,128]{1,0:T(8,128)S(1)}, u32[]{:S(2)}, u32[]{:S(2)}) collective-permute-start(f32[32,128]{1,0:T(8,128)} %get-tuple-element.139), channel_id=1, source_target_pairs={{0,4},{4,0},{1,5},{5,1},{2,6},{6,2},{3,7},{7,3},{8,12},{12,8},{9,1... | collective-permute-start | bytes 49160 | tf_op jit(solution)/shard_map/ppermute | solution.py:229
  63.8 3.6 %collective-permute-start.5 = (bf16[32,40,128]{2,1,0:T(8,128)(2,1)S(1)}, bf16[32,40,128]{2,1,0:T(8,128)(2,1)S(1)}, u32[]{:S(2)}, u32[]{:S(2)}) collective-permute-start(bf16[32,40,128]{2,1,0:T(8,128)(2,1)S(1)} %all_to_all.10.refs_3_), channel_id=1, source_target_pairs={{0,4},{4,0},{1,5},{5,1},{2,6},{6,2},{3,7},{7,3},{8,12},{12,8},{9,1... | collective-permute-start | bytes 983048 | tf_op jit(solution)/shard_map/ppermute | solution.py:229
  71.1 6.3 %collective-permute-start.6 = (bf16[16,4096]{1,0:T(8,128)(2,1)S(1)}, bf16[16,4096]{1,0:T(8,128)(2,1)S(1)}, u32[]{:S(2)}, u32[]{:S(2)}) collective-permute-start(bf16[16,4096]{1,0:T(8,128)(2,1)S(1)} %get-tuple-element.125), channel_id=1, source_target_pairs={{0,2},{1,3},{2,0},{3,1},{4,6},{5,7},{6,4},{7,5},{8,10},{9,11},{10,... | collective-permute-start | bytes 393224 | tf_op jit(solution)/shard_map/ppermute | solution.py:382
  71.4 6.4 %collective-permute-start.7 = (bf16[16,4096]{1,0:T(8,128)(2,1)S(1)}, bf16[16,4096]{1,0:T(8,128)(2,1)S(1)}, u32[]{:S(2)}, u32[]{:S(2)}) collective-permute-start(bf16[16,4096]{1,0:T(8,128)(2,1)S(1)} %get-tuple-element.126), channel_id=1, source_target_pairs={{0,3},{1,0},{2,1},{3,2},{4,7},{5,4},{6,5},{7,6},{8,11},{9,8},{10,9... | collective-permute-start | bytes 393224 | tf_op jit(solution)/shard_map/ppermute | solution.py:382
  73.9 6.5 %collective-permute-start.8 = (bf16[16,4096]{1,0:T(8,128)(2,1)S(1)}, bf16[16,4096]{1,0:T(8,128)(2,1)S(1)}, u32[]{:S(2)}, u32[]{:S(2)}) collective-permute-start(bf16[16,4096]{1,0:T(8,128)(2,1)S(1)} %get-tuple-element.127), channel_id=1, source_target_pairs={{0,1},{1,2},{2,3},{3,0},{4,5},{5,6},{6,7},{7,4},{8,9},{9,10},{10,1... | collective-permute-start | bytes 393224 | tf_op jit(solution)/shard_map/ppermute | solution.py:382

commit v7 on v6

--- a/solution.py
+++ b/solution.py
@@ -13,7 +13,7 @@
 STEP_SIZE = 0.5
 SLOTS = 8
 CHUNK = 1024
-FEATURES_BLOCK = 1024
+FEATURES_BLOCK = 2048
 STEP_BLOCK = 2048
 SMALL_VMEM = 24 * 1024 * 1024
 SIN_TURNS = (
@@ -24,7 +24,7 @@
     39.53670460277009,
 )
 POINT_AXES = ("z", "y", "core")
-CHIP_AXES = ("z", "y")
+ROOT = (4, 2)
 BF16 = jnp.bfloat16
 F32 = jnp.float32
 NT = (((1,), (1,)), ((), ()))
@@ -219,6 +219,13 @@
 
 def in_hbm(value):
     return pltpu.with_memory_space_constraint(value, pltpu.HBM)
+
+
+def exchange(value):
+    z, y = lax.axis_size("z"), lax.axis_size("y")
+    order = [((ROOT[0] + a) % z) * y + (ROOT[1] + b) % y for a in range(z) for b in range(y)]
+    groups = [[2 * chip + core for chip in order] for core in range(2)]
+    return lax.all_to_all(value, POINT_AXES, 0, 0, axis_index_groups=groups)
 
 
 def far_first(n_out):
@@ -292,7 +299,7 @@
         compiler_params=pltpu.CompilerParams(vmem_limit_bytes=SMALL_VMEM),
         name="project",
     )(*weights, pltpu.with_memory_space_constraint(held, pltpu.VMEM), sent_rows)
-    got = lax.all_to_all(pack, CHIP_AXES, 0, 0)
+    got = exchange(pack)
     batch_index, points_now, targets, _ = lax.optimization_barrier((batch_index, points, targets, pack))
 
     key = batch_index * minibatch + lax.iota(jnp.int32, minibatch)
@@ -306,7 +313,10 @@
     same_shard = (batch_index // rows)[None, :] == (batch_index // rows)[:, None]
     most = jnp.max(jnp.sum(same_shard.astype(jnp.int32), 1))
     overflow = most > SLOTS * n_out
-    at = (own_shard // 2) * 32 + slot
+    own_chip = own_shard // 2
+    n_y = lax.axis_size("y")
+    block = (own_chip // n_y - ROOT[0]) % lax.axis_size("z") * n_y + (own_chip - ROOT[1]) % n_y
+    at = block * 32 + slot
     own_core = (own_shard % 2) == core
     at = jnp.stack([jnp.where(own_core, at, -64), jnp.where(own_core, -64, at)])
     at = jnp.broadcast_to(at[:, :, None], (2, own_rows, 128))
@@ -355,7 +365,7 @@
 
     pack = jnp.concatenate([kept + swap_core(given), tile], 0).astype(BF16)
     pack = jnp.broadcast_to(pack[None], (n_chips, *pack.shape))
-    got = lax.all_to_all(pack, CHIP_AXES, 0, 0)
+    got = exchange(pack)
     got_other = swap_core(got)
 
     base, *parts = pl.pallas_call(

time: 81.4 us -> 77.2 us (0.948)
  waiting for transfers between devices: 16.5 us -> 11.2 us
  blocking collectives: 15.8 us -> 17.7 us
    all_to_all x1, waiting for transfers between devices: 6.52 us -> 1.28 us  [exchange(): return lax.all_to_all(value, POINT_AXES, 0, 0, axis_index_groups=groups)]
    ppermute x3, starting transfers between devices: 6.61 us -> 3.7 us  [swap_core(): return lax.ppermute(value, 'core', [(0, 1), (1, 0)])]
    all_to_all x1, starting transfers between devices: 11.2 us -> 13.3 us  [exchange(): return lax.all_to_all(value, POINT_AXES, 0, 0, axis_index_groups=groups)]
    all_to_all x1, blocking collectives: 15.8 us -> 17.7 us  [exchange(): return lax.all_to_all(value, POINT_AXES, 0, 0, axis_index_groups=groups)]
  transfers between devices with their start and end apart: 10 -> 10, of which waited for: 7 -> 7; matrix products, arithmetic and copies ran while one was open for 4% -> 4% of each run, Pallas kernels for 10% -> 11%
where the time goes in v7:
time: 77.2 us; the launch traced here: 77 us
  starting transfers between devices  25.6 us (33%)
  blocking collectives  17.7 us (23%)
  Pallas kernels  16.6 us (22%)
  waiting for transfers between devices  11.2 us (15%)
  other arithmetic  4.06 us (5%)
  between operations  0.84 us (1%)
    all_to_all x1, blocking collectives, exchange(): return lax.all_to_all(value, POINT_AXES, 0, 0, axis_index_groups=groups)  17.7 us
    all_to_all x1, starting transfers between devices, exchange(): return lax.all_to_all(value, POINT_AXES, 0, 0, axis_index_groups=groups)  13.3 us
    pallas_call x1, Pallas kernels, shards(): pl.pallas_call(features_kernel, grid=(rows // FEATURES_BLOCK,), out_shape...  8.44 us
    ppermute x3, waiting for transfers between devices, shards(): lax.ppermute(parts[k - 1], 'out', [(i, (i - k) % n_out) for i in range(n_...  6.48 us
    ppermute x3, starting transfers between devices, shards(): lax.ppermute(low, 'out', [(i, (i + k) % n_out) for i in range(n_out)])  5.72 us
    ppermute x3, starting transfers between devices, swap_core(): return lax.ppermute(value, 'core', [(0, 1), (1, 0)])  3.7 us
    pallas_call x1, Pallas kernels, shards(): pl.pallas_call(functools.partial(step_kernel, n_out, ratio), grid=(rows /...  3.66 us
    ppermute x3, waiting for transfers between devices, swap_core(): return lax.ppermute(value, 'core', [(0, 1), (1, 0)])  3.46 us
  transfers between devices with their start and end apart: 10, of which 7 were waited for; matrix products, arithmetic and copies ran while one was open for 4% of the time, Pallas kernels for 11%

profile of v7, /device:TPU:1, one launch (start us, length us, event | category | flops | bytes accessed | tf_op | source)
XLA Modules:
  0.0 77.0 jit_solution(5915555493510751864)
XLA Ops:
  0.0 1.0 %bitcast_convert_fusion.refs_0_ = bf16[16,4096]{1,0:T(8,128)(2,1)S(1)} fusion(f32[1,4096,16]{1,2,0:T(8,128)} %param.11), kind=kLoop, calls=%fused_computation.13 | loop fusion | flops 65536 | bytes 393216 | tf_op jit(solution)/shard_map/convert_element_type | solution.py:259
  1.0 2.1 %collective-permute-start = (bf16[16,4096]{1,0:T(8,128)(2,1)S(1)}, bf16[16,4096]{1,0:T(8,128)(2,1)S(1)}, u32[]{:S(2)}, u32[]{:S(2)}) collective-permute-start(bf16[16,4096]{1,0:T(8,128)(2,1)S(1)} %bitcast_convert_fusion.refs_0_), channel_id=1, source_target_pairs={{0,1},{1,2},{2,3},{3,0},{4,5},{5,6},{6,7},{7,4},{8,9},{9,10},{10,1... | collective-permute-start | bytes 393224 | tf_op jit(solution)/shard_map/ppermute | solution.py:262
  3.1 2.5 %collective-permute-start.1 = (bf16[16,4096]{1,0:T(8,128)(2,1)S(1)}, bf16[16,4096]{1,0:T(8,128)(2,1)S(1)}, u32[]{:S(2)}, u32[]{:S(2)}) collective-permute-start(bf16[16,4096]{1,0:T(8,128)(2,1)S(1)} %bitcast_convert_fusion.refs_0_), channel_id=1, source_target_pairs={{0,2},{1,3},{2,0},{3,1},{4,6},{5,7},{6,4},{7,5},{8,10},{9,11},{10,... | collective-permute-start | bytes 393224 | tf_op jit(solution)/shard_map/ppermute | solution.py:262
  5.6 1.2 %collective-permute-start.2 = (bf16[16,4096]{1,0:T(8,128)(2,1)S(1)}, bf16[16,4096]{1,0:T(8,128)(2,1)S(1)}, u32[]{:S(2)}, u32[]{:S(2)}) collective-permute-start(bf16[16,4096]{1,0:T(8,128)(2,1)S(1)} %bitcast_convert_fusion.refs_0_), channel_id=1, source_target_pairs={{0,3},{1,0},{2,1},{3,2},{4,7},{5,4},{6,5},{7,6},{8,11},{9,8},{10,9... | collective-permute-start | bytes 393224 | tf_op jit(solution)/shard_map/ppermute | solution.py:262
  6.8 8.4 %features.1 = (bf16[4096,512]{1,0:T(8,128)(2,1)}, bf16[4096,512]{1,0:T(8,128)(2,1)S(1)}, bf16[16,128]{1,0:T(8,128)(2,1)S(1)}) custom-call(s32[1,512]{1,0:T(1,128)} %bitcast.62, bf16[4096,256]{1,0:T(8,128)(2,1)} %points_ref.1, bf16[256,2048]{1,0:T(8,128)(2,1)} %freq_ref.1, f32[1,2048]{1,0:T(1,128)} %bitcast.63), custom_call_target="tpu_custom_call" | custom-call | tf_op jit(solution)/shard_map/features/pallas_call | solution.py:269
  15.3 1.5 %project.1 = bf16[32,32,128]{2,1,0:T(8,128)(2,1)} custom-call(bf16[16,4096]{1,0:T(8,128)(2,1)S(1)} %bitcast_convert_fusion.refs_0_, bf16[16,4096]{1,0:T(8,128)(2,1)S(1)} %collective-permute-done.refs_1_, bf16[16,4096]{1,0:T(8,128)(2,1)S(1)} %collective-permute-done.1.refs_2_, bf16[16,4096]{1,0:T(8,128)(2,1)S(1)} %collective-permute-done.2.refs_3_, ...), custom_call_target="tpu_custom_call" | custom-call | tf_op jit(solution)/shard_map/project/pallas_call | solution.py:294
  16.8 13.3 %all-to-all-start = ((bf16[32,32,128]{2,1,0:T(8,128)(2,1)}), bf16[32,32,128]{2,1,0:T(8,128)(2,1)S(1)}, u32[]{:S(2)}, u32[]{:S(2)}) async-start(bf16[32,32,128]{2,1,0:T(8,128)(2,1)} %project.1), calls=%async_computation | async-start | bytes 524288 | tf_op jit(solution)/shard_map/all_to_all | solution.py:228
  30.2 0.2 convert_reduce_fusion.1
  30.4 0.2 fusion
  30.6 0.2 convert_reduce_fusion.2
  30.8 0.3 fusion.5
  31.2 0.3 convert_reduce_fusion
  31.4 0.6 gather_fusion.1
  32.0 0.7 reduce_max.9
  33.4 0.6 multiply_reduce_fusion
  34.0 1.3 %all-to-all-done = bf16[32,32,128]{2,1,0:T(8,128)(2,1)S(1)} async-done(((bf16[32,32,128]{2,1,0:T(8,128)(2,1)}), bf16[32,32,128]{2,1,0:T(8,128)(2,1)S(1)}, u32[]{:S(2)}, u32[]{:S(2)}) %all-to-all-start) | async-done | bytes 262176 | tf_op jit(solution)/shard_map/all_to_all | solution.py:228
  35.4 2.4 %collective-permute-start.3 = (bf16[32,32,128]{2,1,0:T(8,128)(2,1)S(1)}, bf16[32,32,128]{2,1,0:T(8,128)(2,1)S(1)}, u32[]{:S(2)}, u32[]{:S(2)}) collective-permute-start(bf16[32,32,128]{2,1,0:T(8,128)(2,1)S(1)} %all-to-all-done), channel_id=1, source_target_pairs={{0,4},{4,0},{1,5},{5,1},{2,6},{6,2},{3,7},{7,3},{8,12},{12,8},{9,1... | collective-permute-start | bytes 786440 | tf_op jit(solution)/shard_map/ppermute | solution.py:236
  37.8 1.2 %collective-permute-done.3 = bf16[32,32,128]{2,1,0:T(8,128)(2,1)S(1)} collective-permute-done((bf16[32,32,128]{2,1,0:T(8,128)(2,1)S(1)}, bf16[32,32,128]{2,1,0:T(8,128)(2,1)S(1)}, u32[]{:S(2)}, u32[]{:S(2)}) %collective-permute-start.3) | collective-permute-done | bytes 262176 | tf_op jit(solution)/shard_map/ppermute | solution.py:236
  39.0 3.0 %conditional.1 = ((bf16[128,4096]{1,0:T(8,128)(2,1)}, f32[32,128]{1,0:T(8,128)S(1)}, f32[32,128]{1,0:T(8,128)}, f32[8,128]{1,0:T(8,128)S(1)})) conditional(s32[]{:T(128)} %convert_element_type.44, (bf16[16,4096]{1,0:T(8,128)(2,1)S(1)}, bf16[16,4096]{1,0:T(8,128)(2,1)S(1)}, bf16[16,4096]{1,0:T(8,128)(2,1)S(1)}, bf16[16,4096]{1,0:T(8,128)(2,1)S(1)}, ...), branch_computations={%region_6.7_spmd, %region_7.9_spmd} | conditional | flops 100485 | bytes 531276 | solution.py:364
  39.0 3.0 %gram.1 = (bf16[128,4096]{1,0:T(8,128)(2,1)}, f32[32,128]{1,0:T(8,128)S(1)}, f32[32,128]{1,0:T(8,128)}, f32[8,128]{1,0:T(8,128)S(1)}) custom-call(bf16[16,4096]{1,0:T(8,128)(2,1)S(1)} %get-tuple-element.67.refs_0_, bf16[16,4096]{1,0:T(8,128)(2,1)S(1)} %get-tuple-element.68.refs_1_, bf16[16,4096]{1,0:T(8,128)(2,1)S(1)} %get-tuple-element.69.refs_2_, ...), custom_call_target="tpu_custom_call" | custom-call | tf_op jit(solution)/shard_map/cond/branch_0_fun/gram/pallas_call | solution.py:333
  41.9 0.4 collective-permute-start.4
  42.3 1.0 %collective-permute-done.4 = f32[32,128]{1,0:T(8,128)S(1)} collective-permute-done((f32[32,128]{1,0:T(8,128)}, f32[32,128]{1,0:T(8,128)S(1)}, u32[]{:S(2)}, u32[]{:S(2)}) %collective-permute-start.4) | collective-permute-done | bytes 16416 | tf_op jit(solution)/shard_map/ppermute | solution.py:236
  43.4 17.7 %all_to_all.10.refs_3_ = bf16[32,40,128]{2,1,0:T(8,128)(2,1)S(1)} all-to-all(bf16[32,40,128]{2,1,0:T(8,128)(2,1)S(1)} %broadcast_in_dim.75), channel_id=1, replica_groups={{144,152,128,136,176,184,160,168,208,216,192,200,240,248,224,232,16,24,..., dimensions={0} | all-to-all | bytes 655360 | tf_op jit(solution)/shard_map/all_to_all | solution.py:228
  61.1 1.0 %collective-permute-start.5 = (bf16[32,40,128]{2,1,0:T(8,128)(2,1)S(1)}, bf16[32,40,128]{2,1,0:T(8,128)(2,1)S(1)}, u32[]{:S(2)}, u32[]{:S(2)}) collective-permute-start(bf16[32,40,128]{2,1,0:T(8,128)(2,1)S(1)} %all_to_all.10.refs_3_), channel_id=1, source_target_pairs={{0,4},{4,0},{1,5},{5,1},{2,6},{6,2},{3,7},{7,3},{8,12},{12,8},{9,1... | collective-permute-start | bytes 983048 | tf_op jit(solution)/shard_map/ppermute | solution.py:236
  62.0 1.3 %collective-permute-done.5.refs_4_ = bf16[32,40,128]{2,1,0:T(8,128)(2,1)S(1)} collective-permute-done((bf16[32,40,128]{2,1,0:T(8,128)(2,1)S(1)}, bf16[32,40,128]{2,1,0:T(8,128)(2,1)S(1)}, u32[]{:S(2)}, u32[]{:S(2)}) %collective-permute-start.5) | collective-permute-done | bytes 327712 | tf_op jit(solution)/shard_map/ppermute | solution.py:236
  63.3 3.7 %step.1 = (f32[16,4096]{1,0:T(8,128)S(1)}, bf16[16,4096]{1,0:T(8,128)(2,1)S(1)}, bf16[16,4096]{1,0:T(8,128)(2,1)S(1)}, bf16[16,4096]{1,0:T(8,128)(2,1)S(1)}) custom-call(f32[4,4]{1,0:T(4,128)S(1)} %copy-done.2, f32[4]{0:T(128)S(1)} %copy-done.3, f32[64,128]{1,0:T(8,128)S(1)} %bitcast.59, bf16[32,40,128]{2,1,0:T(8,128)(2,1)S(1)} %all_to_all.10.refs_3_, ...), custom_call_target="tpu_custom_call" | custom-call | tf_op jit(solution)/shard_map/step/pallas_call | solution.py:371
  66.9 0.3 collective-permute-start.6
  67.3 2.5 %collective-permute-start.7 = (bf16[16,4096]{1,0:T(8,128)(2,1)S(1)}, bf16[16,4096]{1,0:T(8,128)(2,1)S(1)}, u32[]{:S(2)}, u32[]{:S(2)}) collective-permute-start(bf16[16,4096]{1,0:T(8,128)(2,1)S(1)} %get-tuple-element.126), channel_id=1, source_target_pairs={{0,3},{1,0},{2,1},{3,2},{4,7},{5,4},{6,5},{7,6},{8,11},{9,8},{10,9... | collective-permute-start | bytes 393224 | tf_op jit(solution)/shard_map/ppermute | solution.py:392
  69.7 3.5 %collective-permute-done.6 = bf16[16,4096]{1,0:T(8,128)(2,1)S(1)} collective-permute-done((bf16[16,4096]{1,0:T(8,128)(2,1)S(1)}, bf16[16,4096]{1,0:T(8,128)(2,1)S(1)}, u32[]{:S(2)}, u32[]{:S(2)}) %collective-permute-start.6) | collective-permute-done | bytes 131104 | tf_op jit(solution)/shard_map/ppermute | solution.py:392
  73.2 0.4 collective-permute-done.7
  73.7 2.6 %collective-permute-done.8 = bf16[16,4096]{1,0:T(8,128)(2,1)S(1)} collective-permute-done((bf16[16,4096]{1,0:T(8,128)(2,1)S(1)}, bf16[16,4096]{1,0:T(8,128)(2,1)S(1)}, u32[]{:S(2)}, u32[]{:S(2)}) %collective-permute-start.8) | collective-permute-done | bytes 131104 | tf_op jit(solution)/shard_map/ppermute | solution.py:392
  76.2 0.8 %fusion.4 = f32[1,4096,16]{1,2,0:T(8,128)} fusion(f32[16,4096]{1,0:T(8,128)S(1)} %get-tuple-element.124, f32[1,4096,16]{1,2,0:T(8,128)S(1)} %copy-done.4, bf16[16,4096]{1,0:T(8,128)(2,1)S(1)} %collective-permute-done.8, bf16[16,4096]{1,0:T(8,128)(2,1)S(1)} %collective-permute-done.7, bf16[16,4096]{1,0:T(8,128)(2,1)S(1)} %collective-permute-done.6), kind=kLoop, calls=%fused_computation.17 | loop fusion | flops 458752 | bytes 1179648 | tf_op jit(solution)/shard_map/broadcast_in_dim | solution.py:394
  (28 shorter events, 0.3 us)
Async XLA Ops:
  0.0 30.8 %copy-start = (f32[4,512,16]{1,2,0:T(8,128)S(1)}, f32[4,512,16]{1,2,0:T(8,128)}, u32[]{:S(2)}) copy-start(f32[4,512,16]{1,2,0:T(8,128)} %param.13) | copy-start | bytes 393220
  1.0 14.2 %collective-permute-start = (bf16[16,4096]{1,0:T(8,128)(2,1)S(1)}, bf16[16,4096]{1,0:T(8,128)(2,1)S(1)}, u32[]{:S(2)}, u32[]{:S(2)}) collective-permute-start(bf16[16,4096]{1,0:T(8,128)(2,1)S(1)} %bitcast_convert_fusion.refs_0_), channel_id=1, source_target_pairs={{0,1},{1,2},{2,3},{3,0},{4,5},{5,6},{6,7},{7,4},{8,9},{9,10},{10,1... | collective-permute-start | bytes 393224 | tf_op jit(solution)/shard_map/ppermute | solution.py:262
  3.1 12.1 %collective-permute-start.1 = (bf16[16,4096]{1,0:T(8,128)(2,1)S(1)}, bf16[16,4096]{1,0:T(8,128)(2,1)S(1)}, u32[]{:S(2)}, u32[]{:S(2)}) collective-permute-start(bf16[16,4096]{1,0:T(8,128)(2,1)S(1)} %bitcast_convert_fusion.refs_0_), channel_id=1, source_target_pairs={{0,2},{1,3},{2,0},{3,1},{4,6},{5,7},{6,4},{7,5},{8,10},{9,11},{10,... | collective-permute-start | bytes 393224 | tf_op jit(solution)/shard_map/ppermute | solution.py:262
  5.6 9.7 %collective-permute-start.2 = (bf16[16,4096]{1,0:T(8,128)(2,1)S(1)}, bf16[16,4096]{1,0:T(8,128)(2,1)S(1)}, u32[]{:S(2)}, u32[]{:S(2)}) collective-permute-start(bf16[16,4096]{1,0:T(8,128)(2,1)S(1)} %bitcast_convert_fusion.refs_0_), channel_id=1, source_target_pairs={{0,3},{1,0},{2,1},{3,2},{4,7},{5,4},{6,5},{7,6},{8,11},{9,8},{10,9... | collective-permute-start | bytes 393224 | tf_op jit(solution)/shard_map/ppermute | solution.py:262
  6.7 23.4 %copy-start.5 = (s32[512]{0:T(512)S(1)}, s32[512]{0:T(512)}, u32[]{:S(2)}) copy-start(s32[512]{0:T(512)} %param.12) | copy-start | bytes 6148
  6.8 26.7 %copy-start.1 = (bf16[4096,256]{1,0:T(8,128)(2,1)S(1)}, bf16[4096,256]{1,0:T(8,128)(2,1)}, u32[]{:S(2)}) copy-start(bf16[4096,256]{1,0:T(8,128)(2,1)} %points_ref.1) | copy-start | bytes 6291460
  16.8 18.5 %all-to-all-start = ((bf16[32,32,128]{2,1,0:T(8,128)(2,1)}), bf16[32,32,128]{2,1,0:T(8,128)(2,1)S(1)}, u32[]{:S(2)}, u32[]{:S(2)}) async-start(bf16[32,32,128]{2,1,0:T(8,128)(2,1)} %project.1), calls=%async_computation | async-start | bytes 524288 | tf_op jit(solution)/shard_map/all_to_all | solution.py:228
  35.4 3.5 %collective-permute-start.3 = (bf16[32,32,128]{2,1,0:T(8,128)(2,1)S(1)}, bf16[32,32,128]{2,1,0:T(8,128)(2,1)S(1)}, u32[]{:S(2)}, u32[]{:S(2)}) collective-permute-start(bf16[32,32,128]{2,1,0:T(8,128)(2,1)S(1)} %all-to-all-done), channel_id=1, source_target_pairs={{0,4},{4,0},{1,5},{5,1},{2,6},{6,2},{3,7},{7,3},{8,12},{12,8},{9,1... | collective-permute-start | bytes 786440 | tf_op jit(solution)/shard_map/ppermute | solution.py:236
  38.9 24.3 %copy-start.2 = (f32[4,4]{1,0:T(4,128)S(1)}, f32[4,4]{1,0:T(4,128)}, u32[]{:S(2)}) copy-start(f32[4,4]{1,0:T(4,128)} %refs_0_.1) | copy-start | bytes 196
  39.0 24.3 %copy-start.3 = (f32[4]{0:T(128)S(1)}, f32[4]{0:T(128)}, u32[]{:S(2)}) copy-start(f32[4]{0:T(128)} %refs_1_.1) | copy-start | bytes 52
  41.9 34.3 %copy-start.4 = (f32[1,4096,16]{1,2,0:T(8,128)S(1)}, f32[1,4096,16]{1,2,0:T(8,128)}, u32[]{:S(2)}) copy-start(f32[1,4096,16]{1,2,0:T(8,128)} %param.11) | copy-start | bytes 786436
  41.9 1.4 %collective-permute-start.4 = (f32[32,128]{1,0:T(8,128)}, f32[32,128]{1,0:T(8,128)S(1)}, u32[]{:S(2)}, u32[]{:S(2)}) collective-permute-start(f32[32,128]{1,0:T(8,128)} %get-tuple-element.139), channel_id=1, source_target_pairs={{0,4},{4,0},{1,5},{5,1},{2,6},{6,2},{3,7},{7,3},{8,12},{12,8},{9,1... | collective-permute-start | bytes 49160 | tf_op jit(solution)/shard_map/ppermute | solution.py:236
  61.1 2.2 %collective-permute-start.5 = (bf16[32,40,128]{2,1,0:T(8,128)(2,1)S(1)}, bf16[32,40,128]{2,1,0:T(8,128)(2,1)S(1)}, u32[]{:S(2)}, u32[]{:S(2)}) collective-permute-start(bf16[32,40,128]{2,1,0:T(8,128)(2,1)S(1)} %all_to_all.10.refs_3_), channel_id=1, source_target_pairs={{0,4},{4,0},{1,5},{5,1},{2,6},{6,2},{3,7},{7,3},{8,12},{12,8},{9,1... | collective-permute-start | bytes 983048 | tf_op jit(solution)/shard_map/ppermute | solution.py:236
  66.9 6.3 %collective-permute-start.6 = (bf16[16,4096]{1,0:T(8,128)(2,1)S(1)}, bf16[16,4096]{1,0:T(8,128)(2,1)S(1)}, u32[]{:S(2)}, u32[]{:S(2)}) collective-permute-start(bf16[16,4096]{1,0:T(8,128)(2,1)S(1)} %get-tuple-element.125), channel_id=1, source_target_pairs={{0,2},{1,3},{2,0},{3,1},{4,6},{5,7},{6,4},{7,5},{8,10},{9,11},{10,... | collective-permute-start | bytes 393224 | tf_op jit(solution)/shard_map/ppermute | solution.py:392
  67.3 6.4 %collective-permute-start.7 = (bf16[16,4096]{1,0:T(8,128)(2,1)S(1)}, bf16[16,4096]{1,0:T(8,128)(2,1)S(1)}, u32[]{:S(2)}, u32[]{:S(2)}) collective-permute-start(bf16[16,4096]{1,0:T(8,128)(2,1)S(1)} %get-tuple-element.126), channel_id=1, source_target_pairs={{0,3},{1,0},{2,1},{3,2},{4,7},{5,4},{6,5},{7,6},{8,11},{9,8},{10,9... | collective-permute-start | bytes 393224 | tf_op jit(solution)/shard_map/ppermute | solution.py:392
  69.7 6.5 %collective-permute-start.8 = (bf16[16,4096]{1,0:T(8,128)(2,1)S(1)}, bf16[16,4096]{1,0:T(8,128)(2,1)S(1)}, u32[]{:S(2)}, u32[]{:S(2)}) collective-permute-start(bf16[16,4096]{1,0:T(8,128)(2,1)S(1)} %get-tuple-element.127), channel_id=1, source_target_pairs={{0,1},{1,2},{2,3},{3,0},{4,5},{5,6},{6,7},{7,4},{8,9},{9,10},{10,1... | collective-permute-start | bytes 393224 | tf_op jit(solution)/shard_map/ppermute | solution.py:392

commit v8 on v7

--- a/solution.py
+++ b/solution.py
@@ -185,7 +185,7 @@
     @pl.when(pl.program_id(0) == 0)
     def _():
         out, core, _ = place_of_device()
-        order = [lax.rem(out - k + n_out, n_out) for k in range(n_out)]
+        order = [lax.rem(out + k, n_out) for k in range(n_out)]
         mixer = [[coregion_ref[a, b] for b in order] for a in order]
 
         def mix(values):
@@ -229,7 +229,7 @@
 
 
 def far_first(n_out):
-    return sorted(range(1, n_out), key=lambda k: -min(k, n_out - k))
+    return sorted(range(1, n_out), key=lambda k: (-min(k, n_out - k), -k))
 
 
 def swap_core(value):
@@ -259,7 +259,7 @@
     low = own_weights.astype(BF16)
     weights = [low] * n_out
     for k in far_first(n_out):
-        weights[k] = lax.ppermute(low, "out", [(i, (i + k) % n_out) for i in range(n_out)])
+        weights[k] = lax.ppermute(low, "out", [(i, (i - k) % n_out) for i in range(n_out)])
     weight_specs = lambda block: [pl.BlockSpec((draws, block), lambda i: (0, i))] * n_out
     point_spec = lambda block: pl.BlockSpec((block, width), lambda i: (i, 0))
     feat_spec = lambda block: pl.BlockSpec((block, own_features), lambda i: (i, 0))
@@ -321,7 +321,7 @@
     at = jnp.stack([jnp.where(own_core, at, -64), jnp.where(own_core, -64, at)])
     at = jnp.broadcast_to(at[:, :, None], (2, own_rows, 128))
     col_norm = jnp.sum(jnp.square(points_now.astype(F32)), 1)[None]
-    order = lax.rem(out - lax.iota(jnp.int32, n_out) + n_out, n_out)
+    order = lax.rem(out + lax.iota(jnp.int32, n_out), n_out)
     own_targets = jnp.einsum("im,qms->qsi", chosen.astype(F32), targets, precision=highest)[order]
     own_targets = own_targets.reshape(cols, own_rows)
     got, at, overflow, own_index, col_norm, own_targets = lax.optimization_barrier(
@@ -389,7 +389,7 @@
     )(coregion, noise_var, own_targets, got, got_other, in_hbm(feats), in_hbm(kern))
     total = own_weights + base
     for k in far_first(n_out):
-        part = lax.ppermute(parts[k - 1], "out", [(i, (i - k) % n_out) for i in range(n_out)])
+        part = lax.ppermute(parts[k - 1], "out", [(i, (i + k) % n_out) for i in range(n_out)])
         total = total + part.astype(F32)
     return total.T[None]
 

time: 77.2 us -> 76.2 us (0.987)
  waiting for transfers between devices: 11.2 us -> 9.78 us
    ppermute x6, waiting for transfers between devices: 6.49 us -> 5.03 us  [the longest x3 5.02 us: shards(): lax.ppermute(parts[k - 1], 'out', [(i, (i + k) % n_out) for i in range(n_...]
where the time goes in v8:
time: 76.2 us; the launch traced here: 75.5 us
  starting transfers between devices  25.6 us (34%)
  blocking collectives  17.7 us (23%)
  Pallas kernels  16.6 us (22%)
  waiting for transfers between devices  9.78 us (13%)
  other arithmetic  4.06 us (5%)
  between operations  0.84 us (1%)
    all_to_all x1, blocking collectives, exchange(): return lax.all_to_all(value, POINT_AXES, 0, 0, axis_index_groups=groups)  17.7 us
    all_to_all x1, starting transfers between devices, exchange(): return lax.all_to_all(value, POINT_AXES, 0, 0, axis_index_groups=groups)  13.3 us
    pallas_call x1, Pallas kernels, shards(): pl.pallas_call(features_kernel, grid=(rows // FEATURES_BLOCK,), out_shape...  8.44 us
    ppermute x3, waiting for transfers between devices, shards(): lax.ppermute(parts[k - 1], 'out', [(i, (i + k) % n_out) for i in range(n_...  5.02 us
    ppermute x3, starting transfers between devices, shards(): lax.ppermute(low, 'out', [(i, (i - k) % n_out) for i in range(n_out)])  4.51 us
    ppermute x3, starting transfers between devices, shards(): lax.ppermute(parts[k - 1], 'out', [(i, (i + k) % n_out) for i in range(n_...  4 us
    ppermute x3, starting transfers between devices, swap_core(): return lax.ppermute(value, 'core', [(0, 1), (1, 0)])  3.7 us
    pallas_call x1, Pallas kernels, shards(): pl.pallas_call(functools.partial(step_kernel, n_out, ratio), grid=(rows /...  3.66 us
  transfers between devices with their start and end apart: 10, of which 7 were waited for; matrix products, arithmetic and copies ran while one was open for 4% of the time, Pallas kernels for 11%

profile of v8, /device:TPU:1, one launch (start us, length us, event | category | flops | bytes accessed | tf_op | source)
XLA Modules:
  0.0 75.5 jit_solution(9647235141172657451)
XLA Ops:
  0.0 1.0 %bitcast_convert_fusion.refs_0_ = bf16[16,4096]{1,0:T(8,128)(2,1)S(1)} fusion(f32[1,4096,16]{1,2,0:T(8,128)} %param.11), kind=kLoop, calls=%fused_computation.13 | loop fusion | flops 65536 | bytes 393216 | tf_op jit(solution)/shard_map/convert_element_type | solution.py:259
  1.0 3.4 %collective-permute-start = (bf16[16,4096]{1,0:T(8,128)(2,1)S(1)}, bf16[16,4096]{1,0:T(8,128)(2,1)S(1)}, u32[]{:S(2)}, u32[]{:S(2)}) collective-permute-start(bf16[16,4096]{1,0:T(8,128)(2,1)S(1)} %bitcast_convert_fusion.refs_0_), channel_id=1, source_target_pairs={{0,3},{1,0},{2,1},{3,2},{4,7},{5,4},{6,5},{7,6},{8,11},{9,8},{10,9... | collective-permute-start | bytes 393224 | tf_op jit(solution)/shard_map/ppermute | solution.py:262
  4.4 0.5 collective-permute-start.1
  4.9 0.6 collective-permute-start.2
  5.6 8.4 %features.1 = (bf16[4096,512]{1,0:T(8,128)(2,1)}, bf16[4096,512]{1,0:T(8,128)(2,1)S(1)}, bf16[16,128]{1,0:T(8,128)(2,1)S(1)}) custom-call(s32[1,512]{1,0:T(1,128)} %bitcast.62, bf16[4096,256]{1,0:T(8,128)(2,1)} %points_ref.1, bf16[256,2048]{1,0:T(8,128)(2,1)} %freq_ref.1, f32[1,2048]{1,0:T(1,128)} %bitcast.63), custom_call_target="tpu_custom_call" | custom-call | tf_op jit(solution)/shard_map/features/pallas_call | solution.py:269
  14.0 1.5 %project.1 = bf16[32,32,128]{2,1,0:T(8,128)(2,1)} custom-call(bf16[16,4096]{1,0:T(8,128)(2,1)S(1)} %bitcast_convert_fusion.refs_0_, bf16[16,4096]{1,0:T(8,128)(2,1)S(1)} %collective-permute-done.refs_1_, bf16[16,4096]{1,0:T(8,128)(2,1)S(1)} %collective-permute-done.1.refs_2_, bf16[16,4096]{1,0:T(8,128)(2,1)S(1)} %collective-permute-done.2.refs_3_, ...), custom_call_target="tpu_custom_call" | custom-call | tf_op jit(solution)/shard_map/project/pallas_call | solution.py:294
  15.6 13.3 %all-to-all-start = ((bf16[32,32,128]{2,1,0:T(8,128)(2,1)}), bf16[32,32,128]{2,1,0:T(8,128)(2,1)S(1)}, u32[]{:S(2)}, u32[]{:S(2)}) async-start(bf16[32,32,128]{2,1,0:T(8,128)(2,1)} %project.1), calls=%async_computation | async-start | bytes 524288 | tf_op jit(solution)/shard_map/all_to_all | solution.py:228
  29.0 0.2 convert_reduce_fusion.1
  29.2 0.2 fusion
  29.4 0.2 convert_reduce_fusion.2
  29.6 0.3 fusion.5
  29.9 0.3 convert_reduce_fusion
  30.2 0.6 gather_fusion.1
  30.8 0.7 reduce_max.9
  32.2 0.6 multiply_reduce_fusion
  32.8 1.3 %all-to-all-done = bf16[32,32,128]{2,1,0:T(8,128)(2,1)S(1)} async-done(((bf16[32,32,128]{2,1,0:T(8,128)(2,1)}), bf16[32,32,128]{2,1,0:T(8,128)(2,1)S(1)}, u32[]{:S(2)}, u32[]{:S(2)}) %all-to-all-start) | async-done | bytes 262176 | tf_op jit(solution)/shard_map/all_to_all | solution.py:228
  34.2 2.4 %collective-permute-start.3 = (bf16[32,32,128]{2,1,0:T(8,128)(2,1)S(1)}, bf16[32,32,128]{2,1,0:T(8,128)(2,1)S(1)}, u32[]{:S(2)}, u32[]{:S(2)}) collective-permute-start(bf16[32,32,128]{2,1,0:T(8,128)(2,1)S(1)} %all-to-all-done), channel_id=1, source_target_pairs={{0,4},{4,0},{1,5},{5,1},{2,6},{6,2},{3,7},{7,3},{8,12},{12,8},{9,1... | collective-permute-start | bytes 786440 | tf_op jit(solution)/shard_map/ppermute | solution.py:236
  36.6 1.2 %collective-permute-done.3 = bf16[32,32,128]{2,1,0:T(8,128)(2,1)S(1)} collective-permute-done((bf16[32,32,128]{2,1,0:T(8,128)(2,1)S(1)}, bf16[32,32,128]{2,1,0:T(8,128)(2,1)S(1)}, u32[]{:S(2)}, u32[]{:S(2)}) %collective-permute-start.3) | collective-permute-done | bytes 262176 | tf_op jit(solution)/shard_map/ppermute | solution.py:236
  37.7 3.0 %conditional.1 = ((bf16[128,4096]{1,0:T(8,128)(2,1)}, f32[32,128]{1,0:T(8,128)S(1)}, f32[32,128]{1,0:T(8,128)}, f32[8,128]{1,0:T(8,128)S(1)})) conditional(s32[]{:T(128)} %convert_element_type.44, (bf16[16,4096]{1,0:T(8,128)(2,1)S(1)}, bf16[16,4096]{1,0:T(8,128)(2,1)S(1)}, bf16[16,4096]{1,0:T(8,128)(2,1)S(1)}, bf16[16,4096]{1,0:T(8,128)(2,1)S(1)}, ...), branch_computations={%region_6.7_spmd, %region_7.9_spmd} | conditional | flops 100485 | bytes 531276 | solution.py:364
  37.7 3.0 %gram.1 = (bf16[128,4096]{1,0:T(8,128)(2,1)}, f32[32,128]{1,0:T(8,128)S(1)}, f32[32,128]{1,0:T(8,128)}, f32[8,128]{1,0:T(8,128)S(1)}) custom-call(bf16[16,4096]{1,0:T(8,128)(2,1)S(1)} %get-tuple-element.67.refs_0_, bf16[16,4096]{1,0:T(8,128)(2,1)S(1)} %get-tuple-element.68.refs_1_, bf16[16,4096]{1,0:T(8,128)(2,1)S(1)} %get-tuple-element.69.refs_2_, ...), custom_call_target="tpu_custom_call" | custom-call | tf_op jit(solution)/shard_map/cond/branch_0_fun/gram/pallas_call | solution.py:333
  40.7 0.4 collective-permute-start.4
  41.1 1.0 %collective-permute-done.4 = f32[32,128]{1,0:T(8,128)S(1)} collective-permute-done((f32[32,128]{1,0:T(8,128)}, f32[32,128]{1,0:T(8,128)S(1)}, u32[]{:S(2)}, u32[]{:S(2)}) %collective-permute-start.4) | collective-permute-done | bytes 16416 | tf_op jit(solution)/shard_map/ppermute | solution.py:236
  42.2 17.7 %all_to_all.10.refs_3_ = bf16[32,40,128]{2,1,0:T(8,128)(2,1)S(1)} all-to-all(bf16[32,40,128]{2,1,0:T(8,128)(2,1)S(1)} %broadcast_in_dim.75), channel_id=1, replica_groups={{144,152,128,136,176,184,160,168,208,216,192,200,240,248,224,232,16,24,..., dimensions={0} | all-to-all | bytes 655360 | tf_op jit(solution)/shard_map/all_to_all | solution.py:228
  59.8 1.0 %collective-permute-start.5 = (bf16[32,40,128]{2,1,0:T(8,128)(2,1)S(1)}, bf16[32,40,128]{2,1,0:T(8,128)(2,1)S(1)}, u32[]{:S(2)}, u32[]{:S(2)}) collective-permute-start(bf16[32,40,128]{2,1,0:T(8,128)(2,1)S(1)} %all_to_all.10.refs_3_), channel_id=1, source_target_pairs={{0,4},{4,0},{1,5},{5,1},{2,6},{6,2},{3,7},{7,3},{8,12},{12,8},{9,1... | collective-permute-start | bytes 983048 | tf_op jit(solution)/shard_map/ppermute | solution.py:236
  60.8 1.3 %collective-permute-done.5.refs_4_ = bf16[32,40,128]{2,1,0:T(8,128)(2,1)S(1)} collective-permute-done((bf16[32,40,128]{2,1,0:T(8,128)(2,1)S(1)}, bf16[32,40,128]{2,1,0:T(8,128)(2,1)S(1)}, u32[]{:S(2)}, u32[]{:S(2)}) %collective-permute-start.5) | collective-permute-done | bytes 327712 | tf_op jit(solution)/shard_map/ppermute | solution.py:236
  62.1 3.7 %step.1 = (f32[16,4096]{1,0:T(8,128)S(1)}, bf16[16,4096]{1,0:T(8,128)(2,1)S(1)}, bf16[16,4096]{1,0:T(8,128)(2,1)S(1)}, bf16[16,4096]{1,0:T(8,128)(2,1)S(1)}) custom-call(f32[4,4]{1,0:T(4,128)S(1)} %copy-done.2, f32[4]{0:T(128)S(1)} %copy-done.3, f32[64,128]{1,0:T(8,128)S(1)} %bitcast.59, bf16[32,40,128]{2,1,0:T(8,128)(2,1)S(1)} %all_to_all.10.refs_3_, ...), custom_call_target="tpu_custom_call" | custom-call | tf_op jit(solution)/shard_map/step/pallas_call | solution.py:371
  65.7 1.9 %collective-permute-start.6 = (bf16[16,4096]{1,0:T(8,128)(2,1)S(1)}, bf16[16,4096]{1,0:T(8,128)(2,1)S(1)}, u32[]{:S(2)}, u32[]{:S(2)}) collective-permute-start(bf16[16,4096]{1,0:T(8,128)(2,1)S(1)} %get-tuple-element.125), channel_id=1, source_target_pairs={{0,2},{1,3},{2,0},{3,1},{4,6},{5,7},{6,4},{7,5},{8,10},{9,11},{10,... | collective-permute-start | bytes 393224 | tf_op jit(solution)/shard_map/ppermute | solution.py:392
  67.7 2.1 %collective-permute-start.7 = (bf16[16,4096]{1,0:T(8,128)(2,1)S(1)}, bf16[16,4096]{1,0:T(8,128)(2,1)S(1)}, u32[]{:S(2)}, u32[]{:S(2)}) collective-permute-start(bf16[16,4096]{1,0:T(8,128)(2,1)S(1)} %get-tuple-element.126), channel_id=1, source_target_pairs={{0,3},{1,0},{2,1},{3,2},{4,7},{5,4},{6,5},{7,6},{8,11},{9,8},{10,9... | collective-permute-start | bytes 393224 | tf_op jit(solution)/shard_map/ppermute | solution.py:392
  69.7 2.3 %collective-permute-done.6 = bf16[16,4096]{1,0:T(8,128)(2,1)S(1)} collective-permute-done((bf16[16,4096]{1,0:T(8,128)(2,1)S(1)}, bf16[16,4096]{1,0:T(8,128)(2,1)S(1)}, u32[]{:S(2)}, u32[]{:S(2)}) %collective-permute-start.6) | collective-permute-done | bytes 131104 | tf_op jit(solution)/shard_map/ppermute | solution.py:392
  72.0 2.5 %collective-permute-done.7 = bf16[16,4096]{1,0:T(8,128)(2,1)S(1)} collective-permute-done((bf16[16,4096]{1,0:T(8,128)(2,1)S(1)}, bf16[16,4096]{1,0:T(8,128)(2,1)S(1)}, u32[]{:S(2)}, u32[]{:S(2)}) %collective-permute-start.7) | collective-permute-done | bytes 131104 | tf_op jit(solution)/shard_map/ppermute | solution.py:392
  74.5 0.2 collective-permute-done.8
  74.8 0.8 %fusion.4 = f32[1,4096,16]{1,2,0:T(8,128)} fusion(f32[16,4096]{1,0:T(8,128)S(1)} %get-tuple-element.124, f32[1,4096,16]{1,2,0:T(8,128)S(1)} %copy-done.4, bf16[16,4096]{1,0:T(8,128)(2,1)S(1)} %collective-permute-done.8, bf16[16,4096]{1,0:T(8,128)(2,1)S(1)} %collective-permute-done.7, bf16[16,4096]{1,0:T(8,128)(2,1)S(1)} %collective-permute-done.6), kind=kLoop, calls=%fused_computation.17 | loop fusion | flops 458752 | bytes 1179648 | tf_op jit(solution)/shard_map/broadcast_in_dim | solution.py:394
  (28 shorter events, 0.3 us)
Async XLA Ops:
  0.0 29.6 %copy-start = (f32[4,512,16]{1,2,0:T(8,128)S(1)}, f32[4,512,16]{1,2,0:T(8,128)}, u32[]{:S(2)}) copy-start(f32[4,512,16]{1,2,0:T(8,128)} %param.13) | copy-start | bytes 393220
  1.0 13.0 %collective-permute-start = (bf16[16,4096]{1,0:T(8,128)(2,1)S(1)}, bf16[16,4096]{1,0:T(8,128)(2,1)S(1)}, u32[]{:S(2)}, u32[]{:S(2)}) collective-permute-start(bf16[16,4096]{1,0:T(8,128)(2,1)S(1)} %bitcast_convert_fusion.refs_0_), channel_id=1, source_target_pairs={{0,3},{1,0},{2,1},{3,2},{4,7},{5,4},{6,5},{7,6},{8,11},{9,8},{10,9... | collective-permute-start | bytes 393224 | tf_op jit(solution)/shard_map/ppermute | solution.py:262
  4.4 9.6 %collective-permute-start.1 = (bf16[16,4096]{1,0:T(8,128)(2,1)S(1)}, bf16[16,4096]{1,0:T(8,128)(2,1)S(1)}, u32[]{:S(2)}, u32[]{:S(2)}) collective-permute-start(bf16[16,4096]{1,0:T(8,128)(2,1)S(1)} %bitcast_convert_fusion.refs_0_), channel_id=1, source_target_pairs={{0,2},{1,3},{2,0},{3,1},{4,6},{5,7},{6,4},{7,5},{8,10},{9,11},{10,... | collective-permute-start | bytes 393224 | tf_op jit(solution)/shard_map/ppermute | solution.py:262
  4.9 9.1 %collective-permute-start.2 = (bf16[16,4096]{1,0:T(8,128)(2,1)S(1)}, bf16[16,4096]{1,0:T(8,128)(2,1)S(1)}, u32[]{:S(2)}, u32[]{:S(2)}) collective-permute-start(bf16[16,4096]{1,0:T(8,128)(2,1)S(1)} %bitcast_convert_fusion.refs_0_), channel_id=1, source_target_pairs={{0,1},{1,2},{2,3},{3,0},{4,5},{5,6},{6,7},{7,4},{8,9},{9,10},{10,1... | collective-permute-start | bytes 393224 | tf_op jit(solution)/shard_map/ppermute | solution.py:262
  5.5 23.4 %copy-start.5 = (s32[512]{0:T(512)S(1)}, s32[512]{0:T(512)}, u32[]{:S(2)}) copy-start(s32[512]{0:T(512)} %param.12) | copy-start | bytes 6148
  5.5 26.7 %copy-start.1 = (bf16[4096,256]{1,0:T(8,128)(2,1)S(1)}, bf16[4096,256]{1,0:T(8,128)(2,1)}, u32[]{:S(2)}) copy-start(bf16[4096,256]{1,0:T(8,128)(2,1)} %points_ref.1) | copy-start | bytes 6291460
  15.6 18.5 %all-to-all-start = ((bf16[32,32,128]{2,1,0:T(8,128)(2,1)}), bf16[32,32,128]{2,1,0:T(8,128)(2,1)S(1)}, u32[]{:S(2)}, u32[]{:S(2)}) async-start(bf16[32,32,128]{2,1,0:T(8,128)(2,1)} %project.1), calls=%async_computation | async-start | bytes 524288 | tf_op jit(solution)/shard_map/all_to_all | solution.py:228
  34.2 3.5 %collective-permute-start.3 = (bf16[32,32,128]{2,1,0:T(8,128)(2,1)S(1)}, bf16[32,32,128]{2,1,0:T(8,128)(2,1)S(1)}, u32[]{:S(2)}, u32[]{:S(2)}) collective-permute-start(bf16[32,32,128]{2,1,0:T(8,128)(2,1)S(1)} %all-to-all-done), channel_id=1, source_target_pairs={{0,4},{4,0},{1,5},{5,1},{2,6},{6,2},{3,7},{7,3},{8,12},{12,8},{9,1... | collective-permute-start | bytes 786440 | tf_op jit(solution)/shard_map/ppermute | solution.py:236
  37.7 24.3 %copy-start.2 = (f32[4,4]{1,0:T(4,128)S(1)}, f32[4,4]{1,0:T(4,128)}, u32[]{:S(2)}) copy-start(f32[4,4]{1,0:T(4,128)} %refs_0_.1) | copy-start | bytes 196
  37.7 24.3 %copy-start.3 = (f32[4]{0:T(128)S(1)}, f32[4]{0:T(128)}, u32[]{:S(2)}) copy-start(f32[4]{0:T(128)} %refs_1_.1) | copy-start | bytes 52
  40.7 34.1 %copy-start.4 = (f32[1,4096,16]{1,2,0:T(8,128)S(1)}, f32[1,4096,16]{1,2,0:T(8,128)}, u32[]{:S(2)}) copy-start(f32[1,4096,16]{1,2,0:T(8,128)} %param.11) | copy-start | bytes 786436
  40.7 1.4 %collective-permute-start.4 = (f32[32,128]{1,0:T(8,128)}, f32[32,128]{1,0:T(8,128)S(1)}, u32[]{:S(2)}, u32[]{:S(2)}) collective-permute-start(f32[32,128]{1,0:T(8,128)} %get-tuple-element.139), channel_id=1, source_target_pairs={{0,4},{4,0},{1,5},{5,1},{2,6},{6,2},{3,7},{7,3},{8,12},{12,8},{9,1... | collective-permute-start | bytes 49160 | tf_op jit(solution)/shard_map/ppermute | solution.py:236
  59.8 2.2 %collective-permute-start.5 = (bf16[32,40,128]{2,1,0:T(8,128)(2,1)S(1)}, bf16[32,40,128]{2,1,0:T(8,128)(2,1)S(1)}, u32[]{:S(2)}, u32[]{:S(2)}) collective-permute-start(bf16[32,40,128]{2,1,0:T(8,128)(2,1)S(1)} %all_to_all.10.refs_3_), channel_id=1, source_target_pairs={{0,4},{4,0},{1,5},{5,1},{2,6},{6,2},{3,7},{7,3},{8,12},{12,8},{9,1... | collective-permute-start | bytes 983048 | tf_op jit(solution)/shard_map/ppermute | solution.py:236
  65.7 6.3 %collective-permute-start.6 = (bf16[16,4096]{1,0:T(8,128)(2,1)S(1)}, bf16[16,4096]{1,0:T(8,128)(2,1)S(1)}, u32[]{:S(2)}, u32[]{:S(2)}) collective-permute-start(bf16[16,4096]{1,0:T(8,128)(2,1)S(1)} %get-tuple-element.125), channel_id=1, source_target_pairs={{0,2},{1,3},{2,0},{3,1},{4,6},{5,7},{6,4},{7,5},{8,10},{9,11},{10,... | collective-permute-start | bytes 393224 | tf_op jit(solution)/shard_map/ppermute | solution.py:392
  67.7 6.9 %collective-permute-start.7 = (bf16[16,4096]{1,0:T(8,128)(2,1)S(1)}, bf16[16,4096]{1,0:T(8,128)(2,1)S(1)}, u32[]{:S(2)}, u32[]{:S(2)}) collective-permute-start(bf16[16,4096]{1,0:T(8,128)(2,1)S(1)} %get-tuple-element.126), channel_id=1, source_target_pairs={{0,3},{1,0},{2,1},{3,2},{4,7},{5,4},{6,5},{7,6},{8,11},{9,8},{10,9... | collective-permute-start | bytes 393224 | tf_op jit(solution)/shard_map/ppermute | solution.py:392
  69.7 5.0 %collective-permute-start.8 = (bf16[16,4096]{1,0:T(8,128)(2,1)S(1)}, bf16[16,4096]{1,0:T(8,128)(2,1)S(1)}, u32[]{:S(2)}, u32[]{:S(2)}) collective-permute-start(bf16[16,4096]{1,0:T(8,128)(2,1)S(1)} %get-tuple-element.127), channel_id=1, source_target_pairs={{0,1},{1,2},{2,3},{3,0},{4,5},{5,6},{6,7},{7,4},{8,9},{9,10},{10,1... | collective-permute-start | bytes 393224 | tf_op jit(solution)/shard_map/ppermute | solution.py:392
